TPU v7x, 256 devices: a whole 4x4x8 slice. The times are simulated.
256 devices in a mesh: pipe: 8 (over y, x_hi), expert: 32 (over x_lo, z, core).
Axes of the slice: x: 4 (x_hi: 2, x_lo: 2; x = x_hi * 2 + x_lo), y: 4, z: 8, core: 2. Of those that a mesh axis runs over, the one named last changes fastest.
Arguments:
- tokens: bfloat16 [8192, 14336], P('expert', 'pipe'), may hold values from -6 to 6
- cotangent: bfloat16 [8192, 14336], P('expert', 'pipe'), may hold values from -6 to 6
- route_a: int32 [8192, 8], P('expert'), may hold values from 0 to 255, all different within a row; in each aligned block of 256 rows (0 to 255, 256 to 511, ...) at most 16 rows name the same one
- route_b: int32 [8192, 8], P('expert'), may hold values from 0 to 255, all different within a row; in each aligned block of 256 rows (0 to 255, 256 to 511, ...) at most 16 rows name the same one
- gates_a: bfloat16 [8192, 8], P('expert'), may hold values from 0.099609375 to 1
- gates_b: bfloat16 [8192, 8], P('expert'), may hold values from 0.099609375 to 1
- w_up: bfloat16 [32, 14336, 1024], P('expert', 'pipe'), as said below
- w_down: bfloat16 [32, 1024, 14336], P('expert', None, 'pipe'), as said below
Outputs:
- out_y: bfloat16 [8192, 14336], P('expert', 'pipe')
- grad_x: bfloat16 [8192, 14336], P('expert', 'pipe')
- grad_down: bfloat16 [32, 512, 14336], P('expert', None, 'pipe')
Inputs may be any that keep to these rules, and one draw needn't show every extreme that they name: `route_a`: each row names 8 different experts. Among the rows of one device no expert is named more than 16 times, and in some device's rows some expert is named exactly 16 times. `route_b`: each row names 8 different experts. Among the rows of one device no expert is named more than 16 times, and in some device's rows some expert is named exactly 16 times. `w_up`: row block k of 1792 rows equals row block 7 - k. `w_down`: column block k of 1792 columns equals column block 7 - k.
All inputs are finite; a program needn't handle non-finite values.
Results may differ from a plain program's by a relative error of at most 0.0065.
Values may be sent and summed in bfloat16 or wider, within the bound.
No kernel may reach another device: no remote copies, remote signals or barrier semaphores. Data moves between devices by JAX's collectives and lax.ppermute only.
A program may use at most 128 MiB of HBM per device.

v0:
```python
import jax
import jax.numpy as jnp
from jax import lax
from jax.sharding import PartitionSpec as P

CAP = 16


def swapped(block, axis, stride):
    count = lax.axis_size(axis)
    route = []
    for low in range(count):
        high = low | 1 << stride
        if high != low and high < count:
            route += [(low, high), (high, low)]
    return lax.ppermute(block, axis, route)


def slot_tables(routing, gate_values, expert_count, capacity):
    flat_routes = routing.reshape(-1)
    experts_iota = jnp.arange(expert_count, dtype=jnp.int32)
    one_hot = (flat_routes[:, None] == experts_iota[None, :]).astype(jnp.int32)
    running = jnp.cumsum(one_hot, axis=0) - 1
    position = jnp.sum(running * one_hot, axis=1)
    slot_ids = jnp.where(flat_routes < expert_count, flat_routes * capacity + position, -1)
    slot_iota = jnp.arange(expert_count * capacity, dtype=jnp.int32)
    slot_match = slot_ids[None, :] == slot_iota[:, None]
    dispatch_table = jnp.any(
        slot_match.reshape(expert_count * capacity, routing.shape[0], routing.shape[1]), axis=2
    ).astype(jnp.bfloat16)
    gate_flat = gate_values.reshape(-1).astype(jnp.float32)
    slot_gates = jnp.sum(
        jnp.where(slot_match, gate_flat[None, :], jnp.zeros((), jnp.float32)), axis=1
    ).astype(jnp.bfloat16)
    return (dispatch_table, slot_gates)


def group_total(partial_sum, level_count):
    running = partial_sum
    for bit_pos in range(level_count):
        running = running + swapped(running, "pipe", bit_pos)
    return running


def shards(tokens, cotangent, route_a, route_b, gates_a, gates_b, w_up, w_down):
    pipe_size = lax.axis_size("pipe")
    half_size = pipe_size // 2
    level_count = half_size.bit_length() - 1
    expert_count = lax.axis_size("expert")
    pipe_index = lax.axis_index("pipe")
    upper_half = pipe_index >= half_size
    routing = jnp.where(upper_half, route_b, route_a)
    gate_values = jnp.where(upper_half, gates_b, gates_a)
    dispatch_table, slot_gates = slot_tables(routing, gate_values, expert_count, CAP)
    slot_count = expert_count * CAP
    sent_x = jnp.dot(dispatch_table, tokens, preferred_element_type=jnp.float32).astype(
        jnp.bfloat16
    )
    arrived_x, arrived_gates = (
        lax.all_to_all(
            sent_x.reshape(expert_count, CAP, -1), "expert", split_axis=0, concat_axis=0, tiled=True
        ),
        lax.all_to_all(
            slot_gates.reshape(expert_count, CAP), "expert", split_axis=0, concat_axis=0, tiled=True
        ),
    )
    slot_rows = arrived_x.reshape(slot_count, -1)
    gate_column = arrived_gates.reshape(slot_count, 1).astype(jnp.float32)
    up_weight = w_up[0]
    down_weight = w_down[0]
    partial_up = jnp.dot(slot_rows, up_weight, preferred_element_type=jnp.float32)
    hidden = group_total(partial_up, level_count)
    activated = (hidden * jax.nn.sigmoid(hidden)).astype(jnp.bfloat16)
    expert_out = (
        gate_column * jnp.dot(activated, down_weight, preferred_element_type=jnp.float32)
    ).astype(jnp.bfloat16)
    returned = lax.all_to_all(
        expert_out.reshape(expert_count, CAP, -1), "expert", split_axis=0, concat_axis=0, tiled=True
    )
    layer_out = lax.dot_general(
        dispatch_table,
        returned.reshape(slot_count, -1),
        (((0,), (0,)), ((), ())),
        preferred_element_type=jnp.float32,
    ).astype(jnp.bfloat16)
    sent_dy = jnp.dot(dispatch_table, cotangent, preferred_element_type=jnp.float32).astype(
        jnp.bfloat16
    )
    arrived_dy = lax.all_to_all(
        sent_dy.reshape(expert_count, CAP, -1), "expert", split_axis=0, concat_axis=0, tiled=True
    )
    d_out = (gate_column * arrived_dy.reshape(slot_count, -1).astype(jnp.float32)).astype(
        jnp.bfloat16
    )
    partial_back = lax.dot_general(
        d_out, down_weight, (((1,), (1,)), ((), ())), preferred_element_type=jnp.float32
    )
    d_act = group_total(partial_back, level_count)
    sigmoid_h = jax.nn.sigmoid(hidden)
    d_hidden = (d_act * sigmoid_h * (1.0 + hidden * (1.0 - sigmoid_h))).astype(jnp.bfloat16)
    d_rows = lax.dot_general(
        d_hidden, up_weight, (((1,), (1,)), ((), ())), preferred_element_type=jnp.float32
    ).astype(jnp.bfloat16)
    returned_dx = lax.all_to_all(
        d_rows.reshape(expert_count, CAP, -1), "expert", split_axis=0, concat_axis=0, tiled=True
    )
    grad_tokens = lax.dot_general(
        dispatch_table,
        returned_dx.reshape(slot_count, -1),
        (((0,), (0,)), ((), ())),
        preferred_element_type=jnp.float32,
    ).astype(jnp.bfloat16)
    weight_part = lax.dot_general(
        activated, d_out, (((0,), (0,)), ((), ())), preferred_element_type=jnp.float32
    ).astype(jnp.bfloat16)
    half_rows = weight_part.shape[0] // 2
    own_half = jnp.where(upper_half, weight_part[half_rows:], weight_part[:half_rows])
    travelling = jnp.where(upper_half, weight_part[:half_rows], weight_part[half_rows:])
    bit_order = list(range(level_count + 1))
    for bit_pos in bit_order:
        travelling = swapped(travelling, "pipe", bit_pos)
    grad_weight = (own_half.astype(jnp.float32) + travelling.astype(jnp.float32)).astype(
        jnp.bfloat16
    )
    return (layer_out, grad_tokens, grad_weight[None])


def solution(mesh):
    in_specs = (
        P("expert", "pipe"),
        P("expert", "pipe"),
        P("expert", None),
        P("expert", None),
        P("expert", None),
        P("expert", None),
        P("expert", "pipe", None),
        P("expert", None, "pipe"),
    )
    out_specs = (P("expert", "pipe"), P("expert", "pipe"), P("expert", None, "pipe"))
    return jax.shard_map(shards, mesh=mesh, in_specs=in_specs, out_specs=out_specs, check_vma=False)
```

profile of v0, /device:TPU:1, one launch (start us, length us, event | category | flops | bytes accessed | tf_op | source)
XLA Modules:
  0.0 374.9 jit_solution(18154066859950236840)
XLA Ops:
  0.6 0.0 copy-start
  0.7 0.9 copy.25
  1.6 0.8 copy.26
  2.4 0.1 eq.49
  2.5 0.1 eq.45
  2.7 9.1 %reduce-window.6 = s32[32,16,128]{2,1,0:T(8,128)S(1)} reduce-window(s32[32,16,128]{2,1,0:T(8,128)S(1)} %fusion.20, s32[]{:T(128)} %constant.9.clone.1), window={size=1x1x128 pad=0_0x0_0x127_0}, to_apply=%region_0.1 | reduce-window | flops 8323072 | bytes 524292 | tf_op jit(solution)/shard_map/reduce-window
  11.8 0.1 slice.18
  11.9 0.2 copy.33
  12.1 0.2 reduce-window.9
  12.3 0.1 add_add_fusion
  12.5 0.1 copy.30
  12.6 0.1 copy.31
  12.8 0.1 reshape.124
  12.9 0.1 fusion.19
  13.0 0.5 select_reduce_fusion
  13.5 0.7 convert_element_type.131
  14.2 11.1 %all-to-all-start = ((bf16[32,1,16]{2,1,0:T(2,128)(2,1)}), bf16[32,1,16]{2,1,0:T(2,128)(2,1)S(1)}, u32[]{:S(2)}, u32[]{:S(2)}) async-start(bf16[32,1,16]{2,1,0:T(2,128)(2,1)} %convert_element_type.131), calls=%async_computation | async-start | bytes 32768 | tf_op jit(solution)/shard_map/all_to_all | solution.py:63
  25.3 0.1 reduce_sum.21
  25.4 0.1 copy.29
  25.4 1.9 fusion
  27.4 1.9 convolution_convert_fusion.2
  29.3 3.8 %all-to-all-done = bf16[32,1,16]{2,1,0:T(2,128)(2,1)S(1)} async-done(((bf16[32,1,16]{2,1,0:T(2,128)(2,1)}), bf16[32,1,16]{2,1,0:T(2,128)(2,1)S(1)}, u32[]{:S(2)}, u32[]{:S(2)}) %all-to-all-start) | async-done | bytes 1056 | tf_op jit(solution)/shard_map/all_to_all | solution.py:63
  33.0 4.5 %all-to-all-start.1 = ((bf16[32,16,1792]{2,1,0:T(8,128)(2,1)}), bf16[32,16,1792]{2,1,0:T(8,128)(2,1)S(1)}, u32[]{:S(2)}, u32[]{:S(2)}) async-start(bf16[32,16,1792]{2,1,0:T(8,128)(2,1)} %bitcast.3), calls=%async_computation.1 | async-start | bytes 3670016 | tf_op jit(solution)/shard_map/all_to_all | solution.py:60
  37.6 3.1 convolution_convert_fusion.1
  40.7 40.7 %all-to-all-done.1 = bf16[32,16,1792]{2,1,0:T(8,128)(2,1)S(1)} async-done(((bf16[32,16,1792]{2,1,0:T(8,128)(2,1)}), bf16[32,16,1792]{2,1,0:T(8,128)(2,1)S(1)}, u32[]{:S(2)}, u32[]{:S(2)}) %all-to-all-start.1) | async-done | bytes 1835040 | tf_op jit(solution)/shard_map/all_to_all | solution.py:60
  81.4 1.2 copy-done.2
  82.6 5.5 %all-to-all-start.3 = ((bf16[32,16,1792]{2,1,0:T(8,128)(2,1)}), bf16[32,16,1792]{2,1,0:T(8,128)(2,1)S(1)}, u32[]{:S(2)}, u32[]{:S(2)}) async-start(bf16[32,16,1792]{2,1,0:T(8,128)(2,1)} %bitcast.59), calls=%async_computation.3 | async-start | bytes 3670016 | tf_op jit(solution)/shard_map/all_to_all | solution.py:89
  88.1 4.7 %fusion.8 = f32[512,1024]{1,0:T(8,128)S(1)} fusion(bf16[512,1792]{1,0:T(8,128)(2,1)} %bitcast.62, bf16[1,1792,1024]{2,1,0:T(8,128)(2,1)} %param.14), kind=kOutput, calls=%fused_computation.13 | convolution fusion | flops 1879048192 | bytes 7602176 | tf_op jit(solution)/shard_map/dot_general | solution.py:71
  92.8 2.5 collective-permute-start
  95.3 62.6 %collective-permute-done = f32[512,1024]{1,0:T(8,128)S(1)} collective-permute-done((f32[512,1024]{1,0:T(8,128)S(1)}, f32[512,1024]{1,0:T(8,128)S(1)}, u32[]{:S(2)}, u32[]{:S(2)}) %collective-permute-start) | collective-permute-done | bytes 2097184 | tf_op jit(solution)/shard_map/ppermute | solution.py:16
  157.9 1.7 add.37
  159.6 1.3 collective-permute-start.1
  160.9 0.0 copy-start.7
  160.9 0.4 multiply_convert_fusion
  161.3 1.7 copy-done.7
  163.0 3.4 fusion.2
  166.4 1.1 collective-permute-start.2
  167.5 0.1 convert_reduce_fusion
  167.6 0.1 reshape.125
  167.6 39.0 %collective-permute-done.1 = f32[512,1024]{1,0:T(8,128)} collective-permute-done((f32[512,1024]{1,0:T(8,128)}, f32[512,1024]{1,0:T(8,128)}, u32[]{:S(2)}, u32[]{:S(2)}) %collective-permute-start.1) | collective-permute-done | bytes 2097184 | tf_op jit(solution)/shard_map/ppermute | solution.py:16
  206.6 2.8 multiply_convert_fusion.3
  209.5 3.3 multiply_convert_fusion.1
  212.8 8.0 %all-to-all-start.2 = ((bf16[32,16,1792]{2,1,0:T(8,128)(2,1)}), bf16[32,16,1792]{2,1,0:T(8,128)(2,1)}, u32[]{:S(2)}, u32[]{:S(2)}) async-start(bf16[32,16,1792]{2,1,0:T(8,128)(2,1)} %bitcast.60), calls=%async_computation.2 | async-start | bytes 3670016 | tf_op jit(solution)/shard_map/all_to_all | solution.py:77
  220.8 0.0 collective-permute-done.2
  220.9 2.7 add.40
  223.6 1.4 collective-permute-start.3
  224.9 0.4 fusion.1
  225.3 2.1 convolution_convert_fusion
  227.5 0.0 copy-start.9
  227.5 1.4 broadcast_select_fusion
  228.9 1.3 copy-done.1
  230.2 2.3 collective-permute-start.4
  232.6 38.1 %collective-permute-done.3 = f32[512,1024]{1,0:T(8,128)S(1)} collective-permute-done((f32[512,1024]{1,0:T(8,128)S(1)}, f32[512,1024]{1,0:T(8,128)S(1)}, u32[]{:S(2)}, u32[]{:S(2)}) %collective-permute-start.3) | collective-permute-done | bytes 2097184 | tf_op jit(solution)/shard_map/ppermute | solution.py:16
  270.7 6.3 %fusion.12 = bf16[512,1792]{1,0:T(8,128)(2,1)} fusion(bf16[1,1792,1024]{2,1,0:T(8,128)(2,1)S(1)} %copy-done.9, f32[512,1024]{1,0:T(8,128)S(1)} %add.40, f32[512,1024]{1,0:T(8,128)S(1)} %collective-permute-done.3, f32[512,1024]{1,0:T(8,128)} %add.37, f32[512,1024]{1,0:T(8,128)} %collective-permute-done.1), kind=kOutput, calls=%fused_computation.18 | convolution fusion | flops 1885732864 | bytes 13893632 | tf_op jit(solution)/shard_map/dot_general | solution.py:101
  276.9 0.0 all-to-all-done.2
  276.9 9.0 %all-to-all-start.4 = ((bf16[32,16,1792]{2,1,0:T(8,128)(2,1)}), bf16[32,16,1792]{2,1,0:T(8,128)(2,1)S(1)}, u32[]{:S(2)}, u32[]{:S(2)}) async-start(bf16[32,16,1792]{2,1,0:T(8,128)(2,1)} %bitcast.61), calls=%async_computation.4 | async-start | bytes 3670016 | tf_op jit(solution)/shard_map/all_to_all | solution.py:104
  285.9 1.4 collective-permute-done.4
  287.3 1.4 collective-permute-start.5
  288.7 39.7 %collective-permute-done.5 = bf16[512,1792]{1,0:T(8,128)(2,1)} collective-permute-done((bf16[512,1792]{1,0:T(8,128)(2,1)}, bf16[512,1792]{1,0:T(8,128)(2,1)}, u32[]{:S(2)}, u32[]{:S(2)}) %collective-permute-start.5) | collective-permute-done | bytes 1835040 | tf_op jit(solution)/shard_map/ppermute | solution.py:16
  328.3 3.2 collective-permute-start.6
  331.5 3.1 convolution_convert_fusion.4
  334.6 1.6 convolution_convert_fusion.3
  336.2 34.2 %collective-permute-done.6 = bf16[512,1792]{1,0:T(8,128)(2,1)} collective-permute-done((bf16[512,1792]{1,0:T(8,128)(2,1)}, bf16[512,1792]{1,0:T(8,128)(2,1)}, u32[]{:S(2)}, u32[]{:S(2)}) %collective-permute-start.6) | collective-permute-done | bytes 1835040 | tf_op jit(solution)/shard_map/ppermute | solution.py:16
  370.4 4.5 %fusion.15 = bf16[1,512,1792]{2,1,0:T(8,128)(2,1)} fusion(bf16[512,1792]{1,0:T(8,128)(2,1)} %collective-permute-done.6, pred[]{:T(512)S(6)} %ge.3, bf16[1024,1792]{1,0:T(8,128)(2,1)} %copy-done.1), kind=kLoop, calls=%fused_computation.26 | loop fusion | flops 4587520 | bytes 7340033 | tf_op jit(solution)/shard_map/broadcast_in_dim | solution.py:125
  (22 shorter events, 0.1 us)
Async XLA Ops:
  0.6 26.7 %copy-start = (bf16[256,1792]{1,0:T(8,128)(2,1)S(1)}, bf16[256,1792]{1,0:T(8,128)(2,1)}, u32[]{:S(2)}) copy-start(bf16[256,1792]{1,0:T(8,128)(2,1)} %param.8) | copy-start | bytes 2752516
  0.6 11.8 %copy-start.5 = (bf16[256,8]{0,1:T(8,128)(2,1)S(1)}, bf16[256,8]{0,1:T(8,128)(2,1)}, u32[]{:S(2)}) copy-start(bf16[256,8]{0,1:T(8,128)(2,1)} %param.13) | copy-start | bytes 12292
  0.7 12.0 %copy-start.6 = (bf16[256,8]{0,1:T(8,128)(2,1)S(1)}, bf16[256,8]{0,1:T(8,128)(2,1)}, u32[]{:S(2)}) copy-start(bf16[256,8]{0,1:T(8,128)(2,1)} %param.12) | copy-start | bytes 12292
  14.2 18.8 %all-to-all-start = ((bf16[32,1,16]{2,1,0:T(2,128)(2,1)}), bf16[32,1,16]{2,1,0:T(2,128)(2,1)S(1)}, u32[]{:S(2)}, u32[]{:S(2)}) async-start(bf16[32,1,16]{2,1,0:T(2,128)(2,1)} %convert_element_type.131), calls=%async_computation | async-start | bytes 32768 | tf_op jit(solution)/shard_map/all_to_all | solution.py:63
  33.0 48.4 %all-to-all-start.1 = ((bf16[32,16,1792]{2,1,0:T(8,128)(2,1)}), bf16[32,16,1792]{2,1,0:T(8,128)(2,1)S(1)}, u32[]{:S(2)}, u32[]{:S(2)}) async-start(bf16[32,16,1792]{2,1,0:T(8,128)(2,1)} %bitcast.3), calls=%async_computation.1 | async-start | bytes 3670016 | tf_op jit(solution)/shard_map/all_to_all | solution.py:60
  81.4 1.2 copy-start.2
  82.6 78.3 %all-to-all-start.3 = ((bf16[32,16,1792]{2,1,0:T(8,128)(2,1)}), bf16[32,16,1792]{2,1,0:T(8,128)(2,1)S(1)}, u32[]{:S(2)}, u32[]{:S(2)}) async-start(bf16[32,16,1792]{2,1,0:T(8,128)(2,1)} %bitcast.59), calls=%async_computation.3 | async-start | bytes 3670016 | tf_op jit(solution)/shard_map/all_to_all | solution.py:89
  92.8 65.1 %collective-permute-start = (f32[512,1024]{1,0:T(8,128)S(1)}, f32[512,1024]{1,0:T(8,128)S(1)}, u32[]{:S(2)}, u32[]{:S(2)}) collective-permute-start(f32[512,1024]{1,0:T(8,128)S(1)} %fusion.8), channel_id=1, source_target_pairs={{0,32},{32,0},{64,96},{96,64},{128,160},{160,128},{192,224},{224,1... | collective-permute-start | bytes 6291464 | tf_op jit(solution)/shard_map/ppermute | solution.py:16
  159.6 47.0 %collective-permute-start.1 = (f32[512,1024]{1,0:T(8,128)}, f32[512,1024]{1,0:T(8,128)}, u32[]{:S(2)}, u32[]{:S(2)}) collective-permute-start(f32[512,1024]{1,0:T(8,128)} %add.37), channel_id=1, source_target_pairs={{0,64},{64,0},{32,96},{96,32},{128,192},{192,128},{160,224},{224,1... | collective-permute-start | bytes 6291464 | tf_op jit(solution)/shard_map/ppermute | solution.py:16
  160.9 2.0 copy-start.7
  166.4 54.5 %collective-permute-start.2 = (f32[512,1024]{1,0:T(8,128)}, f32[512,1024]{1,0:T(8,128)}, u32[]{:S(2)}, u32[]{:S(2)}) collective-permute-start(f32[512,1024]{1,0:T(8,128)} %fusion.2), channel_id=1, source_target_pairs={{0,32},{32,0},{64,96},{96,64},{128,160},{160,128},{192,224},{224,1... | collective-permute-start | bytes 6291464 | tf_op jit(solution)/shard_map/ppermute | solution.py:16
  167.6 41.8 %copy-start.8 = (bf16[1,1024,1792]{2,1,0:T(8,128)(2,1)S(1)}, bf16[1,1024,1792]{2,1,0:T(8,128)(2,1)}, u32[]{:S(2)}) copy-start(bf16[1,1024,1792]{2,1,0:T(8,128)(2,1)} %param.15) | copy-start | bytes 11010052
  209.5 3.3 copy-start.3
  212.8 64.1 %all-to-all-start.2 = ((bf16[32,16,1792]{2,1,0:T(8,128)(2,1)}), bf16[32,16,1792]{2,1,0:T(8,128)(2,1)}, u32[]{:S(2)}, u32[]{:S(2)}) async-start(bf16[32,16,1792]{2,1,0:T(8,128)(2,1)} %bitcast.60), calls=%async_computation.2 | async-start | bytes 3670016 | tf_op jit(solution)/shard_map/all_to_all | solution.py:77
  223.5 1.8 copy-start.4
  223.6 47.1 %collective-permute-start.3 = (f32[512,1024]{1,0:T(8,128)S(1)}, f32[512,1024]{1,0:T(8,128)S(1)}, u32[]{:S(2)}, u32[]{:S(2)}) collective-permute-start(f32[512,1024]{1,0:T(8,128)S(1)} %add.40), channel_id=1, source_target_pairs={{0,64},{64,0},{32,96},{96,32},{128,192},{192,128},{160,224},{224,1... | collective-permute-start | bytes 6291464 | tf_op jit(solution)/shard_map/ppermute | solution.py:16
  227.4 2.8 copy-start.1
  227.5 43.2 %copy-start.9 = (bf16[1,1792,1024]{2,1,0:T(8,128)(2,1)S(1)}, bf16[1,1792,1024]{2,1,0:T(8,128)(2,1)}, u32[]{:S(2)}) copy-start(bf16[1,1792,1024]{2,1,0:T(8,128)(2,1)} %param.14) | copy-start | bytes 11010052
  230.2 57.0 %collective-permute-start.4 = (bf16[512,1792]{1,0:T(8,128)(2,1)}, bf16[512,1792]{1,0:T(8,128)(2,1)}, u32[]{:S(2)}, u32[]{:S(2)}) collective-permute-start(bf16[512,1792]{1,0:T(8,128)(2,1)} %broadcast_select_fusion), channel_id=1, source_target_pairs={{0,32},{32,0},{64,96},{96,64},{128,160},{160,128},{192,224},{224,1... | collective-permute-start | bytes 5505032 | tf_op jit(solution)/shard_map/ppermute | solution.py:16
  276.9 57.7 %all-to-all-start.4 = ((bf16[32,16,1792]{2,1,0:T(8,128)(2,1)}), bf16[32,16,1792]{2,1,0:T(8,128)(2,1)S(1)}, u32[]{:S(2)}, u32[]{:S(2)}) async-start(bf16[32,16,1792]{2,1,0:T(8,128)(2,1)} %bitcast.61), calls=%async_computation.4 | async-start | bytes 3670016 | tf_op jit(solution)/shard_map/all_to_all | solution.py:104
  287.3 41.1 %collective-permute-start.5 = (bf16[512,1792]{1,0:T(8,128)(2,1)}, bf16[512,1792]{1,0:T(8,128)(2,1)}, u32[]{:S(2)}, u32[]{:S(2)}) collective-permute-start(bf16[512,1792]{1,0:T(8,128)(2,1)} %collective-permute-done.4), channel_id=1, source_target_pairs={{0,64},{64,0},{32,96},{96,32},{128,192},{192,128},{160,224},{224,1... | collective-permute-start | bytes 5505032 | tf_op jit(solution)/shard_map/ppermute | solution.py:16
  328.3 42.1 %collective-permute-start.6 = (bf16[512,1792]{1,0:T(8,128)(2,1)}, bf16[512,1792]{1,0:T(8,128)(2,1)}, u32[]{:S(2)}, u32[]{:S(2)}) collective-permute-start(bf16[512,1792]{1,0:T(8,128)(2,1)} %collective-permute-done.5), channel_id=1, source_target_pairs={{0,128},{128,0},{32,160},{160,32},{64,192},{192,64},{96,224},{224,... | collective-permute-start | bytes 5505032 | tf_op jit(solution)/shard_map/ppermute | solution.py:16
where the time goes:
time: 377 us; the launch traced here: 375 us
  waiting for transfers between devices  259 us (69%)
  starting transfers between devices  51.3 us (14%)
  matrix products  29.5 us (8%)
  other arithmetic  26 us (7%)
  local copies, waits for them, and re-layouts  7.87 us (2%)
    ppermute x7, waiting for transfers between devices, swapped(): return lax.ppermute(block, axis, route)  215 us
    all_to_all x1, waiting for transfers between devices, shards(): lax.all_to_all(sent_x.reshape(expert_count, CAP, -1), 'expert', split_axi...  40.7 us
    ppermute x7, starting transfers between devices, swapped(): return lax.ppermute(block, axis, route)  13.2 us
    all_to_all x1, starting transfers between devices, shards(): lax.all_to_all(slot_gates.reshape(expert_count, CAP), 'expert', split_axi...  11.1 us
    another operation x2, other arithmetic  9.27 us
    all_to_all x1, starting transfers between devices, shards(): lax.all_to_all(d_rows.reshape(expert_count, CAP, -1), 'expert', split_axi...  8.96 us
    all_to_all x1, starting transfers between devices, shards(): lax.all_to_all(expert_out.reshape(expert_count, CAP, -1), 'expert', split...  8.04 us
  transfers between devices with their start and end apart: 12, of which 8 were waited for; matrix products, arithmetic and copies ran while one was open for 11% of the time, Pallas kernels for 0%

commit v1 on v0

v1 whole, which is shorter than its diff:
```python
import functools

import jax
import jax.numpy as jnp
from jax import lax
from jax.experimental import pallas as pl
from jax.experimental.pallas import tpu as pltpu
from jax.sharding import PartitionSpec as P

CAP = 16
BF = jnp.bfloat16
F32 = jnp.float32


def params(megabytes):
    return pltpu.CompilerParams(vmem_limit_bytes=megabytes * 1024 * 1024)


def whole(shape):
    return pl.BlockSpec(shape, lambda i, m: (0,) * len(shape))


def dot(a, b, ca, cb):
    return lax.dot_general(a, b, (((ca,), (cb,)), ((), ())), preferred_element_type=F32)


def column_block(width):
    for size in (256, 128):
        if width % size == 0:
            return size
    return width


def dispatch_kernel(side_ref, ra_ref, rb_ref, ga_ref, gb_ref, x_ref, out_ref, plain_ref, gated_ref):
    @pl.when(pl.program_id(0) == 0)
    def _():
        upper = side_ref[1] == 1
        route = jnp.where(upper, rb_ref[...], ra_ref[...])
        gates = jnp.where(upper, gb_ref[...].astype(F32), ga_ref[...].astype(F32))
        top, tokens = route.shape
        slots = plain_ref.shape[0]
        experts = slots // CAP
        expert = lax.broadcasted_iota(jnp.int32, (experts, tokens), 0)
        member = jnp.zeros((experts, tokens), F32)
        gate = jnp.zeros((experts, tokens), F32)
        for k in range(top):
            named = route[k : k + 1, :] == expert
            member = member + jnp.where(named, 1.0, 0.0)
            gate = gate + jnp.where(named, gates[k : k + 1, :], 0.0)
        before = lax.broadcasted_iota(jnp.int32, (tokens, tokens), 0) < lax.broadcasted_iota(
            jnp.int32, (tokens, tokens), 1
        )
        earlier = dot(member.astype(BF), jnp.where(before, 1.0, 0.0).astype(BF), 1, 0)
        place = jnp.where(member > 0.5, earlier, 128.0).astype(BF)
        row = lax.broadcasted_iota(jnp.int32, (slots, experts), 0)
        column = lax.broadcasted_iota(jnp.int32, (slots, experts), 1)
        spread = jnp.where(row // CAP == column, 1.0, 0.0).astype(BF)
        place_rows = dot(spread, place, 1, 0)
        gate_rows = dot(spread, gate.astype(BF), 1, 0)
        slot = lax.broadcasted_iota(jnp.int32, (slots, tokens), 0) % CAP
        hit = place_rows == slot.astype(F32)
        plain_ref[...] = jnp.where(hit, 1.0, 0.0).astype(BF)
        gated_ref[...] = jnp.where(hit, gate_rows, 0.0).astype(BF)

    out_ref[...] = dot(plain_ref[...], x_ref[...], 1, 0).astype(BF)


def dispatch(side, route_a, route_b, gates_a, gates_b, x, slots):
    tokens, width = x.shape
    cols = column_block(width)
    small = whole((route_a.shape[1], tokens))
    return pl.pallas_call(
        dispatch_kernel,
        grid_spec=pltpu.PrefetchScalarGridSpec(
            num_scalar_prefetch=1,
            grid=(width // cols,),
            in_specs=[small] * 4 + [pl.BlockSpec((tokens, cols), lambda i, m: (0, i))],
            out_specs=[
                pl.BlockSpec((slots, cols), lambda i, m: (0, i)),
                whole((slots, tokens)),
                whole((slots, tokens)),
            ],
        ),
        out_shape=[
            jax.ShapeDtypeStruct((slots, width), BF),
            jax.ShapeDtypeStruct((slots, tokens), BF),
            jax.ShapeDtypeStruct((slots, tokens), BF),
        ],
        compiler_params=params(16),
        name="dispatch",
    )(side, route_a.T, route_b.T, gates_a.T, gates_b.T, x)


def partial_kernel(side_ref, x_ref, w_ref, own_ref, s1_ref, s2_ref, s3_ref, *, cb):
    j = pl.program_id(0)
    part = dot(x_ref[...], w_ref[...], 1, cb)
    for step, ref in ((0, s1_ref), (1, s2_ref), (2, s3_ref)):

        @pl.when(j == step)
        def _(ref=ref):
            ref[...] = part.astype(BF)

    @pl.when(j == 3)
    def _():
        own_ref[...] = part


def partials(side, x, w, transposed):
    rows, depth = x.shape
    hid = (w.shape[0] if transposed else w.shape[1]) // 4
    if transposed:
        w_spec = pl.BlockSpec((hid, depth), lambda i, m: (m[0] ^ ((i + 1) % 4), 0))
    else:
        w_spec = pl.BlockSpec((depth, hid), lambda i, m: (0, m[0] ^ ((i + 1) % 4)))
    return pl.pallas_call(
        functools.partial(partial_kernel, cb=1 if transposed else 0),
        grid_spec=pltpu.PrefetchScalarGridSpec(
            num_scalar_prefetch=1,
            grid=(4,),
            in_specs=[whole((rows, depth)), w_spec],
            out_specs=[whole((rows, hid))] * 4,
        ),
        out_shape=[jax.ShapeDtypeStruct((rows, hid), F32)]
        + [jax.ShapeDtypeStruct((rows, hid), BF)] * 3,
        compiler_params=params(24),
        cost_estimate=pl.CostEstimate(
            flops=2 * rows * depth * hid * 4,
            bytes_accessed=2 * (rows * depth + 4 * depth * hid) + 10 * rows * hid,
            transcendentals=0,
        ),
        name="partials",
    )(side, x, w)


def merge_kernel(side_ref, a0_ref, a1_ref, a2_ref, a3_ref, w_ref, out_ref, *, transposed):
    total = None
    hid = a0_ref.shape[1]
    for j, ref in enumerate((a0_ref, a1_ref, a2_ref, a3_ref)):
        start = pl.multiple_of((side_ref[0] ^ j) * hid, hid)
        block = w_ref[:, pl.ds(start, hid)] if transposed else w_ref[pl.ds(start, hid), :]
        part = dot(ref[...], block, 1, 1 if transposed else 0)
        total = part if total is None else total + part
    out_ref[...] = total.astype(BF)


def merged(side, pieces, w, transposed):
    rows, hid = pieces[0].shape
    width = w.shape[0] if transposed else w.shape[1]
    cols = column_block(width)
    if transposed:
        w_spec = pl.BlockSpec((cols, 4 * hid), lambda i, m: (i, 0))
    else:
        w_spec = pl.BlockSpec((4 * hid, cols), lambda i, m: (0, i))
    return pl.pallas_call(
        functools.partial(merge_kernel, transposed=transposed),
        grid_spec=pltpu.PrefetchScalarGridSpec(
            num_scalar_prefetch=1,
            grid=(width // cols,),
            in_specs=[whole((rows, hid))] * 4 + [w_spec],
            out_specs=pl.BlockSpec((rows, cols), lambda i, m: (0, i)),
        ),
        out_shape=jax.ShapeDtypeStruct((rows, width), BF),
        compiler_params=params(24),
        cost_estimate=pl.CostEstimate(
            flops=2 * rows * width * hid * 4,
            bytes_accessed=2 * (rows * width + 4 * width * hid + 4 * rows * hid),
            transcendentals=0,
        ),
        name="merged",
    )(side, *pieces, w)


def weight_kernel(side_ref, a0_ref, a1_ref, a2_ref, a3_ref, d_ref, own_ref, send_ref, act_ref):
    hid = a0_ref.shape[1]

    @pl.when(pl.program_id(0) == 0)
    def _():
        for j, ref in enumerate((a0_ref, a1_ref, a2_ref, a3_ref)):
            start = pl.multiple_of((side_ref[0] ^ j) * hid, hid)
            act_ref[:, pl.ds(start, hid)] = ref[...]

    for half, ref in ((side_ref[1], own_ref), (1 - side_ref[1], send_ref)):
        act = act_ref[:, pl.ds(pl.multiple_of(half * (2 * hid), 2 * hid), 2 * hid)]
        ref[...] = dot(act, d_ref[...], 0, 0).astype(BF)


def weight_parts(side, pieces, d_out):
    rows, hid = pieces[0].shape
    width = d_out.shape[1]
    cols = column_block(width)
    return pl.pallas_call(
        weight_kernel,
        grid_spec=pltpu.PrefetchScalarGridSpec(
            num_scalar_prefetch=1,
            grid=(width // cols,),
            in_specs=[whole((rows, hid))] * 4 + [pl.BlockSpec((rows, cols), lambda i, m: (0, i))],
            out_specs=[pl.BlockSpec((2 * hid, cols), lambda i, m: (0, i))] * 2,
            scratch_shapes=[pltpu.VMEM((rows, 4 * hid), BF)],
        ),
        out_shape=[jax.ShapeDtypeStruct((2 * hid, width), BF)] * 2,
        compiler_params=params(24),
        cost_estimate=pl.CostEstimate(
            flops=2 * rows * width * hid * 4,
            bytes_accessed=2 * (rows * width + 4 * width * hid + 4 * rows * hid),
            transcendentals=0,
        ),
        name="weight_parts",
    )(side, *pieces, d_out)


def to_members(blocks):
    count = lax.axis_size("pipe")
    return [
        lax.ppermute(block, "pipe", [(p, p ^ (j + 1)) for p in range(count)])
        for j, block in enumerate(blocks)
    ]


def exchange(rows):
    experts = lax.axis_size("expert")
    blocks = rows.reshape(experts, CAP, -1)
    blocks = lax.all_to_all(blocks, "expert", split_axis=0, concat_axis=0, tiled=True)
    return blocks.reshape(experts * CAP, -1)


def shards(tokens, cotangent, route_a, route_b, gates_a, gates_b, w_up, w_down):
    pipe_size = lax.axis_size("pipe")
    half_size = pipe_size // 2
    slots = lax.axis_size("expert") * CAP
    pipe = lax.axis_index("pipe")
    side = jnp.stack([pipe % half_size, pipe // half_size]).astype(jnp.int32)
    up, down = w_up[0], w_down[0]

    sent_x, plain, gated = dispatch(side, route_a, route_b, gates_a, gates_b, tokens, slots)
    rows_x = exchange(sent_x)
    d_out = exchange(dot(gated, cotangent, 1, 0).astype(BF))

    own, *others = partials(side, rows_x, up, False)
    hidden = own + sum(block.astype(F32) for block in to_members(others))
    sigmoid = jax.nn.sigmoid(hidden)
    act = (hidden * sigmoid).astype(BF)
    acts = [act] + to_members([act] * 3)
    returned = exchange(merged(side, acts, down, False))

    own, *others = partials(side, d_out, down, True)
    d_act = own + sum(block.astype(F32) for block in to_members(others))
    d_hidden = (d_act * sigmoid * (1.0 + hidden * (1.0 - sigmoid))).astype(BF)
    d_hiddens = [d_hidden] + to_members([d_hidden] * 3)
    returned_dx = exchange(merged(side, d_hiddens, up, True))

    own_weight, travelling = weight_parts(side, acts, d_out)
    arrived = lax.ppermute(travelling, "pipe", [(p, pipe_size - 1 - p) for p in range(pipe_size)])
    grad_weight = (own_weight.astype(F32) + arrived.astype(F32)).astype(BF)

    layer_out = dot(gated, returned, 0, 0).astype(BF)
    grad_tokens = dot(plain, returned_dx, 0, 0).astype(BF)
    return (layer_out, grad_tokens, grad_weight[None])


def solution(mesh):
    in_specs = (
        P("expert", "pipe"),
        P("expert", "pipe"),
        P("expert", None),
        P("expert", None),
        P("expert", None),
        P("expert", None),
        P("expert", "pipe", None),
        P("expert", None, "pipe"),
    )
    out_specs = (P("expert", "pipe"), P("expert", "pipe"), P("expert", None, "pipe"))
    return jax.shard_map(shards, mesh=mesh, in_specs=in_specs, out_specs=out_specs, check_vma=False)
```

time: 377 us -> 292 us (0.77)
  waiting for transfers between devices: 259 us -> 140 us
  blocking collectives: 0 us -> 54.5 us
  Pallas kernels: 0 us -> 25.5 us
  matrix products: 29.5 us -> 6.85 us
  other arithmetic: 26 us -> 4.04 us
  local copies, waits for them, and re-layouts: 7.87 us -> 15.7 us
  starting transfers between devices: 51.3 us -> 43.5 us
    ppermute x7 -> x13, waiting for transfers between devices: 215 us -> 95.3 us  [the longest x1 55.5 us: shards(): lax.ppermute(travelling, 'pipe', [(p, pipe_size - 1 - p) for p in range(p...]
    all_to_all x0 -> x1, blocking collectives: none -> 54.5 us  [exchange(): lax.all_to_all(blocks, 'expert', split_axis=0, concat_axis=0, tiled=True)]
    pallas_call x0 -> x6, Pallas kernels: none -> 25.5 us  [the longest x2 9.89 us: partials(): pl.pallas_call(functools.partial(partial_kernel, cb=1 if transposed else...]
    dot_general x9 -> x3, matrix products: 29.5 us -> 6.85 us  [dot(): lax.dot_general(a, b, (((ca,), (cb,)), ((), ())), preferred_element_type=...]
    all_to_all x5 -> x3, starting transfers between devices: 38.1 us -> 22.2 us  [exchange(): lax.all_to_all(blocks, 'expert', split_axis=0, concat_axis=0, tiled=True)]
    unnamed x24 -> x44, local copies, waits for them, and re-layouts: 6.24 us -> 15.7 us
    another operation x2 -> x1, other arithmetic: 9.27 us -> 0.08 us  [shards(): side = jnp.stack([pipe % half_size, pipe // half_size]).astype(jnp.int32)]
    ppermute x7 -> x13, starting transfers between devices: 13.2 us -> 21.3 us  [the longest x12 16.8 us: to_members(): lax.ppermute(block, 'pipe', [(p, p ^ j + 1) for p in range(count)])]
  transfers between devices with their start and end apart: 12 -> 16, of which waited for: 8 -> 12; matrix products, arithmetic and copies ran while one was open for 11% -> 2% of each run, Pallas kernels for 0% -> 6%
where the time goes in v1:
time: 292 us; the launch traced here: 291 us
  waiting for transfers between devices  140 us (48%)
  blocking collectives  54.5 us (19%)
  starting transfers between devices  43.5 us (15%)
  Pallas kernels  25.5 us (9%)
  local copies, waits for them, and re-layouts  15.7 us (5%)
  matrix products  6.85 us (2%)
  other arithmetic  4.04 us (1%)
    ppermute x1, waiting for transfers between devices, shards(): lax.ppermute(travelling, 'pipe', [(p, pipe_size - 1 - p) for p in range(p...  55.5 us
    all_to_all x1, blocking collectives, exchange(): lax.all_to_all(blocks, 'expert', split_axis=0, concat_axis=0, tiled=True)  54.5 us
    all_to_all x3, waiting for transfers between devices, exchange(): lax.all_to_all(blocks, 'expert', split_axis=0, concat_axis=0, tiled=True)  45.1 us
    ppermute x12, waiting for transfers between devices, to_members(): lax.ppermute(block, 'pipe', [(p, p ^ j + 1) for p in range(count)])  39.8 us
    all_to_all x3, starting transfers between devices, exchange(): lax.all_to_all(blocks, 'expert', split_axis=0, concat_axis=0, tiled=True)  22.2 us
    ppermute x12, starting transfers between devices, to_members(): lax.ppermute(block, 'pipe', [(p, p ^ j + 1) for p in range(count)])  16.8 us
    unnamed x44, local copies, waits for them, and re-layouts  15.7 us
    pallas_call x2, Pallas kernels, partials(): pl.pallas_call(functools.partial(partial_kernel, cb=1 if transposed else...  9.89 us
  transfers between devices with their start and end apart: 16, of which 12 were waited for; matrix products, arithmetic and copies ran while one was open for 2% of the time, Pallas kernels for 6%

profile of v1, /device:TPU:1, one launch (start us, length us, event | category | flops | bytes accessed | tf_op | source)
XLA Modules:
  0.0 291.4 jit_solution(12229759986467982496)
XLA Ops:
  0.6 0.0 copy-start
  0.7 0.1 pad_add_fusion.side_ref
  0.7 1.2 copy-done.4
  2.0 0.7 copy-done.10
  2.7 0.7 copy-done.11
  3.4 0.7 copy-done.12
  4.1 0.7 copy-done.13
  4.8 2.9 dispatch.1
  7.6 0.0 copy-start.3
  7.6 1.2 copy-done.3
  8.9 0.6 convolution_convert_fusion
  9.5 54.5 %all_to_all.20 = bf16[32,16,1792]{2,1,0:T(8,128)(2,1)S(1)} all-to-all(bf16[32,16,1792]{2,1,0:T(8,128)(2,1)S(1)} %bitcast.37), channel_id=1, replica_groups=mesh['pipe'=8,'expert'=32] {'expert'}, dimensions={0} | all-to-all | bytes 3670016 | tf_op jit(solution)/shard_map/all_to_all | solution.py:222
  64.0 6.7 %all-to-all-start = ((bf16[32,16,1792]{2,1,0:T(8,128)(2,1)}), bf16[32,16,1792]{2,1,0:T(8,128)(2,1)}, u32[]{:S(2)}, u32[]{:S(2)}) async-start(bf16[32,16,1792]{2,1,0:T(8,128)(2,1)} %bitcast.28), calls=%async_computation | async-start | bytes 3670016 | tf_op jit(solution)/shard_map/all_to_all | solution.py:222
  70.8 0.0 copy-start.14
  70.8 2.0 copy-done.14
  72.8 4.3 %partials.3 = (f32[512,256]{1,0:T(8,128)S(1)}, bf16[512,256]{1,0:T(8,128)(2,1)}, bf16[512,256]{1,0:T(8,128)(2,1)}, bf16[512,256]{1,0:T(8,128)(2,1)}) custom-call(s32[2]{0:T(128)S(1)} %pad_add_fusion.side_ref, bf16[512,1792]{1,0:T(8,128)(2,1)S(1)} %bitcast.24, bf16[1024,1792]{1,0:T(8,128)(2,1)S(1)} %bitcast.33), custom_call_target="tpu_custom_call" | custom-call | flops 1879048192 | bytes 6815744 | tf_op jit(solution)/shard_map/partials/pallas_call | solution.py:115
  77.1 2.5 collective-permute-start.6
  79.6 1.3 collective-permute-start.7
  80.9 0.4 collective-permute-start.8
  81.3 33.4 %all-to-all-done = bf16[32,16,1792]{2,1,0:T(8,128)(2,1)} async-done(((bf16[32,16,1792]{2,1,0:T(8,128)(2,1)}), bf16[32,16,1792]{2,1,0:T(8,128)(2,1)}, u32[]{:S(2)}, u32[]{:S(2)}) %all-to-all-start) | async-done | bytes 1835040 | tf_op jit(solution)/shard_map/all_to_all | solution.py:222
  114.7 2.0 copy-done.16
  116.7 5.6 %partials.2 = (f32[512,256]{1,0:T(8,128)S(1)}, bf16[512,256]{1,0:T(8,128)(2,1)S(1)}, bf16[512,256]{1,0:T(8,128)(2,1)S(1)}, bf16[512,256]{1,0:T(8,128)(2,1)S(1)}) custom-call(s32[2]{0:T(128)S(1)} %pad_add_fusion.side_ref, bf16[512,1792]{1,0:T(8,128)(2,1)} %bitcast.7.x_ref, bf16[1792,1024]{1,0:T(8,128)(2,1)S(1)} %bitcast.35), custom_call_target="tpu_custom_call" | custom-call | flops 1879048192 | bytes 6815744 | tf_op jit(solution)/shard_map/partials/pallas_call | solution.py:115
  122.3 2.5 collective-permute-start
  124.9 1.3 collective-permute-start.1
  126.2 0.0 collective-permute-done.6
  126.2 0.4 collective-permute-start.2
  126.6 0.0 collective-permute-done.7
  126.6 0.0 collective-permute-done.8
  126.6 3.8 %collective-permute-done = bf16[512,256]{1,0:T(8,128)(2,1)S(1)} collective-permute-done((bf16[512,256]{1,0:T(8,128)(2,1)S(1)}, bf16[512,256]{1,0:T(8,128)(2,1)S(1)}, u32[]{:S(2)}, u32[]{:S(2)}) %collective-permute-start) | collective-permute-done | bytes 262176 | tf_op jit(solution)/shard_map/ppermute | solution.py:214
  130.4 0.7 collective-permute-done.1
  131.0 6.0 %collective-permute-done.2 = bf16[512,256]{1,0:T(8,128)(2,1)S(1)} collective-permute-done((bf16[512,256]{1,0:T(8,128)(2,1)S(1)}, bf16[512,256]{1,0:T(8,128)(2,1)S(1)}, u32[]{:S(2)}, u32[]{:S(2)}) %collective-permute-start.2) | collective-permute-done | bytes 262176 | tf_op jit(solution)/shard_map/ppermute | solution.py:214
  137.0 2.2 multiply_convert_fusion
  139.2 2.5 collective-permute-start.3
  141.7 0.2 collective-permute-start.4
  141.9 1.5 collective-permute-start.5
  143.4 2.9 collective-permute-done.3.a1_ref
  146.3 1.4 collective-permute-done.4.a2_ref
  147.7 4.5 %collective-permute-done.5.a3_ref = bf16[512,256]{1,0:T(8,128)(2,1)S(1)} collective-permute-done((bf16[512,256]{1,0:T(8,128)(2,1)S(1)}, bf16[512,256]{1,0:T(8,128)(2,1)S(1)}, u32[]{:S(2)}, u32[]{:S(2)}) %collective-permute-start.5) | collective-permute-done | bytes 262176 | tf_op jit(solution)/shard_map/ppermute | solution.py:214
  152.2 4.0 %merged.2 = bf16[512,1792]{1,0:T(8,128)(2,1)S(1)} custom-call(s32[2]{0:T(128)S(1)} %pad_add_fusion.side_ref, bf16[512,256]{1,0:T(8,128)(2,1)S(1)} %get-tuple-element.30.a0_ref, bf16[512,256]{1,0:T(8,128)(2,1)S(1)} %collective-permute-done.3.a1_ref, bf16[512,256]{1,0:T(8,128)(2,1)S(1)} %collective-permute-done.4.a2_ref, ...), custom_call_target="tpu_custom_call" | custom-call | flops 1879048192 | bytes 6553600 | tf_op jit(solution)/shard_map/merged/pallas_call | solution.py:154
  156.2 0.0 copy-done.7
  156.2 0.0 copy-done.18
  156.2 0.0 copy-start.2
  156.2 1.2 copy-done.2
  157.4 9.6 %all-to-all-start.1 = ((bf16[32,16,1792]{2,1,0:T(8,128)(2,1)}), bf16[32,16,1792]{2,1,0:T(8,128)(2,1)}, u32[]{:S(2)}, u32[]{:S(2)}) async-start(bf16[32,16,1792]{2,1,0:T(8,128)(2,1)} %bitcast.27), calls=%async_computation.1 | async-start | bytes 3670016 | tf_op jit(solution)/shard_map/all_to_all | solution.py:222
  167.0 0.9 collective-permute-start.10
  168.0 2.3 collective-permute-start.11
  170.3 1.0 collective-permute-start.9
  171.3 5.0 %collective-permute-done.10.a2_ref = bf16[512,256]{1,0:T(8,128)(2,1)S(1)} collective-permute-done((bf16[512,256]{1,0:T(8,128)(2,1)S(1)}, bf16[512,256]{1,0:T(8,128)(2,1)S(1)}, u32[]{:S(2)}, u32[]{:S(2)}) %collective-permute-start.10) | collective-permute-done | bytes 262176 | tf_op jit(solution)/shard_map/ppermute | solution.py:214
  176.3 7.3 %collective-permute-done.11.a3_ref = bf16[512,256]{1,0:T(8,128)(2,1)S(1)} collective-permute-done((bf16[512,256]{1,0:T(8,128)(2,1)S(1)}, bf16[512,256]{1,0:T(8,128)(2,1)S(1)}, u32[]{:S(2)}, u32[]{:S(2)}) %collective-permute-start.11) | collective-permute-done | bytes 262176 | tf_op jit(solution)/shard_map/ppermute | solution.py:214
  183.6 8.3 %collective-permute-done.9.a1_ref = bf16[512,256]{1,0:T(8,128)(2,1)S(1)} collective-permute-done((bf16[512,256]{1,0:T(8,128)(2,1)S(1)}, bf16[512,256]{1,0:T(8,128)(2,1)S(1)}, u32[]{:S(2)}, u32[]{:S(2)}) %collective-permute-start.9) | collective-permute-done | bytes 262176 | tf_op jit(solution)/shard_map/ppermute | solution.py:214
  191.9 2.0 copy-done.17
  193.9 4.0 %merged.3 = bf16[512,1792]{1,0:T(8,128)(2,1)S(1)} custom-call(s32[2]{0:T(128)S(1)} %pad_add_fusion.side_ref, bf16[512,256]{1,0:T(8,128)(2,1)S(1)} %copy-done.9, bf16[512,256]{1,0:T(8,128)(2,1)S(1)} %collective-permute-done.9.a1_ref, bf16[512,256]{1,0:T(8,128)(2,1)S(1)} %collective-permute-done.10.a2_ref, ...), custom_call_target="tpu_custom_call" | custom-call | flops 1879048192 | bytes 6553600 | tf_op jit(solution)/shard_map/merged/pallas_call | solution.py:154
  198.0 1.2 copy-done.1
  199.2 11.7 %all-to-all-done.1 = bf16[32,16,1792]{2,1,0:T(8,128)(2,1)} async-done(((bf16[32,16,1792]{2,1,0:T(8,128)(2,1)}), bf16[32,16,1792]{2,1,0:T(8,128)(2,1)}, u32[]{:S(2)}, u32[]{:S(2)}) %all-to-all-start.1) | async-done | bytes 1835040 | tf_op jit(solution)/shard_map/all_to_all | solution.py:222
  210.9 6.0 %all-to-all-start.3 = ((bf16[32,16,1792]{2,1,0:T(8,128)(2,1)}), bf16[32,16,1792]{2,1,0:T(8,128)(2,1)}, u32[]{:S(2)}, u32[]{:S(2)}) async-start(bf16[32,16,1792]{2,1,0:T(8,128)(2,1)} %bitcast.26), calls=%async_computation.3 | async-start | bytes 3670016 | tf_op jit(solution)/shard_map/all_to_all | solution.py:222
  216.9 0.9 copy-done.19
  217.8 0.9 copy-done.21
  218.8 4.7 %weight_parts.1 = (bf16[512,1792]{1,0:T(8,128)(2,1)S(1)}, bf16[512,1792]{1,0:T(8,128)(2,1)S(1)}) custom-call(s32[2]{0:T(128)S(1)} %pad_add_fusion.side_ref, bf16[512,256]{1,0:T(8,128)(2,1)S(1)} %copy-done.8, bf16[512,256]{1,0:T(8,128)(2,1)S(1)} %collective-permute-done.3.a1_ref, bf16[512,256]{1,0:T(8,128)(2,1)S(1)} %copy-done.19, ...), custom_call_target="tpu_custom_call" | custom-call | flops 1879048192 | bytes 6553600 | tf_op jit(solution)/shard_map/weight_parts/pallas_call | solution.py:191
  223.5 4.5 %collective-permute-start.12 = (bf16[512,1792]{1,0:T(8,128)(2,1)S(1)}, bf16[512,1792]{1,0:T(8,128)(2,1)S(1)}, u32[]{:S(2)}, u32[]{:S(2)}) collective-permute-start(bf16[512,1792]{1,0:T(8,128)(2,1)S(1)} %get-tuple-element.28), channel_id=1, source_target_pairs={{0,224},{32,192},{64,160},{96,128},{128,96},{160,64},{192,32},{224... | collective-permute-start | bytes 5505032 | tf_op jit(solution)/shard_map/ppermute | solution.py:252
  228.0 55.5 %collective-permute-done.12 = bf16[512,1792]{1,0:T(8,128)(2,1)S(1)} collective-permute-done((bf16[512,1792]{1,0:T(8,128)(2,1)S(1)}, bf16[512,1792]{1,0:T(8,128)(2,1)S(1)}, u32[]{:S(2)}, u32[]{:S(2)}) %collective-permute-start.12) | collective-permute-done | bytes 1835040 | tf_op jit(solution)/shard_map/ppermute | solution.py:252
  283.5 1.7 fusion
  285.2 3.1 %convolution_convert_fusion.2 = bf16[256,1792]{1,0:T(8,128)(2,1)} fusion(bf16[512,256]{1,0:T(8,128)(2,1)S(1)} %get-tuple-element.16, bf16[512,1792]{1,0:T(8,128)(2,1)} %bitcast.11), kind=kOutput, calls=%fused_computation.3 | convolution fusion | flops 470220800 | bytes 3014656 | tf_op jit(solution)/shard_map/dot_general | solution.py:24
  288.3 0.0 all-to-all-done.3
  288.3 3.1 %convolution_convert_fusion.1 = bf16[256,1792]{1,0:T(8,128)(2,1)} fusion(bf16[512,256]{1,0:T(8,128)(2,1)S(1)} %copy-done.6, bf16[512,1792]{1,0:T(8,128)(2,1)} %bitcast.15), kind=kOutput, calls=%fused_computation.2 | convolution fusion | flops 470220800 | bytes 3014656 | tf_op jit(solution)/shard_map/dot_general | solution.py:24
  (25 shorter events, 0.0 us)
Async XLA Ops:
  0.6 8.2 %copy-start = (bf16[256,1792]{1,0:T(8,128)(2,1)S(1)}, bf16[256,1792]{1,0:T(8,128)(2,1)}, u32[]{:S(2)}) copy-start(bf16[256,1792]{1,0:T(8,128)(2,1)} %param.9) | copy-start | bytes 2752516
  0.7 1.2 copy-start.4
  2.0 0.7 copy-start.10
  2.7 0.7 copy-start.11
  3.4 0.7 copy-start.12
  4.1 0.7 copy-start.13
  7.6 1.2 copy-start.3
  8.9 55.2 %copy-start.5 = (bf16[512,256]{1,0:T(8,128)(2,1)}, bf16[512,256]{1,0:T(8,128)(2,1)S(1)}, u32[]{:S(2)}) copy-start(bf16[512,256]{1,0:T(8,128)(2,1)S(1)} %get-tuple-element.22) | copy-start | bytes 786436
  64.0 50.7 %all-to-all-start = ((bf16[32,16,1792]{2,1,0:T(8,128)(2,1)}), bf16[32,16,1792]{2,1,0:T(8,128)(2,1)}, u32[]{:S(2)}, u32[]{:S(2)}) async-start(bf16[32,16,1792]{2,1,0:T(8,128)(2,1)} %bitcast.28), calls=%async_computation | async-start | bytes 3670016 | tf_op jit(solution)/shard_map/all_to_all | solution.py:222
  70.8 2.0 copy-start.14
  77.1 49.1 %collective-permute-start.6 = (bf16[512,256]{1,0:T(8,128)(2,1)}, bf16[512,256]{1,0:T(8,128)(2,1)}, u32[]{:S(2)}, u32[]{:S(2)}) collective-permute-start(bf16[512,256]{1,0:T(8,128)(2,1)} %get-tuple-element.24), channel_id=1, source_target_pairs={{0,32},{32,0},{64,96},{96,64},{128,160},{160,128},{192,224},{224,1... | collective-permute-start | bytes 786440 | tf_op jit(solution)/shard_map/ppermute | solution.py:214
  79.6 47.0 %collective-permute-start.7 = (bf16[512,256]{1,0:T(8,128)(2,1)}, bf16[512,256]{1,0:T(8,128)(2,1)}, u32[]{:S(2)}, u32[]{:S(2)}) collective-permute-start(bf16[512,256]{1,0:T(8,128)(2,1)} %get-tuple-element.25), channel_id=1, source_target_pairs={{0,64},{32,96},{64,0},{96,32},{128,192},{160,224},{192,128},{224,1... | collective-permute-start | bytes 786440 | tf_op jit(solution)/shard_map/ppermute | solution.py:214
  80.9 45.7 %collective-permute-start.8 = (bf16[512,256]{1,0:T(8,128)(2,1)}, bf16[512,256]{1,0:T(8,128)(2,1)}, u32[]{:S(2)}, u32[]{:S(2)}) collective-permute-start(bf16[512,256]{1,0:T(8,128)(2,1)} %get-tuple-element.26), channel_id=1, source_target_pairs={{0,96},{32,64},{64,32},{96,0},{128,224},{160,192},{192,160},{224,1... | collective-permute-start | bytes 786440 | tf_op jit(solution)/shard_map/ppermute | solution.py:214
  114.7 2.0 copy-start.16
  116.7 35.4 %copy-start.15 = (bf16[1,1024,1792]{2,1,0:T(8,128)(2,1)S(1)}, bf16[1,1024,1792]{2,1,0:T(8,128)(2,1)}, u32[]{:S(2)}) copy-start(bf16[1,1024,1792]{2,1,0:T(8,128)(2,1)} %param.15) | copy-start | bytes 11010052
  122.3 8.1 %collective-permute-start = (bf16[512,256]{1,0:T(8,128)(2,1)S(1)}, bf16[512,256]{1,0:T(8,128)(2,1)S(1)}, u32[]{:S(2)}, u32[]{:S(2)}) collective-permute-start(bf16[512,256]{1,0:T(8,128)(2,1)S(1)} %get-tuple-element.19), channel_id=1, source_target_pairs={{0,32},{32,0},{64,96},{96,64},{128,160},{160,128},{192,224},{224,1... | collective-permute-start | bytes 786440 | tf_op jit(solution)/shard_map/ppermute | solution.py:214
  124.9 6.2 %collective-permute-start.1 = (bf16[512,256]{1,0:T(8,128)(2,1)S(1)}, bf16[512,256]{1,0:T(8,128)(2,1)S(1)}, u32[]{:S(2)}, u32[]{:S(2)}) collective-permute-start(bf16[512,256]{1,0:T(8,128)(2,1)S(1)} %get-tuple-element.20), channel_id=1, source_target_pairs={{0,64},{32,96},{64,0},{96,32},{128,192},{160,224},{192,128},{224,1... | collective-permute-start | bytes 786440 | tf_op jit(solution)/shard_map/ppermute | solution.py:214
  126.2 10.8 %collective-permute-start.2 = (bf16[512,256]{1,0:T(8,128)(2,1)S(1)}, bf16[512,256]{1,0:T(8,128)(2,1)S(1)}, u32[]{:S(2)}, u32[]{:S(2)}) collective-permute-start(bf16[512,256]{1,0:T(8,128)(2,1)S(1)} %get-tuple-element.21), channel_id=1, source_target_pairs={{0,96},{32,64},{64,32},{96,0},{128,224},{160,192},{192,160},{224,1... | collective-permute-start | bytes 786440 | tf_op jit(solution)/shard_map/ppermute | solution.py:214
  139.2 16.9 %copy-start.7 = (bf16[512,256]{1,0:T(8,128)(2,1)}, bf16[512,256]{1,0:T(8,128)(2,1)S(1)}, u32[]{:S(2)}) copy-start(bf16[512,256]{1,0:T(8,128)(2,1)S(1)} %get-tuple-element.30.a0_ref) | copy-start | bytes 786436
  139.2 7.0 %collective-permute-start.3 = (bf16[512,256]{1,0:T(8,128)(2,1)S(1)}, bf16[512,256]{1,0:T(8,128)(2,1)S(1)}, u32[]{:S(2)}, u32[]{:S(2)}) collective-permute-start(bf16[512,256]{1,0:T(8,128)(2,1)S(1)} %get-tuple-element.30.a0_ref), channel_id=1, source_target_pairs={{0,32},{32,0},{64,96},{96,64},{128,160},{160,128},{192,224},{224,1... | collective-permute-start | bytes 786440 | tf_op jit(solution)/shard_map/ppermute | solution.py:214
  141.7 6.0 %collective-permute-start.4 = (bf16[512,256]{1,0:T(8,128)(2,1)S(1)}, bf16[512,256]{1,0:T(8,128)(2,1)S(1)}, u32[]{:S(2)}, u32[]{:S(2)}) collective-permute-start(bf16[512,256]{1,0:T(8,128)(2,1)S(1)} %get-tuple-element.30.a0_ref), channel_id=1, source_target_pairs={{0,64},{32,96},{64,0},{96,32},{128,192},{160,224},{192,128},{224,1... | collective-permute-start | bytes 786440 | tf_op jit(solution)/shard_map/ppermute | solution.py:214
  141.9 10.3 %collective-permute-start.5 = (bf16[512,256]{1,0:T(8,128)(2,1)S(1)}, bf16[512,256]{1,0:T(8,128)(2,1)S(1)}, u32[]{:S(2)}, u32[]{:S(2)}) collective-permute-start(bf16[512,256]{1,0:T(8,128)(2,1)S(1)} %get-tuple-element.30.a0_ref), channel_id=1, source_target_pairs={{0,96},{32,64},{64,32},{96,0},{128,224},{160,192},{192,160},{224,1... | collective-permute-start | bytes 786440 | tf_op jit(solution)/shard_map/ppermute | solution.py:214
  147.7 8.5 %copy-start.18 = (bf16[512,256]{1,0:T(8,128)(2,1)}, bf16[512,256]{1,0:T(8,128)(2,1)S(1)}, u32[]{:S(2)}) copy-start(bf16[512,256]{1,0:T(8,128)(2,1)S(1)} %collective-permute-done.4.a2_ref) | copy-start | bytes 786436
  152.2 4.1 %copy-start.20 = (bf16[512,256]{1,0:T(8,128)(2,1)}, bf16[512,256]{1,0:T(8,128)(2,1)S(1)}, u32[]{:S(2)}) copy-start(bf16[512,256]{1,0:T(8,128)(2,1)S(1)} %collective-permute-done.5.a3_ref) | copy-start | bytes 786436
  156.2 1.2 copy-start.2
  157.4 9.6 %copy-start.9 = (bf16[512,256]{1,0:T(8,128)(2,1)S(1)}, bf16[512,256]{1,0:T(8,128)(2,1)}, u32[]{:S(2)}) copy-start(bf16[512,256]{1,0:T(8,128)(2,1)} %get-tuple-element.29.a0_ref) | copy-start | bytes 786436
  157.4 53.4 %all-to-all-start.1 = ((bf16[32,16,1792]{2,1,0:T(8,128)(2,1)}), bf16[32,16,1792]{2,1,0:T(8,128)(2,1)}, u32[]{:S(2)}, u32[]{:S(2)}) async-start(bf16[32,16,1792]{2,1,0:T(8,128)(2,1)} %bitcast.27), calls=%async_computation.1 | async-start | bytes 3670016 | tf_op jit(solution)/shard_map/all_to_all | solution.py:222
  167.0 9.2 %collective-permute-start.10 = (bf16[512,256]{1,0:T(8,128)(2,1)S(1)}, bf16[512,256]{1,0:T(8,128)(2,1)S(1)}, u32[]{:S(2)}, u32[]{:S(2)}) collective-permute-start(bf16[512,256]{1,0:T(8,128)(2,1)S(1)} %copy-done.9), channel_id=1, source_target_pairs={{0,64},{32,96},{64,0},{96,32},{128,192},{160,224},{192,128},{224,1... | collective-permute-start | bytes 786440 | tf_op jit(solution)/shard_map/ppermute | solution.py:214
  168.0 15.7 %collective-permute-start.11 = (bf16[512,256]{1,0:T(8,128)(2,1)S(1)}, bf16[512,256]{1,0:T(8,128)(2,1)S(1)}, u32[]{:S(2)}, u32[]{:S(2)}) collective-permute-start(bf16[512,256]{1,0:T(8,128)(2,1)S(1)} %copy-done.9), channel_id=1, source_target_pairs={{0,96},{32,64},{64,32},{96,0},{128,224},{160,192},{192,160},{224,1... | collective-permute-start | bytes 786440 | tf_op jit(solution)/shard_map/ppermute | solution.py:214
  170.3 21.6 %collective-permute-start.9 = (bf16[512,256]{1,0:T(8,128)(2,1)S(1)}, bf16[512,256]{1,0:T(8,128)(2,1)S(1)}, u32[]{:S(2)}, u32[]{:S(2)}) collective-permute-start(bf16[512,256]{1,0:T(8,128)(2,1)S(1)} %copy-done.9), channel_id=1, source_target_pairs={{0,32},{32,0},{64,96},{96,64},{128,160},{160,128},{192,224},{224,1... | collective-permute-start | bytes 786440 | tf_op jit(solution)/shard_map/ppermute | solution.py:214
  191.9 2.0 copy-start.17
  198.0 1.3 copy-start.1
  210.9 6.0 %copy-start.8 = (bf16[512,256]{1,0:T(8,128)(2,1)S(1)}, bf16[512,256]{1,0:T(8,128)(2,1)}, u32[]{:S(2)}) copy-start(bf16[512,256]{1,0:T(8,128)(2,1)} %copy-done.7) | copy-start | bytes 786436
  210.9 77.5 %all-to-all-start.3 = ((bf16[32,16,1792]{2,1,0:T(8,128)(2,1)}), bf16[32,16,1792]{2,1,0:T(8,128)(2,1)}, u32[]{:S(2)}, u32[]{:S(2)}) async-start(bf16[32,16,1792]{2,1,0:T(8,128)(2,1)} %bitcast.26), calls=%async_computation.3 | async-start | bytes 3670016 | tf_op jit(solution)/shard_map/all_to_all | solution.py:222
  216.9 1.0 copy-start.19
  217.8 0.9 copy-start.21
  223.5 60.0 %collective-permute-start.12 = (bf16[512,1792]{1,0:T(8,128)(2,1)S(1)}, bf16[512,1792]{1,0:T(8,128)(2,1)S(1)}, u32[]{:S(2)}, u32[]{:S(2)}) collective-permute-start(bf16[512,1792]{1,0:T(8,128)(2,1)S(1)} %get-tuple-element.28), channel_id=1, source_target_pairs={{0,224},{32,192},{64,160},{96,128},{128,96},{160,64},{192,32},{224... | collective-permute-start | bytes 5505032 | tf_op jit(solution)/shard_map/ppermute | solution.py:252
  285.2 3.1 %copy-start.6 = (bf16[512,256]{1,0:T(8,128)(2,1)S(1)}, bf16[512,256]{1,0:T(8,128)(2,1)}, u32[]{:S(2)}) copy-start(bf16[512,256]{1,0:T(8,128)(2,1)} %copy-done.5) | copy-start | bytes 786436

commit v2 on v0

v2 whole, which is shorter than its diff:
```python
import functools

import jax
import jax.numpy as jnp
from jax import lax
from jax.experimental import pallas as pl
from jax.experimental.pallas import tpu as pltpu
from jax.sharding import PartitionSpec as P

CAP = 16
BF = jnp.bfloat16
F32 = jnp.float32
RESIDENT = pl.BlockSpec(memory_space=pltpu.VMEM)
SCALARS = pl.BlockSpec(memory_space=pltpu.SMEM)
FAR = pl.BlockSpec(memory_space=pltpu.HBM)


def params():
    return pltpu.CompilerParams(vmem_limit_bytes=20 * 1024 * 1024)


def cost(flops, bytes_accessed):
    return pl.CostEstimate(flops=flops, bytes_accessed=bytes_accessed, transcendentals=0)


def near(array):
    return pltpu.with_memory_space_constraint(array, pltpu.VMEM)


def far(array):
    return pltpu.with_memory_space_constraint(array, pltpu.HBM)


def dot(a, b, ca, cb):
    return lax.dot_general(a, b, (((ca,), (cb,)), ((), ())), preferred_element_type=F32)


def column_block(width):
    for size in (256, 128):
        if width % size == 0:
            return size
    return width


def table_of(side_ref, ra_ref, rb_ref, ga_ref, gb_ref, expert_of, slots):
    upper = side_ref[1] == 1
    route = jnp.where(upper, rb_ref[...], ra_ref[...])
    gates = jnp.where(upper, gb_ref[...].astype(F32), ga_ref[...].astype(F32))
    top, tokens = route.shape
    experts = slots // CAP
    expert = lax.broadcasted_iota(jnp.int32, (experts, tokens), 0)
    member = jnp.zeros((experts, tokens), F32)
    gate = jnp.zeros((experts, tokens), F32)
    for k in range(top):
        named = route[k : k + 1, :] == expert
        member = member + jnp.where(named, 1.0, 0.0)
        gate = gate + jnp.where(named, gates[k : k + 1, :], 0.0)
    before = lax.broadcasted_iota(jnp.int32, (tokens, tokens), 0) < lax.broadcasted_iota(
        jnp.int32, (tokens, tokens), 1
    )
    earlier = dot(member.astype(BF), jnp.where(before, 1.0, 0.0).astype(BF), 1, 0)
    place = jnp.where(member > 0.5, earlier, 128.0).astype(BF)
    row = lax.broadcasted_iota(jnp.int32, (slots, experts), 0)
    column = lax.broadcasted_iota(jnp.int32, (slots, experts), 1)
    spread = jnp.where(expert_of(row // CAP) == column, 1.0, 0.0).astype(BF)
    place_rows = dot(spread, place, 1, 0)
    gate_rows = dot(spread, gate.astype(BF), 1, 0)
    slot = lax.broadcasted_iota(jnp.int32, (slots, tokens), 0) % CAP
    hit = place_rows == slot.astype(F32)
    return jnp.where(hit, 1.0, 0.0).astype(BF), jnp.where(hit, gate_rows, 0.0).astype(BF)


def fetch(source, target, sems, axis, parts):
    size = source.shape[axis] // parts
    copies = []
    for i in range(parts):
        span = tuple(pl.ds(i * size, size) if d == axis else slice(None) for d in range(2))
        copies.append(pltpu.make_async_copy(source.at[span], target.at[span], sems.at[i]))
    return copies


def streamed(source, target, sems, cols):
    step = pl.program_id(0)

    @pl.when(step == 0)
    def _():
        for copy in fetch(source, target, sems, 1, source.shape[1] // cols):
            copy.start()

    span = (slice(None), pl.ds(pl.multiple_of(step * cols, cols), cols))
    pltpu.make_async_copy(source.at[span], target.at[span], sems.at[step]).wait()
    return target[span]


def dispatch_kernel(side_ref, ra_ref, rb_ref, ga_ref, gb_ref, x_ref, *refs, depth, count):
    outs, flipped, (table_ref, x_all, out_all, sem, sems) = refs[:count], refs[count:-5], refs[-5:]
    routing = (side_ref, ra_ref, rb_ref, ga_ref, gb_ref)
    copy = pltpu.make_async_copy(x_ref, x_all, sem)

    def by_depth(block):
        return block // 2 % 2 * (2 * depth) + block // 4 * 2 + block % 2

    def by_plane(block):
        flip_x, flip_core = block // (2 * depth), block // depth % 2
        return (side_ref[2] ^ flip_x) * (2 * depth) + block % depth * 2 + (side_ref[3] ^ flip_core)

    copy.start()
    slots = table_ref.shape[0]
    if count == 1:
        table_ref[...] = table_of(*routing, by_depth, slots)[0]
    else:
        table_ref[...] = table_of(*routing, by_plane, slots)[1]
        for ref, table in zip(flipped, table_of(*routing, by_depth, slots)):
            ref[...] = table.T
    copy.wait()
    height, width = outs[0].shape
    cols = column_block(width)
    copies = []
    for k in range(width // cols):
        span = slice(k * cols, (k + 1) * cols)
        out_all[:, span] = dot(table_ref[...], x_all[:, span], 1, 0).astype(BF)
        for i, out_ref in enumerate(outs):
            source = out_all.at[i * height : (i + 1) * height, span]
            copies.append(pltpu.make_async_copy(source, out_ref.at[:, span], sems.at[len(copies)]))
            copies[-1].start()
    for copy in copies:
        copy.wait()


def dispatch(side, routing, x, slots, depth, count):
    tokens, width = x.shape
    tables = 0 if count == 1 else 2
    return pl.pallas_call(
        functools.partial(dispatch_kernel, depth=depth, count=count),
        in_specs=[SCALARS] + [RESIDENT] * 4 + [FAR],
        out_specs=[FAR] * count + [RESIDENT] * tables,
        out_shape=[pltpu.HBM((slots // count, width), BF)] * count
        + [jax.ShapeDtypeStruct((tokens, slots), BF)] * tables,
        scratch_shapes=[
            pltpu.VMEM((slots, tokens), BF),
            pltpu.VMEM((tokens, width), BF),
            pltpu.VMEM((slots, width), BF),
            pltpu.SemaphoreType.DMA,
            pltpu.SemaphoreType.DMA((count * (width // column_block(width)),)),
        ],
        compiler_params=params(),
        cost_estimate=cost(2 * slots * tokens * width, 2 * (slots + tokens) * width),
        name="dispatch",
    )(side, *[far(array) for array in routing], far(x))


def regroup_kernel(side_ref, *refs, members):
    pieces, (out_ref, held, sems) = refs[: len(members)], refs[-3:]
    arriving = [pltpu.make_async_copy(ref, held.at[i], sems.at[i]) for i, ref in enumerate(pieces)]
    leaving = []
    for copy in arriving:
        copy.start()
    for i, (j, copy) in enumerate(zip(members, arriving)):
        place = (side_ref[2] ^ (j // 2)) * 2 + (side_ref[3] ^ (j % 2))
        copy.wait()
        leaving.append(pltpu.make_async_copy(held.at[i], out_ref.at[:, place], sems.at[len(members) + i]))
        leaving[-1].start()
    for copy in leaving:
        copy.wait()


def regroup(side, pieces, depth, members, base=None):
    width = pieces[0].shape[1]
    pieces = [far(piece.reshape(depth, CAP, width)) for piece in pieces]
    more = [] if base is None else [far(base)]
    return pl.pallas_call(
        functools.partial(regroup_kernel, members=members),
        in_specs=[SCALARS] + [FAR] * (len(pieces) + len(more)),
        out_specs=FAR,
        out_shape=pltpu.HBM((depth, 4, CAP, width), BF),
        scratch_shapes=[
            pltpu.VMEM((len(members), depth, CAP, width), BF),
            pltpu.SemaphoreType.DMA((2 * len(members),)),
        ],
        input_output_aliases={1 + len(pieces): 0} if more else {},
        compiler_params=params(),
        cost_estimate=cost(0, 4 * CAP * depth * width * len(members)),
        name="regroup",
    )(side, *pieces, *more)


def hold_kernel(source, target, sems):
    copies = fetch(source, target, sems, 0, 4)
    for copy in copies:
        copy.start()
    for copy in copies:
        copy.wait()


def hold(weight):
    return pl.pallas_call(
        hold_kernel,
        in_specs=[FAR],
        out_specs=RESIDENT,
        out_shape=pltpu.VMEM(weight.shape, BF),
        scratch_shapes=[pltpu.SemaphoreType.DMA((4,))],
        compiler_params=params(),
        cost_estimate=cost(0, 4 * weight.size),
        name="hold",
    )(far(weight))


def partial_kernel(side_ref, x_ref, w_ref, own_ref, s1_ref, s2_ref, s3_ref, *refs, transposed):
    *kept, own_all, sent_all, sems = refs
    hid = own_ref.shape[1]
    copies = [pltpu.make_async_copy(x_ref, ref, sems.at[4]) for ref in kept]
    for copy in copies:
        copy.start()
    for j, ref in ((3, s3_ref), (1, s1_ref), (2, s2_ref), (0, own_ref)):
        block = pl.ds(pl.multiple_of((side_ref[0] ^ j) * hid, hid), hid)
        weight = w_ref[block, :] if transposed else w_ref[:, block]
        part = dot(x_ref[...], weight, 1, 1 if transposed else 0)
        held = sent_all.at[j - 1] if ref.dtype == BF else own_all.at[j]
        held[...] = part.astype(ref.dtype)
        copies.append(pltpu.make_async_copy(held, ref, sems.at[j]))
        copies[-1].start()
    for copy in copies:
        copy.wait()


def partials(side, x, w, transposed):
    rows, depth = x.shape
    hid = (w.shape[0] if transposed else w.shape[1]) // 4
    shapes = [pltpu.HBM((rows, hid), F32)] + [pltpu.HBM((rows, hid), BF)] * 3
    if transposed:
        shapes[1] = shapes[0]
        shapes.append(pltpu.HBM(x.shape, BF))
    return pl.pallas_call(
        functools.partial(partial_kernel, transposed=transposed),
        in_specs=[SCALARS, RESIDENT, RESIDENT],
        out_specs=[FAR] * len(shapes),
        out_shape=shapes,
        scratch_shapes=[
            pltpu.VMEM((2, rows, hid), F32),
            pltpu.VMEM((3, rows, hid), BF),
            pltpu.SemaphoreType.DMA((5,)),
        ],
        compiler_params=params(),
        cost_estimate=cost(8 * rows * depth * hid, 2 * (rows * depth + 4 * depth * hid) + 10 * rows * hid),
        name="partials",
    )(side, near(x), near(w))


def merge_kernel(side_ref, a0_ref, a1_ref, a2_ref, a3_ref, w_ref, out_ref, *refs, transposed):
    *flipped_ref, out_all, flipped, sems = refs
    pieces = (a0_ref, a1_ref, a2_ref, a3_ref)
    rows, hid = a0_ref.shape
    width = out_all.shape[1]
    cols = column_block(width)
    blocks = [pl.ds(pl.multiple_of((side_ref[0] ^ j) * hid, hid), hid) for j in range(4)]
    copies = []
    for i in range(width // cols):
        span = slice(i * cols, (i + 1) * cols)
        total = None
        for ref, block in zip(pieces, blocks):
            if transposed:
                part = dot(ref[...], w_ref[span, block], 1, 1)
            else:
                part = dot(ref[...], w_ref[block, span], 1, 0)
            total = part if total is None else total + part
        out_all[:, span] = total.astype(BF)
        copies.append(pltpu.make_async_copy(out_all.at[:, span], out_ref.at[:, span], sems.at[i]))
        copies[-1].start()
    if flipped_ref:
        for ref, block in zip(pieces, blocks):
            flipped[block, :] = ref[...].T
        copies.append(pltpu.make_async_copy(flipped, flipped_ref[0], sems.at[width // cols]))
        copies[-1].start()
    for copy in copies:
        copy.wait()


def merged(side, pieces, w, transposed):
    rows, hid = pieces[0].shape
    width = w.shape[0] if transposed else w.shape[1]
    shapes = [pltpu.HBM((rows, width), BF)]
    if not transposed:
        shapes.append(pltpu.HBM((4 * hid, rows), BF))
    return pl.pallas_call(
        functools.partial(merge_kernel, transposed=transposed),
        in_specs=[SCALARS] + [RESIDENT] * 5,
        out_specs=[FAR] * len(shapes),
        out_shape=shapes,
        scratch_shapes=[
            pltpu.VMEM((rows, width), BF),
            pltpu.VMEM((4 * hid, rows), BF),
            pltpu.SemaphoreType.DMA((width // column_block(width) + 1,)),
        ],
        compiler_params=params(),
        cost_estimate=cost(8 * rows * width * hid, 2 * (rows * width + 4 * width * hid + 4 * rows * hid)),
        name="merged",
    )(side, *pieces, near(w))


def weight_kernel(side_ref, act_ref, d_ref, first_ref, rest_ref, own_ref, d_all, sems):
    rows, cols = own_ref.shape
    early = first_ref.shape[0]
    d_out = streamed(d_ref, d_all, sems, cols)
    own = act_ref[pl.ds(pl.multiple_of(side_ref[1] * rows, rows), rows), :]
    other = act_ref[pl.ds(pl.multiple_of((1 - side_ref[1]) * rows, rows), rows), :]
    sent = dot(other, d_out, 1, 0).astype(BF)
    first_ref[...] = sent[:early]
    rest_ref[...] = sent[early:]
    own_ref[...] = dot(own, d_out, 1, 0).astype(BF)


def weight_parts(side, acts, d_out, early):
    hid, rows = acts.shape
    width = d_out.shape[1]
    cols = column_block(width)
    heights = (early, hid // 2 - early, hid // 2)
    return pl.pallas_call(
        weight_kernel,
        grid=(width // cols,),
        in_specs=[SCALARS, pl.BlockSpec((hid, rows), lambda i: (0, 0)), FAR],
        out_specs=[pl.BlockSpec((height, cols), lambda i: (0, i)) for height in heights],
        out_shape=[pltpu.HBM((height, width), BF) for height in heights],
        scratch_shapes=[pltpu.VMEM((rows, width), BF), pltpu.SemaphoreType.DMA((width // cols,))],
        compiler_params=params(),
        cost_estimate=cost(2 * rows * width * hid, 2 * (rows * width + width * hid + rows * hid)),
        name="weight_parts",
    )(side, far(acts), far(d_out))


def combine_kernel(table_ref, x_ref, *refs, kept):
    if kept:
        next_ref, out_ref, next_out, out_all, sems = refs
    else:
        out_ref, out_all, sems = refs
    copies = []
    tokens, width = out_all.shape
    cols = column_block(width)
    for i in range(width // cols):
        span = (slice(None), slice(i * cols, (i + 1) * cols))
        out_all[span] = dot(table_ref[...], x_ref[span], 1, 0).astype(BF)
        copies.append(pltpu.make_async_copy(out_all.at[span], out_ref.at[span], sems.at[i]))
        copies[-1].start()
    if kept:
        next_out[...] = next_ref[...]
    for copy in copies:
        copy.wait()


def combine(table, rows, following=None):
    tokens, slots = table.shape
    width = rows.shape[1]
    kept = following is not None
    return pl.pallas_call(
        functools.partial(combine_kernel, kept=kept),
        in_specs=[RESIDENT] * (3 if kept else 2),
        out_specs=[FAR] + [RESIDENT] * kept,
        out_shape=[pltpu.HBM((tokens, width), BF)] + [pltpu.VMEM(table.shape, BF)] * kept,
        scratch_shapes=[pltpu.VMEM((tokens, width), BF), pltpu.SemaphoreType.DMA((width // column_block(width),))],
        compiler_params=params(),
        cost_estimate=cost(2 * slots * tokens * width, 2 * (slots + tokens) * width),
        name="combine",
    )(*((table, rows, following) if kept else (near(table), near(rows))))


def to_member(block, flip):
    count = lax.axis_size("pipe")
    return lax.ppermute(block, "pipe", [(p, p ^ flip) for p in range(count)])


def to_members(blocks):
    return [to_member(block, j + 1) for j, block in enumerate(blocks)]


def to_mirror(block):
    count = lax.axis_size("pipe")
    return lax.ppermute(block, "pipe", [(p, count - 1 - p) for p in range(count)])


def exchange(rows, groups):
    ranks = len(groups[0])
    blocks = rows.reshape(ranks, rows.shape[0] // ranks, -1)
    blocks = lax.all_to_all(
        blocks, "expert", split_axis=0, concat_axis=0, tiled=True, axis_index_groups=groups
    )
    return blocks.reshape(rows.shape)


def shards(tokens, cotangent, route_a, route_b, gates_a, gates_b, w_up, w_down):
    half_size = lax.axis_size("pipe") // 2
    experts = lax.axis_size("expert")
    slots, depth = experts * CAP, experts // 4
    up, down = w_up[0], w_down[0]
    pipe, expert = lax.axis_index("pipe"), lax.axis_index("expert")
    side = [pipe % half_size, pipe // half_size, expert // (2 * depth), expert % 2]
    side = jnp.stack(side).astype(jnp.int32)
    columns = [[(x * depth + z) * 2 + core for z in range(depth)] for x in range(2) for core in range(2)]
    everyone = [[column[z] for z in range(depth) for column in columns]]

    routing = [route_a.T, route_b.T, gates_a.T, gates_b.T]
    (sent_x,) = dispatch(side, routing, tokens, slots, depth, 1)
    rows_x = exchange(sent_x, everyone)
    *pieces, plain_flipped, gated_flipped = dispatch(side, routing, cotangent, slots, depth, 4)
    for j in range(1, 4):
        flip = j // 2 * (2 * depth) + j % 2
        pieces[j] = lax.ppermute(pieces[j], "expert", [(e, e ^ flip) for e in range(experts)])
    grouped = regroup(side, pieces[:3], depth, (0, 1, 2))
    grouped = regroup(side, pieces[3:], depth, (3,), grouped).reshape(slots, -1)

    grouped, rows_x = lax.optimization_barrier((grouped, rows_x))
    d_out = exchange(grouped, columns)
    own, *others = partials(side, rows_x, up, False)
    hidden = own + sum(block.astype(F32) for block in to_members(others))
    sigmoid = jax.nn.sigmoid(hidden)
    act = (hidden * sigmoid).astype(BF)
    act, down = lax.optimization_barrier((act, down))
    down_held = hold(down)
    acts = [act] + to_members([act] * 3)
    result, acts_flipped = merged(side, acts, down_held, False)
    result, d_out = lax.optimization_barrier((result, d_out))

    own, beside, far_off, diagonal, d_out = partials(side, d_out, down, True)
    result, own, beside, far_off, diagonal, d_out = lax.optimization_barrier(
        (result, own, beside, far_off, diagonal, d_out)
    )
    returned = exchange(result, everyone)
    diagonal = to_member(diagonal, 2)
    far_off = to_member(far_off, 2)
    beside = to_member((beside + diagonal.astype(F32)).astype(BF), 1)
    first, rest, own_weight = weight_parts(side, acts_flipped, d_out, slots // 8 * 3)
    d_act = own + far_off.astype(F32) + beside.astype(F32)
    d_hidden = (d_act * sigmoid * (1.0 + hidden * (1.0 - sigmoid))).astype(BF)
    d_hidden, first, rest, up = lax.optimization_barrier((d_hidden, first, rest, up))
    beside = to_member(d_hidden, 1)
    far_off = to_member(d_hidden, 2)
    up_held = hold(up)
    beside, far_off, first = lax.optimization_barrier((beside, far_off, first))
    d_hiddens = [d_hidden, beside, far_off, to_member(beside, 2)]
    first = to_mirror(first)
    (d_rows,) = merged(side, d_hiddens, up_held, True)
    d_rows, returned, first = lax.optimization_barrier((d_rows, returned, first))
    returned_dx = exchange(d_rows, everyone)
    rest = to_mirror(rest)

    layer_out, plain_held = combine(gated_flipped, returned, plain_flipped)
    layer_out, rest = lax.optimization_barrier((layer_out, rest))
    arrived = jnp.concatenate([first, rest])
    grad_weight = (own_weight.astype(F32) + arrived.astype(F32)).astype(BF)
    (grad_tokens,) = combine(plain_held, returned_dx)
    return (layer_out, grad_tokens, grad_weight[None])


def solution(mesh):
    in_specs = (
        P("expert", "pipe"),
        P("expert", "pipe"),
        P("expert", None),
        P("expert", None),
        P("expert", None),
        P("expert", None),
        P("expert", "pipe", None),
        P("expert", None, "pipe"),
    )
    out_specs = (P("expert", "pipe"), P("expert", "pipe"), P("expert", None, "pipe"))
    return jax.shard_map(shards, mesh=mesh, in_specs=in_specs, out_specs=out_specs, check_vma=False)
```

time: 377 us -> 247 us (0.66)
  waiting for transfers between devices: 259 us -> 136 us
  Pallas kernels: 0 us -> 42.7 us
  matrix products: 29.5 us -> 0 us
  other arithmetic: 26 us -> 4.47 us
    ppermute x7 -> x17, waiting for transfers between devices: 215 us -> 136 us  [the longest x12 51.8 us: to_member(): return lax.ppermute(block, 'pipe', [(p, p ^ flip) for p in range(count)])]
    all_to_all x5 -> x4, waiting for transfers between devices: 44.5 us -> 0.01 us  [exchange(): lax.all_to_all(blocks, 'expert', split_axis=0, concat_axis=0, tiled=True,...]
    pallas_call x0 -> x13, Pallas kernels: none -> 42.7 us  [the longest x2 7.51 us: merged(): pl.pallas_call(functools.partial(merge_kernel, transposed=transposed), in...]
    dot_general x9 -> x0, matrix products: 29.5 us -> none  [the longest x1 6.25 us: shards(): lax.dot_general(d_hidden, up_weight, (((1,), (1,)), ((), ())), preferred_...]
    ppermute x7 -> x17, starting transfers between devices: 13.2 us -> 23 us  [the longest x12 13.7 us: to_member(): return lax.ppermute(block, 'pipe', [(p, p ^ flip) for p in range(count)])]
    another operation x2 -> x1, other arithmetic: 9.27 us -> 0.08 us  [shards(): side = jnp.stack(side).astype(jnp.int32)]
    all_to_all x5 -> x4, starting transfers between devices: 38.1 us -> 30.9 us  [exchange(): lax.all_to_all(blocks, 'expert', split_axis=0, concat_axis=0, tiled=True,...]
    add x2 -> x0, other arithmetic: 4.41 us -> none  [group_total(): running = running + swapped(running, 'pipe', bit_pos)]
  transfers between devices with their start and end apart: 12 -> 21, of which waited for: 8 -> 14; matrix products, arithmetic and copies ran while one was open for 11% -> 2% of each run, Pallas kernels for 0% -> 13%
where the time goes in v2:
time: 247 us; the launch traced here: 246 us
  waiting for transfers between devices  136 us (55%)
  starting transfers between devices  54 us (22%)
  Pallas kernels  42.7 us (17%)
  local copies, waits for them, and re-layouts  8.36 us (3%)
  other arithmetic  4.47 us (2%)
    ppermute x12, waiting for transfers between devices, to_member(): return lax.ppermute(block, 'pipe', [(p, p ^ flip) for p in range(count)])  51.8 us
    ppermute x2, waiting for transfers between devices, to_mirror(): lax.ppermute(block, 'pipe', [(p, count - 1 - p) for p in range(count)])  49.9 us
    ppermute x3, waiting for transfers between devices, shards(): lax.ppermute(pieces[j], 'expert', [(e, e ^ flip) for e in range(experts)])  34.3 us
    all_to_all x4, starting transfers between devices, exchange(): lax.all_to_all(blocks, 'expert', split_axis=0, concat_axis=0, tiled=True,...  30.9 us
    ppermute x12, starting transfers between devices, to_member(): return lax.ppermute(block, 'pipe', [(p, p ^ flip) for p in range(count)])  13.7 us
    unnamed x24, local copies, waits for them, and re-layouts  8.36 us
    pallas_call x2, Pallas kernels, merged(): pl.pallas_call(functools.partial(merge_kernel, transposed=transposed), in...  7.51 us
    pallas_call x1, Pallas kernels, weight_parts(): pl.pallas_call(weight_kernel, grid=(width // cols,), in_specs=[SCALARS, p...  7.26 us
  transfers between devices with their start and end apart: 21, of which 14 were waited for; matrix products, arithmetic and copies ran while one was open for 2% of the time, Pallas kernels for 13%

profile of v2, /device:TPU:1, one launch (start us, length us, event | category | flops | bytes accessed | tf_op | source)
XLA Modules:
  0.0 246.5 jit_solution(12720994235762332669)
XLA Ops:
  0.7 0.1 pad_add_fusion.side_ref
  0.7 3.5 %dispatch.3 = bf16[512,1792]{1,0:T(8,128)(2,1)} custom-call(s32[4]{0:T(128)S(1)} %pad_add_fusion.side_ref, s32[8,256]{1,0:T(8,128)} %bitcast.40, s32[8,256]{1,0:T(8,128)} %bitcast.42, bf16[8,256]{1,0:T(8,128)(2,1)} %bitcast.44, bf16[8,256]{1,0:T(8,128)(2,1)} %bitcast.46, bf16[256,1792]{1,0:T(8,128)(2,1)} %x_ref.3), custom_call_target="tpu_custom_call" | custom-call | flops 469762048 | bytes 2752512 | tf_op jit(solution)/shard_map/dispatch/pallas_call | solution.py:133
  4.3 11.1 %all-to-all-start = ((bf16[32,16,1792]{2,1,0:T(8,128)(2,1)}), bf16[32,16,1792]{2,1,0:T(8,128)(2,1)S(1)}, u32[]{:S(2)}, u32[]{:S(2)}) async-start(bf16[32,16,1792]{2,1,0:T(8,128)(2,1)} %bitcast.33), calls=%async_computation | async-start | bytes 3670016 | tf_op jit(solution)/shard_map/all_to_all | solution.py:382
  15.3 3.7 %dispatch.2 = (bf16[128,1792]{1,0:T(8,128)(2,1)}, bf16[128,1792]{1,0:T(8,128)(2,1)}, bf16[128,1792]{1,0:T(8,128)(2,1)}, bf16[128,1792]{1,0:T(8,128)(2,1)}, bf16[...) custom-call(s32[4]{0:T(128)S(1)} %pad_add_fusion.side_ref, s32[8,256]{1,0:T(8,128)} %bitcast.41, s32[8,256]{1,0:T(8,128)} %bitcast.43, ...), custom_call_target="tpu_custom_call" | custom-call | flops 469762048 | bytes 2752512 | tf_op jit(solution)/shard_map/dispatch/pallas_call | solution.py:133
  19.0 0.3 collective-permute-start.1
  19.4 1.5 collective-permute-start.2
  20.9 0.4 collective-permute-start
  21.3 0.0 collective-permute-done.1
  21.3 18.4 %collective-permute-done.2 = bf16[128,1792]{1,0:T(8,128)(2,1)S(1)} collective-permute-done((bf16[128,1792]{1,0:T(8,128)(2,1)}, bf16[128,1792]{1,0:T(8,128)(2,1)S(1)}, u32[]{:S(2)}, u32[]{:S(2)}) %collective-permute-start.2) | collective-permute-done | bytes 458784 | tf_op jit(solution)/shard_map/ppermute | solution.py:405
  39.7 0.8 copy-done.9
  40.5 2.8 %regroup.2.refs_1_ = bf16[8,4,16,1792]{3,2,1,0:T(8,128)(2,1)} custom-call(s32[4]{0:T(128)S(1)} %pad_add_fusion.side_ref, bf16[8,16,1792]{2,1,0:T(8,128)(2,1)} %bitcast.37, bf16[8,16,1792]{2,1,0:T(8,128)(2,1)} %bitcast.38, bf16[8,16,1792]{2,1,0:T(8,128)(2,1)} %bitcast.39), custom_call_target="tpu_custom_call" | custom-call | bytes 2752512 | tf_op jit(solution)/shard_map/regroup/pallas_call | solution.py:171
  43.2 15.8 %collective-permute-done = bf16[128,1792]{1,0:T(8,128)(2,1)S(1)} collective-permute-done((bf16[128,1792]{1,0:T(8,128)(2,1)}, bf16[128,1792]{1,0:T(8,128)(2,1)S(1)}, u32[]{:S(2)}, u32[]{:S(2)}) %collective-permute-start) | collective-permute-done | bytes 458784 | tf_op jit(solution)/shard_map/ppermute | solution.py:405
  59.1 0.8 copy-done.7
  59.8 2.4 regroup.3
  62.2 0.0 copy-start.2
  62.2 1.2 copy-done.2
  63.5 5.1 %all-to-all-start.1 = ((bf16[8,64,1792]{2,1,0:T(8,128)(2,1)}), bf16[8,64,1792]{2,1,0:T(8,128)(2,1)S(1)}, u32[]{:S(2)}, u32[]{:S(2)}) async-start(bf16[8,64,1792]{2,1,0:T(8,128)(2,1)} %bitcast.32), calls=%async_computation.1 | async-start | bytes 3670016 | tf_op jit(solution)/shard_map/all_to_all | solution.py:382
  68.6 2.0 copy-done.1
  70.6 1.5 copy-done.3
  72.1 3.6 %partials.2 = (f32[512,256]{1,0:T(8,128)}, bf16[512,256]{1,0:T(8,128)(2,1)}, bf16[512,256]{1,0:T(8,128)(2,1)}, bf16[512,256]{1,0:T(8,128)(2,1)}) custom-call(s32[4]{0:T(128)S(1)} %pad_add_fusion.side_ref, bf16[512,1792]{1,0:T(8,128)(2,1)S(1)} %bitcast.31, bf16[1792,1024]{1,0:T(8,128)(2,1)S(1)} %bitcast.29), custom_call_target="tpu_custom_call" | custom-call | flops 1879048192 | bytes 6815744 | tf_op jit(solution)/shard_map/partials/pallas_call | solution.py:233
  75.7 2.5 %collective-permute-start.3 = (bf16[512,256]{1,0:T(8,128)(2,1)}, bf16[512,256]{1,0:T(8,128)(2,1)S(1)}, u32[]{:S(2)}, u32[]{:S(2)}) collective-permute-start(bf16[512,256]{1,0:T(8,128)(2,1)} %get-tuple-element.56), channel_id=1, source_target_pairs={{0,32},{32,0},{64,96},{96,64},{128,160},{160,128},{192,224},{224,1... | collective-permute-start | bytes 786440 | tf_op jit(solution)/shard_map/ppermute | solution.py:367
  78.3 1.3 collective-permute-start.4
  79.5 0.4 collective-permute-start.5
  79.9 4.7 %collective-permute-done.3 = bf16[512,256]{1,0:T(8,128)(2,1)S(1)} collective-permute-done((bf16[512,256]{1,0:T(8,128)(2,1)}, bf16[512,256]{1,0:T(8,128)(2,1)S(1)}, u32[]{:S(2)}, u32[]{:S(2)}) %collective-permute-start.3) | collective-permute-done | bytes 262176 | tf_op jit(solution)/shard_map/ppermute | solution.py:367
  84.7 0.6 collective-permute-done.4
  85.3 6.0 %collective-permute-done.5 = bf16[512,256]{1,0:T(8,128)(2,1)S(1)} collective-permute-done((bf16[512,256]{1,0:T(8,128)(2,1)}, bf16[512,256]{1,0:T(8,128)(2,1)S(1)}, u32[]{:S(2)}, u32[]{:S(2)}) %collective-permute-start.5) | collective-permute-done | bytes 262176 | tf_op jit(solution)/shard_map/ppermute | solution.py:367
  91.3 1.3 multiply_convert_fusion.1.a0_ref
  92.6 2.4 collective-permute-start.8
  95.0 1.3 collective-permute-start.7
  96.3 0.5 collective-permute-start.6
  96.8 2.0 hold.2.w_ref
  98.9 2.4 collective-permute-done.8.a3_ref
  101.3 7.5 %collective-permute-done.7.a2_ref = bf16[512,256]{1,0:T(8,128)(2,1)S(1)} collective-permute-done((bf16[512,256]{1,0:T(8,128)(2,1)S(1)}, bf16[512,256]{1,0:T(8,128)(2,1)S(1)}, u32[]{:S(2)}, u32[]{:S(2)}) %collective-permute-start.7) | collective-permute-done | bytes 262176 | tf_op jit(solution)/shard_map/ppermute | solution.py:367
  108.8 0.0 collective-permute-done.6.a1_ref
  108.8 3.9 %merged.2 = (bf16[512,1792]{1,0:T(8,128)(2,1)}, bf16[1024,512]{1,0:T(8,128)(2,1)}) custom-call(s32[4]{0:T(128)S(1)} %pad_add_fusion.side_ref, bf16[512,256]{1,0:T(8,128)(2,1)S(1)} %multiply_convert_fusion.1.a0_ref, bf16[512,256]{1,0:T(8,128)(2,1)S(1)} %collective-permute-done.6.a1_ref, bf16[512,256]{1,0:T(8,128)(2,1)S(1)} %collective-permute-done.7.a2_ref, ...), custom_call_target="tpu_custom_call" | custom-call | flops 1879048192 | bytes 6553600 | tf_op jit(solution)/shard_map/merged/pallas_call | solution.py:284
  112.7 0.0 copy-start
  112.7 2.0 copy-done
  114.7 3.6 %partials.3 = (f32[512,256]{1,0:T(8,128)}, f32[512,256]{1,0:T(8,128)}, bf16[512,256]{1,0:T(8,128)(2,1)}, bf16[512,256]{1,0:T(8,128)(2,1)}, bf16[512,1792]{1,0:T(8,128)(2,1)}) custom-call(s32[4]{0:T(128)S(1)} %pad_add_fusion.side_ref, bf16[512,1792]{1,0:T(8,128)(2,1)S(1)} %bitcast.30, bf16[1024,1792]{1,0:T(8,128)(2,1)S(1)} %bitcast.27), custom_call_target="tpu_custom_call" | custom-call | flops 1879048192 | bytes 6815744 | tf_op jit(solution)/shard_map/partials/pallas_call | solution.py:233
  118.3 7.5 %all-to-all-start.2 = ((bf16[32,16,1792]{2,1,0:T(8,128)(2,1)}), bf16[32,16,1792]{2,1,0:T(8,128)(2,1)S(1)}, u32[]{:S(2)}, u32[]{:S(2)}) async-start(bf16[32,16,1792]{2,1,0:T(8,128)(2,1)} %bitcast.34), calls=%async_computation.2 | async-start | bytes 3670016 | tf_op jit(solution)/shard_map/all_to_all | solution.py:382
  125.8 0.5 collective-permute-start.10
  126.3 1.1 collective-permute-start.9
  127.4 6.4 %collective-permute-done.10 = bf16[512,256]{1,0:T(8,128)(2,1)S(1)} collective-permute-done((bf16[512,256]{1,0:T(8,128)(2,1)}, bf16[512,256]{1,0:T(8,128)(2,1)S(1)}, u32[]{:S(2)}, u32[]{:S(2)}) %collective-permute-start.10) | collective-permute-done | bytes 262176 | tf_op jit(solution)/shard_map/ppermute | solution.py:367
  133.8 1.1 add_convert_fusion.1
  134.9 1.6 collective-permute-start.11
  136.5 7.3 %weight_parts.1 = (bf16[192,1792]{1,0:T(8,128)(2,1)}, bf16[320,1792]{1,0:T(8,128)(2,1)}, bf16[512,1792]{1,0:T(8,128)(2,1)}) custom-call(s32[4]{0:T(128)S(1)} %pad_add_fusion.side_ref, bf16[1024,512]{1,0:T(8,128)(2,1)} %get-tuple-element.74.act_ref, bf16[512,1792]{1,0:T(8,128)(2,1)} %get-tuple-element.75.d_ref), custom_call_target="tpu_custom_call" | custom-call | flops 1879048192 | bytes 6553600 | tf_op jit(solution)/shard_map/weight_parts/pallas_call | solution.py:317
  143.8 0.0 copy-start.10
  143.8 4.4 %collective-permute-done.11 = bf16[512,256]{1,0:T(8,128)(2,1)S(1)} collective-permute-done((bf16[512,256]{1,0:T(8,128)(2,1)S(1)}, bf16[512,256]{1,0:T(8,128)(2,1)S(1)}, u32[]{:S(2)}, u32[]{:S(2)}) %collective-permute-start.11) | collective-permute-done | bytes 262176 | tf_op jit(solution)/shard_map/ppermute | solution.py:367
  148.2 0.4 multiply_convert_fusion.a0_ref
  148.6 1.2 collective-permute-start.13
  149.7 0.8 collective-permute-start.12
  150.6 4.8 %collective-permute-done.13.a2_ref = bf16[512,256]{1,0:T(8,128)(2,1)S(1)} collective-permute-done((bf16[512,256]{1,0:T(8,128)(2,1)S(1)}, bf16[512,256]{1,0:T(8,128)(2,1)S(1)}, u32[]{:S(2)}, u32[]{:S(2)}) %collective-permute-start.13) | collective-permute-done | bytes 262176 | tf_op jit(solution)/shard_map/ppermute | solution.py:367
  155.4 10.6 %collective-permute-done.12.a1_ref = bf16[512,256]{1,0:T(8,128)(2,1)S(1)} collective-permute-done((bf16[512,256]{1,0:T(8,128)(2,1)S(1)}, bf16[512,256]{1,0:T(8,128)(2,1)S(1)}, u32[]{:S(2)}, u32[]{:S(2)}) %collective-permute-start.12) | collective-permute-done | bytes 262176 | tf_op jit(solution)/shard_map/ppermute | solution.py:367
  166.0 3.1 %collective-permute-start.15 = (bf16[192,1792]{1,0:T(8,128)(2,1)S(1)}, bf16[192,1792]{1,0:T(8,128)(2,1)S(1)}, u32[]{:S(2)}, u32[]{:S(2)}) collective-permute-start(bf16[192,1792]{1,0:T(8,128)(2,1)S(1)} %copy-done.10), channel_id=1, source_target_pairs={{0,224},{32,192},{64,160},{96,128},{128,96},{160,64},{192,32},{224... | collective-permute-start | bytes 2064392 | tf_op jit(solution)/shard_map/ppermute | solution.py:376
  169.1 0.0 collective-permute-start.14
  169.1 2.0 hold.3.w_ref
  171.1 4.3 %collective-permute-done.14.a3_ref = bf16[512,256]{1,0:T(8,128)(2,1)S(1)} collective-permute-done((bf16[512,256]{1,0:T(8,128)(2,1)S(1)}, bf16[512,256]{1,0:T(8,128)(2,1)S(1)}, u32[]{:S(2)}, u32[]{:S(2)}) %collective-permute-start.14) | collective-permute-done | bytes 262176 | tf_op jit(solution)/shard_map/ppermute | solution.py:367
  175.4 3.7 %merged.3 = bf16[512,1792]{1,0:T(8,128)(2,1)} custom-call(s32[4]{0:T(128)S(1)} %pad_add_fusion.side_ref, bf16[512,256]{1,0:T(8,128)(2,1)S(1)} %multiply_convert_fusion.a0_ref, bf16[512,256]{1,0:T(8,128)(2,1)S(1)} %collective-permute-done.12.a1_ref, bf16[512,256]{1,0:T(8,128)(2,1)S(1)} %collective-permute-done.13.a2_ref, ...), custom_call_target="tpu_custom_call" | custom-call | flops 1879048192 | bytes 6553600 | tf_op jit(solution)/shard_map/merged/pallas_call | solution.py:284
  179.1 6.3 %collective-permute-done.15 = bf16[192,1792]{1,0:T(8,128)(2,1)S(1)} collective-permute-done((bf16[192,1792]{1,0:T(8,128)(2,1)S(1)}, bf16[192,1792]{1,0:T(8,128)(2,1)S(1)}, u32[]{:S(2)}, u32[]{:S(2)}) %collective-permute-start.15) | collective-permute-done | bytes 688160 | tf_op jit(solution)/shard_map/ppermute | solution.py:376
  185.4 7.3 %all-to-all-start.3 = ((bf16[32,16,1792]{2,1,0:T(8,128)(2,1)}), bf16[32,16,1792]{2,1,0:T(8,128)(2,1)}, u32[]{:S(2)}, u32[]{:S(2)}) async-start(bf16[32,16,1792]{2,1,0:T(8,128)(2,1)} %bitcast.35), calls=%async_computation.3 | async-start | bytes 3670016 | tf_op jit(solution)/shard_map/all_to_all | solution.py:382
  192.7 4.0 %collective-permute-start.16 = (bf16[320,1792]{1,0:T(8,128)(2,1)}, bf16[320,1792]{1,0:T(8,128)(2,1)S(1)}, u32[]{:S(2)}, u32[]{:S(2)}) collective-permute-start(bf16[320,1792]{1,0:T(8,128)(2,1)} %get-tuple-element.88), channel_id=1, source_target_pairs={{0,224},{32,192},{64,160},{96,128},{128,96},{160,64},{192,32},{224... | collective-permute-start | bytes 3440648 | tf_op jit(solution)/shard_map/ppermute | solution.py:376
  196.7 1.4 combine.2
  198.1 43.6 %collective-permute-done.16 = bf16[320,1792]{1,0:T(8,128)(2,1)S(1)} collective-permute-done((bf16[320,1792]{1,0:T(8,128)(2,1)}, bf16[320,1792]{1,0:T(8,128)(2,1)S(1)}, u32[]{:S(2)}, u32[]{:S(2)}) %collective-permute-start.16) | collective-permute-done | bytes 1146912 | tf_op jit(solution)/shard_map/ppermute | solution.py:376
  241.7 1.7 fusion
  243.4 2.9 %combine.3 = bf16[256,1792]{1,0:T(8,128)(2,1)} custom-call(bf16[256,512]{1,0:T(8,128)(2,1)S(1)} %get-tuple-element.90.table_ref, bf16[512,1792]{1,0:T(8,128)(2,1)} %bitcast.22.x_ref), custom_call_target="tpu_custom_call" | custom-call | flops 469762048 | bytes 2752512 | tf_op jit(solution)/shard_map/combine/pallas_call | solution.py:353
  (20 shorter events, 0.0 us)
Async XLA Ops:
  4.3 57.9 %all-to-all-start = ((bf16[32,16,1792]{2,1,0:T(8,128)(2,1)}), bf16[32,16,1792]{2,1,0:T(8,128)(2,1)S(1)}, u32[]{:S(2)}, u32[]{:S(2)}) async-start(bf16[32,16,1792]{2,1,0:T(8,128)(2,1)} %bitcast.33), calls=%async_computation | async-start | bytes 3670016 | tf_op jit(solution)/shard_map/all_to_all | solution.py:382
  19.0 2.2 collective-permute-start.1
  19.4 20.3 %collective-permute-start.2 = (bf16[128,1792]{1,0:T(8,128)(2,1)}, bf16[128,1792]{1,0:T(8,128)(2,1)S(1)}, u32[]{:S(2)}, u32[]{:S(2)}) collective-permute-start(bf16[128,1792]{1,0:T(8,128)(2,1)} %get-tuple-element.53), channel_id=1, source_target_pairs={{0,16},{1,17},{2,18},{3,19},{4,20},{5,21},{6,22},{7,23},{8,24},{9,... | collective-permute-start | bytes 1376264 | tf_op jit(solution)/shard_map/ppermute | solution.py:405
  20.9 38.2 %collective-permute-start = (bf16[128,1792]{1,0:T(8,128)(2,1)}, bf16[128,1792]{1,0:T(8,128)(2,1)S(1)}, u32[]{:S(2)}, u32[]{:S(2)}) collective-permute-start(bf16[128,1792]{1,0:T(8,128)(2,1)} %get-tuple-element.50), channel_id=1, source_target_pairs={{0,17},{1,16},{2,19},{3,18},{4,21},{5,20},{6,23},{7,22},{8,25},{9,... | collective-permute-start | bytes 1376264 | tf_op jit(solution)/shard_map/ppermute | solution.py:405
  21.3 18.4 %copy-start.8 = (bf16[128,1792]{1,0:T(8,128)(2,1)}, bf16[128,1792]{1,0:T(8,128)(2,1)S(1)}, u32[]{:S(2)}) copy-start(bf16[128,1792]{1,0:T(8,128)(2,1)S(1)} %collective-permute-done.1) | copy-start | bytes 1376260
  39.7 0.8 copy-start.9
  59.1 0.8 copy-start.7
  62.2 1.2 copy-start.2
  63.5 49.2 %all-to-all-start.1 = ((bf16[8,64,1792]{2,1,0:T(8,128)(2,1)}), bf16[8,64,1792]{2,1,0:T(8,128)(2,1)S(1)}, u32[]{:S(2)}, u32[]{:S(2)}) async-start(bf16[8,64,1792]{2,1,0:T(8,128)(2,1)} %bitcast.32), calls=%async_computation.1 | async-start | bytes 3670016 | tf_op jit(solution)/shard_map/all_to_all | solution.py:382
  68.6 2.0 copy-start.1
  70.6 1.5 copy-start.3
  75.7 9.0 %collective-permute-start.3 = (bf16[512,256]{1,0:T(8,128)(2,1)}, bf16[512,256]{1,0:T(8,128)(2,1)S(1)}, u32[]{:S(2)}, u32[]{:S(2)}) collective-permute-start(bf16[512,256]{1,0:T(8,128)(2,1)} %get-tuple-element.56), channel_id=1, source_target_pairs={{0,32},{32,0},{64,96},{96,64},{128,160},{160,128},{192,224},{224,1... | collective-permute-start | bytes 786440 | tf_op jit(solution)/shard_map/ppermute | solution.py:367
  78.3 7.1 %collective-permute-start.4 = (bf16[512,256]{1,0:T(8,128)(2,1)}, bf16[512,256]{1,0:T(8,128)(2,1)S(1)}, u32[]{:S(2)}, u32[]{:S(2)}) collective-permute-start(bf16[512,256]{1,0:T(8,128)(2,1)} %get-tuple-element.57), channel_id=1, source_target_pairs={{0,64},{32,96},{64,0},{96,32},{128,192},{160,224},{192,128},{224,1... | collective-permute-start | bytes 786440 | tf_op jit(solution)/shard_map/ppermute | solution.py:367
  79.5 11.8 %collective-permute-start.5 = (bf16[512,256]{1,0:T(8,128)(2,1)}, bf16[512,256]{1,0:T(8,128)(2,1)S(1)}, u32[]{:S(2)}, u32[]{:S(2)}) collective-permute-start(bf16[512,256]{1,0:T(8,128)(2,1)} %get-tuple-element.58), channel_id=1, source_target_pairs={{0,96},{32,64},{64,32},{96,0},{128,224},{160,192},{192,160},{224,1... | collective-permute-start | bytes 786440 | tf_op jit(solution)/shard_map/ppermute | solution.py:367
  92.6 8.7 %collective-permute-start.8 = (bf16[512,256]{1,0:T(8,128)(2,1)S(1)}, bf16[512,256]{1,0:T(8,128)(2,1)S(1)}, u32[]{:S(2)}, u32[]{:S(2)}) collective-permute-start(bf16[512,256]{1,0:T(8,128)(2,1)S(1)} %multiply_convert_fusion.1.a0_ref), channel_id=1, source_target_pairs={{0,96},{32,64},{64,32},{96,0},{128,224},{160,192},{192,160},{224,1... | collective-permute-start | bytes 786440 | tf_op jit(solution)/shard_map/ppermute | solution.py:367
  95.0 13.8 %collective-permute-start.7 = (bf16[512,256]{1,0:T(8,128)(2,1)S(1)}, bf16[512,256]{1,0:T(8,128)(2,1)S(1)}, u32[]{:S(2)}, u32[]{:S(2)}) collective-permute-start(bf16[512,256]{1,0:T(8,128)(2,1)S(1)} %multiply_convert_fusion.1.a0_ref), channel_id=1, source_target_pairs={{0,64},{32,96},{64,0},{96,32},{128,192},{160,224},{192,128},{224,1... | collective-permute-start | bytes 786440 | tf_op jit(solution)/shard_map/ppermute | solution.py:367
  96.3 12.5 %collective-permute-start.6 = (bf16[512,256]{1,0:T(8,128)(2,1)S(1)}, bf16[512,256]{1,0:T(8,128)(2,1)S(1)}, u32[]{:S(2)}, u32[]{:S(2)}) collective-permute-start(bf16[512,256]{1,0:T(8,128)(2,1)S(1)} %multiply_convert_fusion.1.a0_ref), channel_id=1, source_target_pairs={{0,32},{32,0},{64,96},{96,64},{128,160},{160,128},{192,224},{224,1... | collective-permute-start | bytes 786440 | tf_op jit(solution)/shard_map/ppermute | solution.py:367
  112.7 2.0 copy-start
  118.3 8.0 %copy-start.11 = (bf16[512,256]{1,0:T(8,128)(2,1)S(1)}, bf16[512,256]{1,0:T(8,128)(2,1)}, u32[]{:S(2)}) copy-start(bf16[512,256]{1,0:T(8,128)(2,1)} %get-tuple-element.71) | copy-start | bytes 786436
  118.3 67.0 %all-to-all-start.2 = ((bf16[32,16,1792]{2,1,0:T(8,128)(2,1)}), bf16[32,16,1792]{2,1,0:T(8,128)(2,1)S(1)}, u32[]{:S(2)}, u32[]{:S(2)}) async-start(bf16[32,16,1792]{2,1,0:T(8,128)(2,1)} %bitcast.34), calls=%async_computation.2 | async-start | bytes 3670016 | tf_op jit(solution)/shard_map/all_to_all | solution.py:382
  125.8 8.0 %collective-permute-start.10 = (bf16[512,256]{1,0:T(8,128)(2,1)}, bf16[512,256]{1,0:T(8,128)(2,1)S(1)}, u32[]{:S(2)}, u32[]{:S(2)}) collective-permute-start(bf16[512,256]{1,0:T(8,128)(2,1)} %get-tuple-element.73), channel_id=1, source_target_pairs={{0,64},{32,96},{64,0},{96,32},{128,192},{160,224},{192,128},{224,1... | collective-permute-start | bytes 786440 | tf_op jit(solution)/shard_map/ppermute | solution.py:367
  126.3 17.5 %collective-permute-start.9 = (bf16[512,256]{1,0:T(8,128)(2,1)S(1)}, bf16[512,256]{1,0:T(8,128)(2,1)S(1)}, u32[]{:S(2)}, u32[]{:S(2)}) collective-permute-start(bf16[512,256]{1,0:T(8,128)(2,1)S(1)} %copy-done.11), channel_id=1, source_target_pairs={{0,64},{32,96},{64,0},{96,32},{128,192},{160,224},{192,128},{224,1... | collective-permute-start | bytes 786440 | tf_op jit(solution)/shard_map/ppermute | solution.py:367
  134.9 13.3 %collective-permute-start.11 = (bf16[512,256]{1,0:T(8,128)(2,1)S(1)}, bf16[512,256]{1,0:T(8,128)(2,1)S(1)}, u32[]{:S(2)}, u32[]{:S(2)}) collective-permute-start(bf16[512,256]{1,0:T(8,128)(2,1)S(1)} %add_convert_fusion.1), channel_id=1, source_target_pairs={{0,32},{32,0},{64,96},{96,64},{128,160},{160,128},{192,224},{224,1... | collective-permute-start | bytes 786440 | tf_op jit(solution)/shard_map/ppermute | solution.py:367
  136.5 11.7 %copy-start.4 = (f32[512,256]{1,0:T(8,128)S(1)}, f32[512,256]{1,0:T(8,128)}, u32[]{:S(2)}) copy-start(f32[512,256]{1,0:T(8,128)} %get-tuple-element.55) | copy-start | bytes 1572868
  136.5 11.7 %copy-start.6 = (f32[512,256]{1,0:T(8,128)S(1)}, f32[512,256]{1,0:T(8,128)}, u32[]{:S(2)}) copy-start(f32[512,256]{1,0:T(8,128)} %get-tuple-element.70) | copy-start | bytes 1572868
  143.8 22.2 %copy-start.10 = (bf16[192,1792]{1,0:T(8,128)(2,1)S(1)}, bf16[192,1792]{1,0:T(8,128)(2,1)}, u32[]{:S(2)}) copy-start(bf16[192,1792]{1,0:T(8,128)(2,1)} %get-tuple-element.84) | copy-start | bytes 2064388
  148.6 6.8 %collective-permute-start.13 = (bf16[512,256]{1,0:T(8,128)(2,1)S(1)}, bf16[512,256]{1,0:T(8,128)(2,1)S(1)}, u32[]{:S(2)}, u32[]{:S(2)}) collective-permute-start(bf16[512,256]{1,0:T(8,128)(2,1)S(1)} %multiply_convert_fusion.a0_ref), channel_id=1, source_target_pairs={{0,64},{32,96},{64,0},{96,32},{128,192},{160,224},{192,128},{224,1... | collective-permute-start | bytes 786440 | tf_op jit(solution)/shard_map/ppermute | solution.py:367
  149.7 16.2 %collective-permute-start.12 = (bf16[512,256]{1,0:T(8,128)(2,1)S(1)}, bf16[512,256]{1,0:T(8,128)(2,1)S(1)}, u32[]{:S(2)}, u32[]{:S(2)}) collective-permute-start(bf16[512,256]{1,0:T(8,128)(2,1)S(1)} %multiply_convert_fusion.a0_ref), channel_id=1, source_target_pairs={{0,32},{32,0},{64,96},{96,64},{128,160},{160,128},{192,224},{224,1... | collective-permute-start | bytes 786440 | tf_op jit(solution)/shard_map/ppermute | solution.py:367
  166.0 19.4 %collective-permute-start.15 = (bf16[192,1792]{1,0:T(8,128)(2,1)S(1)}, bf16[192,1792]{1,0:T(8,128)(2,1)S(1)}, u32[]{:S(2)}, u32[]{:S(2)}) collective-permute-start(bf16[192,1792]{1,0:T(8,128)(2,1)S(1)} %copy-done.10), channel_id=1, source_target_pairs={{0,224},{32,192},{64,160},{96,128},{128,96},{160,64},{192,32},{224... | collective-permute-start | bytes 2064392 | tf_op jit(solution)/shard_map/ppermute | solution.py:376
  169.1 6.4 %collective-permute-start.14 = (bf16[512,256]{1,0:T(8,128)(2,1)S(1)}, bf16[512,256]{1,0:T(8,128)(2,1)S(1)}, u32[]{:S(2)}, u32[]{:S(2)}) collective-permute-start(bf16[512,256]{1,0:T(8,128)(2,1)S(1)} %collective-permute-done.12.a1_ref), channel_id=1, source_target_pairs={{0,64},{32,96},{64,0},{96,32},{128,192},{160,224},{192,128},{224,1... | collective-permute-start | bytes 786440 | tf_op jit(solution)/shard_map/ppermute | solution.py:367
  185.4 58.1 %all-to-all-start.3 = ((bf16[32,16,1792]{2,1,0:T(8,128)(2,1)}), bf16[32,16,1792]{2,1,0:T(8,128)(2,1)}, u32[]{:S(2)}, u32[]{:S(2)}) async-start(bf16[32,16,1792]{2,1,0:T(8,128)(2,1)} %bitcast.35), calls=%async_computation.3 | async-start | bytes 3670016 | tf_op jit(solution)/shard_map/all_to_all | solution.py:382
  192.7 49.1 %copy-start.5 = (bf16[512,1792]{1,0:T(8,128)(2,1)S(1)}, bf16[512,1792]{1,0:T(8,128)(2,1)}, u32[]{:S(2)}) copy-start(bf16[512,1792]{1,0:T(8,128)(2,1)} %get-tuple-element.92) | copy-start | bytes 5505028
  192.7 49.1 %collective-permute-start.16 = (bf16[320,1792]{1,0:T(8,128)(2,1)}, bf16[320,1792]{1,0:T(8,128)(2,1)S(1)}, u32[]{:S(2)}, u32[]{:S(2)}) collective-permute-start(bf16[320,1792]{1,0:T(8,128)(2,1)} %get-tuple-element.88), channel_id=1, source_target_pairs={{0,224},{32,192},{64,160},{96,128},{128,96},{160,64},{192,32},{224... | collective-permute-start | bytes 3440648 | tf_op jit(solution)/shard_map/ppermute | solution.py:376

commit v3 on v2

--- a/solution.py
+++ b/solution.py
@@ -327,17 +327,22 @@
     )(side, far(acts), far(d_out))
 
 
-def combine_kernel(table_ref, x_ref, *refs, kept):
+def combine_kernel(*refs, count, kept):
+    table_ref, parts, refs = refs[0], refs[1 : count + 1], refs[count + 1 :]
     if kept:
         next_ref, out_ref, next_out, out_all, sems = refs
     else:
         out_ref, out_all, sems = refs
     copies = []
     tokens, width = out_all.shape
-    cols = column_block(width)
+    cols, rows = column_block(width), parts[0].shape[0]
     for i in range(width // cols):
         span = (slice(None), slice(i * cols, (i + 1) * cols))
-        out_all[span] = dot(table_ref[...], x_ref[span], 1, 0).astype(BF)
+        total = None
+        for k, ref in enumerate(parts):
+            part = dot(table_ref[:, k * rows : (k + 1) * rows], ref[span], 1, 0)
+            total = part if total is None else total + part
+        out_all[span] = total.astype(BF)
         copies.append(pltpu.make_async_copy(out_all.at[span], out_ref.at[span], sems.at[i]))
         copies[-1].start()
     if kept:
@@ -346,20 +351,20 @@
         copy.wait()
 
 
-def combine(table, rows, following=None):
+def combine(table, parts, following=None):
     tokens, slots = table.shape
-    width = rows.shape[1]
+    width = parts[0].shape[1]
     kept = following is not None
     return pl.pallas_call(
-        functools.partial(combine_kernel, kept=kept),
-        in_specs=[RESIDENT] * (3 if kept else 2),
+        functools.partial(combine_kernel, count=len(parts), kept=kept),
+        in_specs=[RESIDENT] * (1 + len(parts) + kept),
         out_specs=[FAR] + [RESIDENT] * kept,
         out_shape=[pltpu.HBM((tokens, width), BF)] + [pltpu.VMEM(table.shape, BF)] * kept,
         scratch_shapes=[pltpu.VMEM((tokens, width), BF), pltpu.SemaphoreType.DMA((width // column_block(width),))],
         compiler_params=params(),
         cost_estimate=cost(2 * slots * tokens * width, 2 * (slots + tokens) * width),
         name="combine",
-    )(*((table, rows, following) if kept else (near(table), near(rows))))
+    )(*((table, *parts, following) if kept else (near(table), *[near(part) for part in parts])))
 
 
 def to_member(block, flip):
@@ -433,7 +438,7 @@
     beside = to_member(d_hidden, 1)
     far_off = to_member(d_hidden, 2)
     up_held = hold(up)
-    beside, far_off, first = lax.optimization_barrier((beside, far_off, first))
+    far_off, first = lax.optimization_barrier((far_off, first))
     d_hiddens = [d_hidden, beside, far_off, to_member(beside, 2)]
     first = to_mirror(first)
     (d_rows,) = merged(side, d_hiddens, up_held, True)
@@ -441,11 +446,11 @@
     returned_dx = exchange(d_rows, everyone)
     rest = to_mirror(rest)
 
-    layer_out, plain_held = combine(gated_flipped, returned, plain_flipped)
-    layer_out, rest = lax.optimization_barrier((layer_out, rest))
+    layer_out, plain_held = combine(gated_flipped, [returned], plain_flipped)
+    (grad_tokens,) = combine(plain_held, [returned_dx])
+    grad_tokens, rest = lax.optimization_barrier((grad_tokens, rest))
     arrived = jnp.concatenate([first, rest])
     grad_weight = (own_weight.astype(F32) + arrived.astype(F32)).astype(BF)
-    (grad_tokens,) = combine(plain_held, returned_dx)
     return (layer_out, grad_tokens, grad_weight[None])
 
 

time: 247 us -> 242 us (0.980)
  waiting for transfers between devices: 136 us -> 130 us
    ppermute x2, waiting for transfers between devices: 49.9 us -> 6.9 us  [to_mirror(): lax.ppermute(block, 'pipe', [(p, count - 1 - p) for p in range(count)])]
    all_to_all x4, waiting for transfers between devices: 0.01 us -> 40.9 us  [exchange(): lax.all_to_all(blocks, 'expert', split_axis=0, concat_axis=0, tiled=True,...]
    ppermute x12, waiting for transfers between devices: 51.8 us -> 48.3 us  [to_member(): return lax.ppermute(block, 'pipe', [(p, p ^ flip) for p in range(count)])]
  transfers between devices with their start and end apart: 21 -> 21, of which waited for: 14 -> 14; matrix products, arithmetic and copies ran while one was open for 2% -> 1% of each run, Pallas kernels for 13% -> 15%
where the time goes in v3:
time: 242 us; the launch traced here: 241 us
  waiting for transfers between devices  130 us (54%)
  starting transfers between devices  52.7 us (22%)
  Pallas kernels  42.6 us (18%)
  local copies, waits for them, and re-layouts  8.36 us (3%)
  other arithmetic  5.73 us (2%)
    ppermute x12, waiting for transfers between devices, to_member(): return lax.ppermute(block, 'pipe', [(p, p ^ flip) for p in range(count)])  48.3 us
    all_to_all x4, waiting for transfers between devices, exchange(): lax.all_to_all(blocks, 'expert', split_axis=0, concat_axis=0, tiled=True,...  40.9 us
    ppermute x3, waiting for transfers between devices, shards(): lax.ppermute(pieces[j], 'expert', [(e, e ^ flip) for e in range(experts)])  34.3 us
    all_to_all x4, starting transfers between devices, exchange(): lax.all_to_all(blocks, 'expert', split_axis=0, concat_axis=0, tiled=True,...  31.4 us
    ppermute x12, starting transfers between devices, to_member(): return lax.ppermute(block, 'pipe', [(p, p ^ flip) for p in range(count)])  13.7 us
    unnamed x24, local copies, waits for them, and re-layouts  8.36 us
    pallas_call x2, Pallas kernels, merged(): pl.pallas_call(functools.partial(merge_kernel, transposed=transposed), in...  7.51 us
    pallas_call x1, Pallas kernels, weight_parts(): pl.pallas_call(weight_kernel, grid=(width // cols,), in_specs=[SCALARS, p...  7.24 us
  transfers between devices with their start and end apart: 21, of which 14 were waited for; matrix products, arithmetic and copies ran while one was open for 1% of the time, Pallas kernels for 15%

profile of v3, /device:TPU:1, one launch (start us, length us, event | category | flops | bytes accessed | tf_op | source)
XLA Modules:
  0.0 240.8 jit_solution(8640462121705160681)
XLA Ops:
  0.7 0.1 pad_add_fusion.side_ref
  0.7 3.5 %dispatch.3 = bf16[512,1792]{1,0:T(8,128)(2,1)} custom-call(s32[4]{0:T(128)S(1)} %pad_add_fusion.side_ref, s32[8,256]{1,0:T(8,128)} %bitcast.40, s32[8,256]{1,0:T(8,128)} %bitcast.42, bf16[8,256]{1,0:T(8,128)(2,1)} %bitcast.44, bf16[8,256]{1,0:T(8,128)(2,1)} %bitcast.46, bf16[256,1792]{1,0:T(8,128)(2,1)} %x_ref.3), custom_call_target="tpu_custom_call" | custom-call | flops 469762048 | bytes 2752512 | tf_op jit(solution)/shard_map/dispatch/pallas_call | solution.py:133
  4.3 11.1 %all-to-all-start = ((bf16[32,16,1792]{2,1,0:T(8,128)(2,1)}), bf16[32,16,1792]{2,1,0:T(8,128)(2,1)S(1)}, u32[]{:S(2)}, u32[]{:S(2)}) async-start(bf16[32,16,1792]{2,1,0:T(8,128)(2,1)} %bitcast.33), calls=%async_computation | async-start | bytes 3670016 | tf_op jit(solution)/shard_map/all_to_all | solution.py:387
  15.3 3.7 %dispatch.2 = (bf16[128,1792]{1,0:T(8,128)(2,1)}, bf16[128,1792]{1,0:T(8,128)(2,1)}, bf16[128,1792]{1,0:T(8,128)(2,1)}, bf16[128,1792]{1,0:T(8,128)(2,1)}, bf16[...) custom-call(s32[4]{0:T(128)S(1)} %pad_add_fusion.side_ref, s32[8,256]{1,0:T(8,128)} %bitcast.41, s32[8,256]{1,0:T(8,128)} %bitcast.43, ...), custom_call_target="tpu_custom_call" | custom-call | flops 469762048 | bytes 2752512 | tf_op jit(solution)/shard_map/dispatch/pallas_call | solution.py:133
  19.0 0.3 collective-permute-start.1
  19.4 1.5 collective-permute-start.2
  20.9 0.4 collective-permute-start
  21.3 0.0 collective-permute-done.1
  21.3 18.4 %collective-permute-done.2 = bf16[128,1792]{1,0:T(8,128)(2,1)S(1)} collective-permute-done((bf16[128,1792]{1,0:T(8,128)(2,1)}, bf16[128,1792]{1,0:T(8,128)(2,1)S(1)}, u32[]{:S(2)}, u32[]{:S(2)}) %collective-permute-start.2) | collective-permute-done | bytes 458784 | tf_op jit(solution)/shard_map/ppermute | solution.py:410
  39.7 0.8 copy-done.9
  40.5 2.8 %regroup.2.refs_1_ = bf16[8,4,16,1792]{3,2,1,0:T(8,128)(2,1)} custom-call(s32[4]{0:T(128)S(1)} %pad_add_fusion.side_ref, bf16[8,16,1792]{2,1,0:T(8,128)(2,1)} %bitcast.37, bf16[8,16,1792]{2,1,0:T(8,128)(2,1)} %bitcast.38, bf16[8,16,1792]{2,1,0:T(8,128)(2,1)} %bitcast.39), custom_call_target="tpu_custom_call" | custom-call | bytes 2752512 | tf_op jit(solution)/shard_map/regroup/pallas_call | solution.py:171
  43.2 15.8 %collective-permute-done = bf16[128,1792]{1,0:T(8,128)(2,1)S(1)} collective-permute-done((bf16[128,1792]{1,0:T(8,128)(2,1)}, bf16[128,1792]{1,0:T(8,128)(2,1)S(1)}, u32[]{:S(2)}, u32[]{:S(2)}) %collective-permute-start) | collective-permute-done | bytes 458784 | tf_op jit(solution)/shard_map/ppermute | solution.py:410
  59.1 0.8 copy-done.7
  59.8 2.4 regroup.3
  62.2 0.0 copy-start.2
  62.2 1.2 copy-done.2
  63.5 5.1 %all-to-all-start.1 = ((bf16[8,64,1792]{2,1,0:T(8,128)(2,1)}), bf16[8,64,1792]{2,1,0:T(8,128)(2,1)S(1)}, u32[]{:S(2)}, u32[]{:S(2)}) async-start(bf16[8,64,1792]{2,1,0:T(8,128)(2,1)} %bitcast.32), calls=%async_computation.1 | async-start | bytes 3670016 | tf_op jit(solution)/shard_map/all_to_all | solution.py:387
  68.6 2.0 copy-done.1
  70.6 1.5 copy-done.3
  72.1 3.6 %partials.2 = (f32[512,256]{1,0:T(8,128)}, bf16[512,256]{1,0:T(8,128)(2,1)}, bf16[512,256]{1,0:T(8,128)(2,1)}, bf16[512,256]{1,0:T(8,128)(2,1)}) custom-call(s32[4]{0:T(128)S(1)} %pad_add_fusion.side_ref, bf16[512,1792]{1,0:T(8,128)(2,1)S(1)} %bitcast.31, bf16[1792,1024]{1,0:T(8,128)(2,1)S(1)} %bitcast.29), custom_call_target="tpu_custom_call" | custom-call | flops 1879048192 | bytes 6815744 | tf_op jit(solution)/shard_map/partials/pallas_call | solution.py:233
  75.7 2.5 %collective-permute-start.3 = (bf16[512,256]{1,0:T(8,128)(2,1)}, bf16[512,256]{1,0:T(8,128)(2,1)S(1)}, u32[]{:S(2)}, u32[]{:S(2)}) collective-permute-start(bf16[512,256]{1,0:T(8,128)(2,1)} %get-tuple-element.55), channel_id=1, source_target_pairs={{0,32},{32,0},{64,96},{96,64},{128,160},{160,128},{192,224},{224,1... | collective-permute-start | bytes 786440 | tf_op jit(solution)/shard_map/ppermute | solution.py:372
  78.3 1.3 collective-permute-start.4
  79.5 0.4 collective-permute-start.5
  79.9 4.7 %collective-permute-done.3 = bf16[512,256]{1,0:T(8,128)(2,1)S(1)} collective-permute-done((bf16[512,256]{1,0:T(8,128)(2,1)}, bf16[512,256]{1,0:T(8,128)(2,1)S(1)}, u32[]{:S(2)}, u32[]{:S(2)}) %collective-permute-start.3) | collective-permute-done | bytes 262176 | tf_op jit(solution)/shard_map/ppermute | solution.py:372
  84.7 0.6 collective-permute-done.4
  85.3 6.0 %collective-permute-done.5 = bf16[512,256]{1,0:T(8,128)(2,1)S(1)} collective-permute-done((bf16[512,256]{1,0:T(8,128)(2,1)}, bf16[512,256]{1,0:T(8,128)(2,1)S(1)}, u32[]{:S(2)}, u32[]{:S(2)}) %collective-permute-start.5) | collective-permute-done | bytes 262176 | tf_op jit(solution)/shard_map/ppermute | solution.py:372
  91.3 1.3 multiply_convert_fusion.1.a0_ref
  92.6 2.4 %collective-permute-start.8 = (bf16[512,256]{1,0:T(8,128)(2,1)S(1)}, bf16[512,256]{1,0:T(8,128)(2,1)S(1)}, u32[]{:S(2)}, u32[]{:S(2)}) collective-permute-start(bf16[512,256]{1,0:T(8,128)(2,1)S(1)} %multiply_convert_fusion.1.a0_ref), channel_id=1, source_target_pairs={{0,96},{32,64},{64,32},{96,0},{128,224},{160,192},{192,160},{224,1... | collective-permute-start | bytes 786440 | tf_op jit(solution)/shard_map/ppermute | solution.py:372
  95.0 1.3 collective-permute-start.7
  96.3 0.5 collective-permute-start.6
  96.8 2.0 hold.2.w_ref
  98.9 2.4 %collective-permute-done.8.a3_ref = bf16[512,256]{1,0:T(8,128)(2,1)S(1)} collective-permute-done((bf16[512,256]{1,0:T(8,128)(2,1)S(1)}, bf16[512,256]{1,0:T(8,128)(2,1)S(1)}, u32[]{:S(2)}, u32[]{:S(2)}) %collective-permute-start.8) | collective-permute-done | bytes 262176 | tf_op jit(solution)/shard_map/ppermute | solution.py:372
  101.3 7.5 %collective-permute-done.7.a2_ref = bf16[512,256]{1,0:T(8,128)(2,1)S(1)} collective-permute-done((bf16[512,256]{1,0:T(8,128)(2,1)S(1)}, bf16[512,256]{1,0:T(8,128)(2,1)S(1)}, u32[]{:S(2)}, u32[]{:S(2)}) %collective-permute-start.7) | collective-permute-done | bytes 262176 | tf_op jit(solution)/shard_map/ppermute | solution.py:372
  108.8 0.0 collective-permute-done.6.a1_ref
  108.8 3.9 %merged.2 = (bf16[512,1792]{1,0:T(8,128)(2,1)}, bf16[1024,512]{1,0:T(8,128)(2,1)}) custom-call(s32[4]{0:T(128)S(1)} %pad_add_fusion.side_ref, bf16[512,256]{1,0:T(8,128)(2,1)S(1)} %multiply_convert_fusion.1.a0_ref, bf16[512,256]{1,0:T(8,128)(2,1)S(1)} %collective-permute-done.6.a1_ref, bf16[512,256]{1,0:T(8,128)(2,1)S(1)} %collective-permute-done.7.a2_ref, ...), custom_call_target="tpu_custom_call" | custom-call | flops 1879048192 | bytes 6553600 | tf_op jit(solution)/shard_map/merged/pallas_call | solution.py:284
  112.7 0.0 copy-start
  112.7 2.0 copy-done
  114.7 3.6 %partials.3 = (f32[512,256]{1,0:T(8,128)}, f32[512,256]{1,0:T(8,128)}, bf16[512,256]{1,0:T(8,128)(2,1)}, bf16[512,256]{1,0:T(8,128)(2,1)}, bf16[512,1792]{1,0:T(8,128)(2,1)}) custom-call(s32[4]{0:T(128)S(1)} %pad_add_fusion.side_ref, bf16[512,1792]{1,0:T(8,128)(2,1)S(1)} %bitcast.30, bf16[1024,1792]{1,0:T(8,128)(2,1)S(1)} %bitcast.27), custom_call_target="tpu_custom_call" | custom-call | flops 1879048192 | bytes 6815744 | tf_op jit(solution)/shard_map/partials/pallas_call | solution.py:233
  118.3 7.5 %all-to-all-start.2 = ((bf16[32,16,1792]{2,1,0:T(8,128)(2,1)}), bf16[32,16,1792]{2,1,0:T(8,128)(2,1)S(1)}, u32[]{:S(2)}, u32[]{:S(2)}) async-start(bf16[32,16,1792]{2,1,0:T(8,128)(2,1)} %bitcast.34), calls=%async_computation.2 | async-start | bytes 3670016 | tf_op jit(solution)/shard_map/all_to_all | solution.py:387
  125.8 0.5 collective-permute-start.10
  126.3 1.1 collective-permute-start.9
  127.4 6.4 %collective-permute-done.10 = bf16[512,256]{1,0:T(8,128)(2,1)S(1)} collective-permute-done((bf16[512,256]{1,0:T(8,128)(2,1)}, bf16[512,256]{1,0:T(8,128)(2,1)S(1)}, u32[]{:S(2)}, u32[]{:S(2)}) %collective-permute-start.10) | collective-permute-done | bytes 262176 | tf_op jit(solution)/shard_map/ppermute | solution.py:372
  133.8 1.1 add_convert_fusion.1
  134.9 1.6 collective-permute-start.11
  136.5 7.2 %weight_parts.1 = (bf16[192,1792]{1,0:T(8,128)(2,1)}, bf16[320,1792]{1,0:T(8,128)(2,1)}, bf16[512,1792]{1,0:T(8,128)(2,1)}) custom-call(s32[4]{0:T(128)S(1)} %pad_add_fusion.side_ref, bf16[1024,512]{1,0:T(8,128)(2,1)} %get-tuple-element.73.act_ref, bf16[512,1792]{1,0:T(8,128)(2,1)} %get-tuple-element.74.d_ref), custom_call_target="tpu_custom_call" | custom-call | flops 1879048192 | bytes 6553600 | tf_op jit(solution)/shard_map/weight_parts/pallas_call | solution.py:317
  143.8 0.0 copy-start.10
  143.8 0.0 collective-permute-done.9
  143.8 4.4 %collective-permute-done.11 = bf16[512,256]{1,0:T(8,128)(2,1)S(1)} collective-permute-done((bf16[512,256]{1,0:T(8,128)(2,1)S(1)}, bf16[512,256]{1,0:T(8,128)(2,1)S(1)}, u32[]{:S(2)}, u32[]{:S(2)}) %collective-permute-start.11) | collective-permute-done | bytes 262176 | tf_op jit(solution)/shard_map/ppermute | solution.py:372
  148.2 0.4 multiply_convert_fusion.a0_ref
  148.6 1.2 collective-permute-start.13
  149.7 0.8 collective-permute-start.12
  150.6 4.8 %collective-permute-done.13.a2_ref = bf16[512,256]{1,0:T(8,128)(2,1)S(1)} collective-permute-done((bf16[512,256]{1,0:T(8,128)(2,1)S(1)}, bf16[512,256]{1,0:T(8,128)(2,1)S(1)}, u32[]{:S(2)}, u32[]{:S(2)}) %collective-permute-start.13) | collective-permute-done | bytes 262176 | tf_op jit(solution)/shard_map/ppermute | solution.py:372
  155.4 3.1 %collective-permute-start.15 = (bf16[192,1792]{1,0:T(8,128)(2,1)S(1)}, bf16[192,1792]{1,0:T(8,128)(2,1)S(1)}, u32[]{:S(2)}, u32[]{:S(2)}) collective-permute-start(bf16[192,1792]{1,0:T(8,128)(2,1)S(1)} %copy-done.10), channel_id=1, source_target_pairs={{0,224},{32,192},{64,160},{96,128},{128,96},{160,64},{192,32},{224... | collective-permute-start | bytes 2064392 | tf_op jit(solution)/shard_map/ppermute | solution.py:381
  158.4 7.5 %collective-permute-done.12.a1_ref = bf16[512,256]{1,0:T(8,128)(2,1)S(1)} collective-permute-done((bf16[512,256]{1,0:T(8,128)(2,1)S(1)}, bf16[512,256]{1,0:T(8,128)(2,1)S(1)}, u32[]{:S(2)}, u32[]{:S(2)}) %collective-permute-start.12) | collective-permute-done | bytes 262176 | tf_op jit(solution)/shard_map/ppermute | solution.py:372
  166.0 2.0 hold.3.w_ref
  168.0 3.9 %collective-permute-done.14.a3_ref = bf16[512,256]{1,0:T(8,128)(2,1)S(1)} collective-permute-done((bf16[512,256]{1,0:T(8,128)(2,1)S(1)}, bf16[512,256]{1,0:T(8,128)(2,1)S(1)}, u32[]{:S(2)}, u32[]{:S(2)}) %collective-permute-start.14) | collective-permute-done | bytes 262176 | tf_op jit(solution)/shard_map/ppermute | solution.py:372
  171.9 3.6 %merged.3 = bf16[512,1792]{1,0:T(8,128)(2,1)} custom-call(s32[4]{0:T(128)S(1)} %pad_add_fusion.side_ref, bf16[512,256]{1,0:T(8,128)(2,1)S(1)} %multiply_convert_fusion.a0_ref, bf16[512,256]{1,0:T(8,128)(2,1)S(1)} %collective-permute-done.12.a1_ref, bf16[512,256]{1,0:T(8,128)(2,1)S(1)} %collective-permute-done.13.a2_ref, ...), custom_call_target="tpu_custom_call" | custom-call | flops 1879048192 | bytes 6553600 | tf_op jit(solution)/shard_map/merged/pallas_call | solution.py:284
  175.5 6.9 %collective-permute-done.15 = bf16[192,1792]{1,0:T(8,128)(2,1)S(1)} collective-permute-done((bf16[192,1792]{1,0:T(8,128)(2,1)S(1)}, bf16[192,1792]{1,0:T(8,128)(2,1)S(1)}, u32[]{:S(2)}, u32[]{:S(2)}) %collective-permute-start.15) | collective-permute-done | bytes 688160 | tf_op jit(solution)/shard_map/ppermute | solution.py:381
  182.4 7.8 %all-to-all-start.3 = ((bf16[32,16,1792]{2,1,0:T(8,128)(2,1)}), bf16[32,16,1792]{2,1,0:T(8,128)(2,1)}, u32[]{:S(2)}, u32[]{:S(2)}) async-start(bf16[32,16,1792]{2,1,0:T(8,128)(2,1)} %bitcast.35), calls=%async_computation.3 | async-start | bytes 3670016 | tf_op jit(solution)/shard_map/all_to_all | solution.py:387
  190.2 2.4 collective-permute-start.16
  192.6 1.4 combine.2
  194.0 40.9 %all-to-all-done.3 = bf16[32,16,1792]{2,1,0:T(8,128)(2,1)} async-done(((bf16[32,16,1792]{2,1,0:T(8,128)(2,1)}), bf16[32,16,1792]{2,1,0:T(8,128)(2,1)}, u32[]{:S(2)}, u32[]{:S(2)}) %all-to-all-start.3) | async-done | bytes 1835040 | tf_op jit(solution)/shard_map/all_to_all | solution.py:387
  234.9 2.9 %combine.3 = bf16[256,1792]{1,0:T(8,128)(2,1)} custom-call(bf16[256,512]{1,0:T(8,128)(2,1)S(1)} %get-tuple-element.86.refs_0_, bf16[512,1792]{1,0:T(8,128)(2,1)} %bitcast.22.refs_1_), custom_call_target="tpu_custom_call" | custom-call | flops 469762048 | bytes 2752512 | tf_op jit(solution)/shard_map/combine/pallas_call | solution.py:358
  237.8 2.9 %fusion = bf16[1,512,1792]{2,1,0:T(8,128)(2,1)} fusion(bf16[512,1792]{1,0:T(8,128)(2,1)S(1)} %copy-done.5, bf16[320,1792]{1,0:T(8,128)(2,1)} %collective-permute-done.16, bf16[192,1792]{1,0:T(8,128)(2,1)S(1)} %collective-permute-done.15), kind=kLoop, calls=%fused_computation.1 | loop fusion | flops 6422528 | bytes 5505024 | tf_op jit(solution)/shard_map/broadcast_in_dim | solution.py:454
  (20 shorter events, 0.0 us)
Async XLA Ops:
  4.3 57.9 %all-to-all-start = ((bf16[32,16,1792]{2,1,0:T(8,128)(2,1)}), bf16[32,16,1792]{2,1,0:T(8,128)(2,1)S(1)}, u32[]{:S(2)}, u32[]{:S(2)}) async-start(bf16[32,16,1792]{2,1,0:T(8,128)(2,1)} %bitcast.33), calls=%async_computation | async-start | bytes 3670016 | tf_op jit(solution)/shard_map/all_to_all | solution.py:387
  19.0 2.2 collective-permute-start.1
  19.4 20.3 %collective-permute-start.2 = (bf16[128,1792]{1,0:T(8,128)(2,1)}, bf16[128,1792]{1,0:T(8,128)(2,1)S(1)}, u32[]{:S(2)}, u32[]{:S(2)}) collective-permute-start(bf16[128,1792]{1,0:T(8,128)(2,1)} %get-tuple-element.52), channel_id=1, source_target_pairs={{0,16},{1,17},{2,18},{3,19},{4,20},{5,21},{6,22},{7,23},{8,24},{9,... | collective-permute-start | bytes 1376264 | tf_op jit(solution)/shard_map/ppermute | solution.py:410
  20.9 38.2 %collective-permute-start = (bf16[128,1792]{1,0:T(8,128)(2,1)}, bf16[128,1792]{1,0:T(8,128)(2,1)S(1)}, u32[]{:S(2)}, u32[]{:S(2)}) collective-permute-start(bf16[128,1792]{1,0:T(8,128)(2,1)} %get-tuple-element.49), channel_id=1, source_target_pairs={{0,17},{1,16},{2,19},{3,18},{4,21},{5,20},{6,23},{7,22},{8,25},{9,... | collective-permute-start | bytes 1376264 | tf_op jit(solution)/shard_map/ppermute | solution.py:410
  21.3 18.4 %copy-start.8 = (bf16[128,1792]{1,0:T(8,128)(2,1)}, bf16[128,1792]{1,0:T(8,128)(2,1)S(1)}, u32[]{:S(2)}) copy-start(bf16[128,1792]{1,0:T(8,128)(2,1)S(1)} %collective-permute-done.1) | copy-start | bytes 1376260
  39.7 0.8 copy-start.9
  59.1 0.8 copy-start.7
  62.2 1.2 copy-start.2
  63.5 49.2 %all-to-all-start.1 = ((bf16[8,64,1792]{2,1,0:T(8,128)(2,1)}), bf16[8,64,1792]{2,1,0:T(8,128)(2,1)S(1)}, u32[]{:S(2)}, u32[]{:S(2)}) async-start(bf16[8,64,1792]{2,1,0:T(8,128)(2,1)} %bitcast.32), calls=%async_computation.1 | async-start | bytes 3670016 | tf_op jit(solution)/shard_map/all_to_all | solution.py:387
  68.6 2.0 copy-start.1
  70.6 1.5 copy-start.3
  75.7 9.0 %collective-permute-start.3 = (bf16[512,256]{1,0:T(8,128)(2,1)}, bf16[512,256]{1,0:T(8,128)(2,1)S(1)}, u32[]{:S(2)}, u32[]{:S(2)}) collective-permute-start(bf16[512,256]{1,0:T(8,128)(2,1)} %get-tuple-element.55), channel_id=1, source_target_pairs={{0,32},{32,0},{64,96},{96,64},{128,160},{160,128},{192,224},{224,1... | collective-permute-start | bytes 786440 | tf_op jit(solution)/shard_map/ppermute | solution.py:372
  78.3 7.1 %collective-permute-start.4 = (bf16[512,256]{1,0:T(8,128)(2,1)}, bf16[512,256]{1,0:T(8,128)(2,1)S(1)}, u32[]{:S(2)}, u32[]{:S(2)}) collective-permute-start(bf16[512,256]{1,0:T(8,128)(2,1)} %get-tuple-element.56), channel_id=1, source_target_pairs={{0,64},{32,96},{64,0},{96,32},{128,192},{160,224},{192,128},{224,1... | collective-permute-start | bytes 786440 | tf_op jit(solution)/shard_map/ppermute | solution.py:372
  79.5 11.8 %collective-permute-start.5 = (bf16[512,256]{1,0:T(8,128)(2,1)}, bf16[512,256]{1,0:T(8,128)(2,1)S(1)}, u32[]{:S(2)}, u32[]{:S(2)}) collective-permute-start(bf16[512,256]{1,0:T(8,128)(2,1)} %get-tuple-element.57), channel_id=1, source_target_pairs={{0,96},{32,64},{64,32},{96,0},{128,224},{160,192},{192,160},{224,1... | collective-permute-start | bytes 786440 | tf_op jit(solution)/shard_map/ppermute | solution.py:372
  92.6 8.7 %collective-permute-start.8 = (bf16[512,256]{1,0:T(8,128)(2,1)S(1)}, bf16[512,256]{1,0:T(8,128)(2,1)S(1)}, u32[]{:S(2)}, u32[]{:S(2)}) collective-permute-start(bf16[512,256]{1,0:T(8,128)(2,1)S(1)} %multiply_convert_fusion.1.a0_ref), channel_id=1, source_target_pairs={{0,96},{32,64},{64,32},{96,0},{128,224},{160,192},{192,160},{224,1... | collective-permute-start | bytes 786440 | tf_op jit(solution)/shard_map/ppermute | solution.py:372
  95.0 13.8 %collective-permute-start.7 = (bf16[512,256]{1,0:T(8,128)(2,1)S(1)}, bf16[512,256]{1,0:T(8,128)(2,1)S(1)}, u32[]{:S(2)}, u32[]{:S(2)}) collective-permute-start(bf16[512,256]{1,0:T(8,128)(2,1)S(1)} %multiply_convert_fusion.1.a0_ref), channel_id=1, source_target_pairs={{0,64},{32,96},{64,0},{96,32},{128,192},{160,224},{192,128},{224,1... | collective-permute-start | bytes 786440 | tf_op jit(solution)/shard_map/ppermute | solution.py:372
  96.3 12.5 %collective-permute-start.6 = (bf16[512,256]{1,0:T(8,128)(2,1)S(1)}, bf16[512,256]{1,0:T(8,128)(2,1)S(1)}, u32[]{:S(2)}, u32[]{:S(2)}) collective-permute-start(bf16[512,256]{1,0:T(8,128)(2,1)S(1)} %multiply_convert_fusion.1.a0_ref), channel_id=1, source_target_pairs={{0,32},{32,0},{64,96},{96,64},{128,160},{160,128},{192,224},{224,1... | collective-permute-start | bytes 786440 | tf_op jit(solution)/shard_map/ppermute | solution.py:372
  112.7 2.0 copy-start
  118.3 8.0 %copy-start.11 = (bf16[512,256]{1,0:T(8,128)(2,1)S(1)}, bf16[512,256]{1,0:T(8,128)(2,1)}, u32[]{:S(2)}) copy-start(bf16[512,256]{1,0:T(8,128)(2,1)} %get-tuple-element.70) | copy-start | bytes 786436
  118.3 64.1 %all-to-all-start.2 = ((bf16[32,16,1792]{2,1,0:T(8,128)(2,1)}), bf16[32,16,1792]{2,1,0:T(8,128)(2,1)S(1)}, u32[]{:S(2)}, u32[]{:S(2)}) async-start(bf16[32,16,1792]{2,1,0:T(8,128)(2,1)} %bitcast.34), calls=%async_computation.2 | async-start | bytes 3670016 | tf_op jit(solution)/shard_map/all_to_all | solution.py:387
  125.8 8.0 %collective-permute-start.10 = (bf16[512,256]{1,0:T(8,128)(2,1)}, bf16[512,256]{1,0:T(8,128)(2,1)S(1)}, u32[]{:S(2)}, u32[]{:S(2)}) collective-permute-start(bf16[512,256]{1,0:T(8,128)(2,1)} %get-tuple-element.72), channel_id=1, source_target_pairs={{0,64},{32,96},{64,0},{96,32},{128,192},{160,224},{192,128},{224,1... | collective-permute-start | bytes 786440 | tf_op jit(solution)/shard_map/ppermute | solution.py:372
  126.3 17.5 %collective-permute-start.9 = (bf16[512,256]{1,0:T(8,128)(2,1)S(1)}, bf16[512,256]{1,0:T(8,128)(2,1)S(1)}, u32[]{:S(2)}, u32[]{:S(2)}) collective-permute-start(bf16[512,256]{1,0:T(8,128)(2,1)S(1)} %copy-done.11), channel_id=1, source_target_pairs={{0,64},{32,96},{64,0},{96,32},{128,192},{160,224},{192,128},{224,1... | collective-permute-start | bytes 786440 | tf_op jit(solution)/shard_map/ppermute | solution.py:372
  134.9 13.3 %collective-permute-start.11 = (bf16[512,256]{1,0:T(8,128)(2,1)S(1)}, bf16[512,256]{1,0:T(8,128)(2,1)S(1)}, u32[]{:S(2)}, u32[]{:S(2)}) collective-permute-start(bf16[512,256]{1,0:T(8,128)(2,1)S(1)} %add_convert_fusion.1), channel_id=1, source_target_pairs={{0,32},{32,0},{64,96},{96,64},{128,160},{160,128},{192,224},{224,1... | collective-permute-start | bytes 786440 | tf_op jit(solution)/shard_map/ppermute | solution.py:372
  136.5 11.7 %copy-start.4 = (f32[512,256]{1,0:T(8,128)S(1)}, f32[512,256]{1,0:T(8,128)}, u32[]{:S(2)}) copy-start(f32[512,256]{1,0:T(8,128)} %get-tuple-element.54) | copy-start | bytes 1572868
  136.5 11.7 %copy-start.6 = (f32[512,256]{1,0:T(8,128)S(1)}, f32[512,256]{1,0:T(8,128)}, u32[]{:S(2)}) copy-start(f32[512,256]{1,0:T(8,128)} %get-tuple-element.69) | copy-start | bytes 1572868
  143.8 11.6 %copy-start.10 = (bf16[192,1792]{1,0:T(8,128)(2,1)S(1)}, bf16[192,1792]{1,0:T(8,128)(2,1)}, u32[]{:S(2)}) copy-start(bf16[192,1792]{1,0:T(8,128)(2,1)} %get-tuple-element.82) | copy-start | bytes 2064388
  148.6 6.8 %collective-permute-start.13 = (bf16[512,256]{1,0:T(8,128)(2,1)S(1)}, bf16[512,256]{1,0:T(8,128)(2,1)S(1)}, u32[]{:S(2)}, u32[]{:S(2)}) collective-permute-start(bf16[512,256]{1,0:T(8,128)(2,1)S(1)} %multiply_convert_fusion.a0_ref), channel_id=1, source_target_pairs={{0,64},{32,96},{64,0},{96,32},{128,192},{160,224},{192,128},{224,1... | collective-permute-start | bytes 786440 | tf_op jit(solution)/shard_map/ppermute | solution.py:372
  149.7 16.2 %collective-permute-start.12 = (bf16[512,256]{1,0:T(8,128)(2,1)S(1)}, bf16[512,256]{1,0:T(8,128)(2,1)S(1)}, u32[]{:S(2)}, u32[]{:S(2)}) collective-permute-start(bf16[512,256]{1,0:T(8,128)(2,1)S(1)} %multiply_convert_fusion.a0_ref), channel_id=1, source_target_pairs={{0,32},{32,0},{64,96},{96,64},{128,160},{160,128},{192,224},{224,1... | collective-permute-start | bytes 786440 | tf_op jit(solution)/shard_map/ppermute | solution.py:372
  155.4 27.1 %collective-permute-start.15 = (bf16[192,1792]{1,0:T(8,128)(2,1)S(1)}, bf16[192,1792]{1,0:T(8,128)(2,1)S(1)}, u32[]{:S(2)}, u32[]{:S(2)}) collective-permute-start(bf16[192,1792]{1,0:T(8,128)(2,1)S(1)} %copy-done.10), channel_id=1, source_target_pairs={{0,224},{32,192},{64,160},{96,128},{128,96},{160,64},{192,32},{224... | collective-permute-start | bytes 2064392 | tf_op jit(solution)/shard_map/ppermute | solution.py:381
  165.9 5.9 %collective-permute-start.14 = (bf16[512,256]{1,0:T(8,128)(2,1)S(1)}, bf16[512,256]{1,0:T(8,128)(2,1)S(1)}, u32[]{:S(2)}, u32[]{:S(2)}) collective-permute-start(bf16[512,256]{1,0:T(8,128)(2,1)S(1)} %collective-permute-done.12.a1_ref), channel_id=1, source_target_pairs={{0,64},{32,96},{64,0},{96,32},{128,192},{160,224},{192,128},{224,1... | collective-permute-start | bytes 786440 | tf_op jit(solution)/shard_map/ppermute | solution.py:372
  182.4 52.5 %all-to-all-start.3 = ((bf16[32,16,1792]{2,1,0:T(8,128)(2,1)}), bf16[32,16,1792]{2,1,0:T(8,128)(2,1)}, u32[]{:S(2)}, u32[]{:S(2)}) async-start(bf16[32,16,1792]{2,1,0:T(8,128)(2,1)} %bitcast.35), calls=%async_computation.3 | async-start | bytes 3670016 | tf_op jit(solution)/shard_map/all_to_all | solution.py:387
  190.2 47.6 %collective-permute-start.16 = (bf16[320,1792]{1,0:T(8,128)(2,1)}, bf16[320,1792]{1,0:T(8,128)(2,1)}, u32[]{:S(2)}, u32[]{:S(2)}) collective-permute-start(bf16[320,1792]{1,0:T(8,128)(2,1)} %get-tuple-element.88), channel_id=1, source_target_pairs={{0,224},{32,192},{64,160},{96,128},{128,96},{160,64},{192,32},{224... | collective-permute-start | bytes 3440648 | tf_op jit(solution)/shard_map/ppermute | solution.py:381
  194.0 43.8 %copy-start.5 = (bf16[512,1792]{1,0:T(8,128)(2,1)S(1)}, bf16[512,1792]{1,0:T(8,128)(2,1)}, u32[]{:S(2)}) copy-start(bf16[512,1792]{1,0:T(8,128)(2,1)} %get-tuple-element.90) | copy-start | bytes 5505028

commit v4 on v3

--- a/solution.py
+++ b/solution.py
@@ -297,23 +297,25 @@
     )(side, *pieces, near(w))
 
 
-def weight_kernel(side_ref, act_ref, d_ref, first_ref, rest_ref, own_ref, d_all, sems):
+def weight_kernel(side_ref, act_ref, d_ref, own_ref, *refs):
+    *sent_refs, d_all, sems = refs
     rows, cols = own_ref.shape
-    early = first_ref.shape[0]
     d_out = streamed(d_ref, d_all, sems, cols)
     own = act_ref[pl.ds(pl.multiple_of(side_ref[1] * rows, rows), rows), :]
     other = act_ref[pl.ds(pl.multiple_of((1 - side_ref[1]) * rows, rows), rows), :]
     sent = dot(other, d_out, 1, 0).astype(BF)
-    first_ref[...] = sent[:early]
-    rest_ref[...] = sent[early:]
+    start = 0
+    for ref in sent_refs:
+        ref[...] = sent[start : start + ref.shape[0]]
+        start += ref.shape[0]
     own_ref[...] = dot(own, d_out, 1, 0).astype(BF)
 
 
-def weight_parts(side, acts, d_out, early):
+def weight_parts(side, acts, d_out, eighths):
     hid, rows = acts.shape
     width = d_out.shape[1]
     cols = column_block(width)
-    heights = (early, hid // 2 - early, hid // 2)
+    heights = [hid // 2] + [hid // 16 * part for part in eighths]
     return pl.pallas_call(
         weight_kernel,
         grid=(width // cols,),
@@ -325,6 +327,42 @@
         cost_estimate=cost(2 * rows * width * hid, 2 * (rows * width + width * hid + rows * hid)),
         name="weight_parts",
     )(side, far(acts), far(d_out))
+
+
+def add_kernel(part_ref, own_ref, out_ref, own, sems, *, start, step):
+    rows = part_ref.shape[0]
+    spans = [slice(i, i + step) for i in range(0, rows, step)]
+    targets = [out_ref.at[start + span.start : start + span.stop, :] for span in spans]
+    arriving = [
+        pltpu.make_async_copy(target, own.at[span, :], sems.at[0, i])
+        for i, (span, target) in enumerate(zip(spans, targets))
+    ]
+    for copy in arriving:
+        copy.start()
+    leaving = []
+    for i, (span, target) in enumerate(zip(spans, targets)):
+        arriving[i].wait()
+        own[span, :] = (own[span, :].astype(F32) + part_ref[span, :].astype(F32)).astype(BF)
+        leaving.append(pltpu.make_async_copy(own.at[span, :], target, sems.at[1, i]))
+        leaving[i].start()
+    for copy in leaving:
+        copy.wait()
+
+
+def add_rows(own, part, start):
+    rows, width = part.shape
+    step = 64
+    return pl.pallas_call(
+        functools.partial(add_kernel, start=start, step=step),
+        in_specs=[RESIDENT, FAR],
+        out_specs=FAR,
+        out_shape=pltpu.HBM(own.shape, BF),
+        scratch_shapes=[pltpu.VMEM((rows, width), BF), pltpu.SemaphoreType.DMA((2, rows // step))],
+        input_output_aliases={1: 0},
+        compiler_params=params(),
+        cost_estimate=cost(rows * width, 6 * rows * width),
+        name="add_rows",
+    )(part, far(own))
 
 
 def combine_kernel(*refs, count, kept):
@@ -409,9 +447,8 @@
         flip = j // 2 * (2 * depth) + j % 2
         pieces[j] = lax.ppermute(pieces[j], "expert", [(e, e ^ flip) for e in range(experts)])
     grouped = regroup(side, pieces[:3], depth, (0, 1, 2))
+    grouped, rows_x, pieces[3] = lax.optimization_barrier((grouped, rows_x, pieces[3]))
     grouped = regroup(side, pieces[3:], depth, (3,), grouped).reshape(slots, -1)
-
-    grouped, rows_x = lax.optimization_barrier((grouped, rows_x))
     d_out = exchange(grouped, columns)
     own, *others = partials(side, rows_x, up, False)
     hidden = own + sum(block.astype(F32) for block in to_members(others))
@@ -423,18 +460,15 @@
     result, acts_flipped = merged(side, acts, down_held, False)
     result, d_out = lax.optimization_barrier((result, d_out))
 
+    returned = exchange(result, everyone)
     own, beside, far_off, diagonal, d_out = partials(side, d_out, down, True)
-    result, own, beside, far_off, diagonal, d_out = lax.optimization_barrier(
-        (result, own, beside, far_off, diagonal, d_out)
-    )
-    returned = exchange(result, everyone)
     diagonal = to_member(diagonal, 2)
     far_off = to_member(far_off, 2)
     beside = to_member((beside + diagonal.astype(F32)).astype(BF), 1)
-    first, rest, own_weight = weight_parts(side, acts_flipped, d_out, slots // 8 * 3)
+    own_weight, first, rest, last = weight_parts(side, acts_flipped, d_out, (3, 3, 2))
     d_act = own + far_off.astype(F32) + beside.astype(F32)
     d_hidden = (d_act * sigmoid * (1.0 + hidden * (1.0 - sigmoid))).astype(BF)
-    d_hidden, first, rest, up = lax.optimization_barrier((d_hidden, first, rest, up))
+    d_hidden, first, rest, last, up = lax.optimization_barrier((d_hidden, first, rest, last, up))
     beside = to_member(d_hidden, 1)
     far_off = to_member(d_hidden, 2)
     up_held = hold(up)
@@ -444,13 +478,14 @@
     (d_rows,) = merged(side, d_hiddens, up_held, True)
     d_rows, returned, first = lax.optimization_barrier((d_rows, returned, first))
     returned_dx = exchange(d_rows, everyone)
-    rest = to_mirror(rest)
+    rest, last = to_mirror(rest), to_mirror(last)
 
     layer_out, plain_held = combine(gated_flipped, [returned], plain_flipped)
+    height = first.shape[0]
+    grad_weight = add_rows(add_rows(own_weight, first, 0), rest, height)
     (grad_tokens,) = combine(plain_held, [returned_dx])
-    grad_tokens, rest = lax.optimization_barrier((grad_tokens, rest))
-    arrived = jnp.concatenate([first, rest])
-    grad_weight = (own_weight.astype(F32) + arrived.astype(F32)).astype(BF)
+    grad_tokens, last, grad_weight = lax.optimization_barrier((grad_tokens, last, grad_weight))
+    grad_weight = add_rows(grad_weight, last, height + rest.shape[0])
     return (layer_out, grad_tokens, grad_weight[None])
 
 

time: 242 us -> 238 us (0.983)
  waiting for transfers between devices: 130 us -> 120 us
  Pallas kernels: 42.6 us -> 48.2 us
  other arithmetic: 5.73 us -> 2.79 us
  starting transfers between devices: 52.7 us -> 55.5 us
    all_to_all x4, waiting for transfers between devices: 40.9 us -> 9.44 us  [exchange(): lax.all_to_all(blocks, 'expert', split_axis=0, concat_axis=0, tiled=True,...]
    ppermute x2 -> x3, waiting for transfers between devices: 6.9 us -> 32.9 us  [to_mirror(): lax.ppermute(block, 'pipe', [(p, count - 1 - p) for p in range(count)])]
    pallas_call x0 -> x3, Pallas kernels: none -> 5.75 us  [add_rows(): pl.pallas_call(functools.partial(add_kernel, start=start, step=step), in_...]
    ppermute x12, waiting for transfers between devices: 48.3 us -> 43.1 us  [to_member(): return lax.ppermute(block, 'pipe', [(p, p ^ flip) for p in range(count)])]
    broadcast_in_dim x1 -> x0, other arithmetic: 2.94 us -> none  [shards(): return (layer_out, grad_tokens, grad_weight[None])]
    ppermute x2 -> x3, starting transfers between devices: 5.44 us -> 7.49 us  [to_mirror(): lax.ppermute(block, 'pipe', [(p, count - 1 - p) for p in range(count)])]
  transfers between devices with their start and end apart: 21 -> 22, of which waited for: 14 -> 16; matrix products, arithmetic and copies ran while one was open for 1% -> 1% of each run, Pallas kernels for 15% -> 17%
where the time goes in v4:
time: 238 us; the launch traced here: 236 us
  waiting for transfers between devices  120 us (50%)
  starting transfers between devices  55.5 us (23%)
  Pallas kernels  48.2 us (20%)
  local copies, waits for them, and re-layouts  9.1 us (4%)
  other arithmetic  2.79 us (1%)
    ppermute x12, waiting for transfers between devices, to_member(): return lax.ppermute(block, 'pipe', [(p, p ^ flip) for p in range(count)])  43.1 us
    ppermute x3, waiting for transfers between devices, shards(): lax.ppermute(pieces[j], 'expert', [(e, e ^ flip) for e in range(experts)])  34.3 us
    ppermute x3, waiting for transfers between devices, to_mirror(): lax.ppermute(block, 'pipe', [(p, count - 1 - p) for p in range(count)])  32.9 us
    all_to_all x4, starting transfers between devices, exchange(): lax.all_to_all(blocks, 'expert', split_axis=0, concat_axis=0, tiled=True,...  32.6 us
    ppermute x12, starting transfers between devices, to_member(): return lax.ppermute(block, 'pipe', [(p, p ^ flip) for p in range(count)])  13.1 us
    all_to_all x4, waiting for transfers between devices, exchange(): lax.all_to_all(blocks, 'expert', split_axis=0, concat_axis=0, tiled=True,...  9.44 us
    unnamed x24, local copies, waits for them, and re-layouts  9.1 us
    pallas_call x2, Pallas kernels, merged(): pl.pallas_call(functools.partial(merge_kernel, transposed=transposed), in...  7.54 us
  transfers between devices with their start and end apart: 22, of which 16 were waited for; matrix products, arithmetic and copies ran while one was open for 1% of the time, Pallas kernels for 17%

profile of v4, /device:TPU:1, one launch (start us, length us, event | category | flops | bytes accessed | tf_op | source)
XLA Modules:
  0.0 236.5 jit_solution(10631384726439124920)
XLA Ops:
  0.7 0.1 pad_add_fusion.side_ref
  0.7 3.5 %dispatch.3 = bf16[512,1792]{1,0:T(8,128)(2,1)} custom-call(s32[4]{0:T(128)S(1)} %pad_add_fusion.side_ref, s32[8,256]{1,0:T(8,128)} %bitcast.39, s32[8,256]{1,0:T(8,128)} %bitcast.41, bf16[8,256]{1,0:T(8,128)(2,1)} %bitcast.43, bf16[8,256]{1,0:T(8,128)(2,1)} %bitcast.45, bf16[256,1792]{1,0:T(8,128)(2,1)} %x_ref.3), custom_call_target="tpu_custom_call" | custom-call | flops 469762048 | bytes 2752512 | tf_op jit(solution)/shard_map/dispatch/pallas_call | solution.py:133
  4.3 11.1 %all-to-all-start = ((bf16[32,16,1792]{2,1,0:T(8,128)(2,1)}), bf16[32,16,1792]{2,1,0:T(8,128)(2,1)S(1)}, u32[]{:S(2)}, u32[]{:S(2)}) async-start(bf16[32,16,1792]{2,1,0:T(8,128)(2,1)} %bitcast.32), calls=%async_computation | async-start | bytes 3670016 | tf_op jit(solution)/shard_map/all_to_all | solution.py:425
  15.3 3.7 %dispatch.2 = (bf16[128,1792]{1,0:T(8,128)(2,1)}, bf16[128,1792]{1,0:T(8,128)(2,1)}, bf16[128,1792]{1,0:T(8,128)(2,1)}, bf16[128,1792]{1,0:T(8,128)(2,1)}, bf16[...) custom-call(s32[4]{0:T(128)S(1)} %pad_add_fusion.side_ref, s32[8,256]{1,0:T(8,128)} %bitcast.40, s32[8,256]{1,0:T(8,128)} %bitcast.42, ...), custom_call_target="tpu_custom_call" | custom-call | flops 469762048 | bytes 2752512 | tf_op jit(solution)/shard_map/dispatch/pallas_call | solution.py:133
  19.1 0.3 collective-permute-start
  19.4 1.5 collective-permute-start.1
  20.9 0.4 collective-permute-start.2
  21.3 18.4 %collective-permute-done.1 = bf16[128,1792]{1,0:T(8,128)(2,1)S(1)} collective-permute-done((bf16[128,1792]{1,0:T(8,128)(2,1)}, bf16[128,1792]{1,0:T(8,128)(2,1)S(1)}, u32[]{:S(2)}, u32[]{:S(2)}) %collective-permute-start.1) | collective-permute-done | bytes 458784 | tf_op jit(solution)/shard_map/ppermute | solution.py:448
  39.7 0.8 copy-done.10
  40.5 2.7 %regroup.2.refs_1_ = bf16[8,4,16,1792]{3,2,1,0:T(8,128)(2,1)} custom-call(s32[4]{0:T(128)S(1)} %pad_add_fusion.side_ref, bf16[8,16,1792]{2,1,0:T(8,128)(2,1)} %bitcast.36, bf16[8,16,1792]{2,1,0:T(8,128)(2,1)} %bitcast.37, bf16[8,16,1792]{2,1,0:T(8,128)(2,1)} %bitcast.38), custom_call_target="tpu_custom_call" | custom-call | bytes 2752512 | tf_op jit(solution)/shard_map/regroup/pallas_call | solution.py:171
  43.2 15.9 %collective-permute-done.2 = bf16[128,1792]{1,0:T(8,128)(2,1)S(1)} collective-permute-done((bf16[128,1792]{1,0:T(8,128)(2,1)}, bf16[128,1792]{1,0:T(8,128)(2,1)S(1)}, u32[]{:S(2)}, u32[]{:S(2)}) %collective-permute-start.2) | collective-permute-done | bytes 458784 | tf_op jit(solution)/shard_map/ppermute | solution.py:448
  59.1 0.9 all-to-all-done
  60.0 2.4 %regroup.3 = bf16[8,4,16,1792]{3,2,1,0:T(8,128)(2,1)} custom-call(s32[4]{0:T(128)S(1)} %pad_add_fusion.side_ref, bf16[8,16,1792]{2,1,0:T(8,128)(2,1)} %bitcast.35, bf16[8,4,16,1792]{3,2,1,0:T(8,128)(2,1)} %regroup.2.refs_1_), custom_call_target="tpu_custom_call", output_to_operand_aliasing={{}: (2, {})} | custom-call | bytes 917504 | tf_op jit(solution)/shard_map/regroup/pallas_call | solution.py:171
  62.4 4.9 %all-to-all-start.1 = ((bf16[8,64,1792]{2,1,0:T(8,128)(2,1)}), bf16[8,64,1792]{2,1,0:T(8,128)(2,1)S(1)}, u32[]{:S(2)}, u32[]{:S(2)}) async-start(bf16[8,64,1792]{2,1,0:T(8,128)(2,1)} %bitcast.30), calls=%async_computation.1 | async-start | bytes 3670016 | tf_op jit(solution)/shard_map/all_to_all | solution.py:425
  67.4 2.0 copy-done.1
  69.4 1.5 copy-done.5
  70.9 3.6 %partials.2 = (f32[512,256]{1,0:T(8,128)}, bf16[512,256]{1,0:T(8,128)(2,1)}, bf16[512,256]{1,0:T(8,128)(2,1)}, bf16[512,256]{1,0:T(8,128)(2,1)}) custom-call(s32[4]{0:T(128)S(1)} %pad_add_fusion.side_ref, bf16[512,1792]{1,0:T(8,128)(2,1)S(1)} %bitcast.29, bf16[1792,1024]{1,0:T(8,128)(2,1)S(1)} %bitcast.27), custom_call_target="tpu_custom_call" | custom-call | flops 1879048192 | bytes 6815744 | tf_op jit(solution)/shard_map/partials/pallas_call | solution.py:233
  74.5 2.5 %collective-permute-start.3 = (bf16[512,256]{1,0:T(8,128)(2,1)}, bf16[512,256]{1,0:T(8,128)(2,1)S(1)}, u32[]{:S(2)}, u32[]{:S(2)}) collective-permute-start(bf16[512,256]{1,0:T(8,128)(2,1)} %get-tuple-element.53), channel_id=1, source_target_pairs={{0,32},{32,0},{64,96},{96,64},{128,160},{160,128},{192,224},{224,1... | collective-permute-start | bytes 786440 | tf_op jit(solution)/shard_map/ppermute | solution.py:410
  77.1 1.3 collective-permute-start.4
  78.4 0.4 collective-permute-start.5
  78.8 4.8 %collective-permute-done.3 = bf16[512,256]{1,0:T(8,128)(2,1)S(1)} collective-permute-done((bf16[512,256]{1,0:T(8,128)(2,1)}, bf16[512,256]{1,0:T(8,128)(2,1)S(1)}, u32[]{:S(2)}, u32[]{:S(2)}) %collective-permute-start.3) | collective-permute-done | bytes 262176 | tf_op jit(solution)/shard_map/ppermute | solution.py:410
  83.5 0.6 collective-permute-done.4
  84.2 6.0 %collective-permute-done.5 = bf16[512,256]{1,0:T(8,128)(2,1)S(1)} collective-permute-done((bf16[512,256]{1,0:T(8,128)(2,1)}, bf16[512,256]{1,0:T(8,128)(2,1)S(1)}, u32[]{:S(2)}, u32[]{:S(2)}) %collective-permute-start.5) | collective-permute-done | bytes 262176 | tf_op jit(solution)/shard_map/ppermute | solution.py:410
  90.2 1.3 multiply_convert_fusion.1.a0_ref
  91.5 2.4 %collective-permute-start.8 = (bf16[512,256]{1,0:T(8,128)(2,1)S(1)}, bf16[512,256]{1,0:T(8,128)(2,1)S(1)}, u32[]{:S(2)}, u32[]{:S(2)}) collective-permute-start(bf16[512,256]{1,0:T(8,128)(2,1)S(1)} %multiply_convert_fusion.1.a0_ref), channel_id=1, source_target_pairs={{0,96},{32,64},{64,32},{96,0},{128,224},{160,192},{192,160},{224,1... | collective-permute-start | bytes 786440 | tf_op jit(solution)/shard_map/ppermute | solution.py:410
  93.9 1.3 collective-permute-start.7
  95.2 0.5 collective-permute-start.6
  95.7 2.0 hold.2.w_ref
  97.7 2.5 %collective-permute-done.8.a3_ref = bf16[512,256]{1,0:T(8,128)(2,1)S(1)} collective-permute-done((bf16[512,256]{1,0:T(8,128)(2,1)S(1)}, bf16[512,256]{1,0:T(8,128)(2,1)S(1)}, u32[]{:S(2)}, u32[]{:S(2)}) %collective-permute-start.8) | collective-permute-done | bytes 262176 | tf_op jit(solution)/shard_map/ppermute | solution.py:410
  100.2 7.4 %collective-permute-done.7.a2_ref = bf16[512,256]{1,0:T(8,128)(2,1)S(1)} collective-permute-done((bf16[512,256]{1,0:T(8,128)(2,1)S(1)}, bf16[512,256]{1,0:T(8,128)(2,1)S(1)}, u32[]{:S(2)}, u32[]{:S(2)}) %collective-permute-start.7) | collective-permute-done | bytes 262176 | tf_op jit(solution)/shard_map/ppermute | solution.py:410
  107.7 3.9 %merged.2 = (bf16[512,1792]{1,0:T(8,128)(2,1)}, bf16[1024,512]{1,0:T(8,128)(2,1)}) custom-call(s32[4]{0:T(128)S(1)} %pad_add_fusion.side_ref, bf16[512,256]{1,0:T(8,128)(2,1)S(1)} %multiply_convert_fusion.1.a0_ref, bf16[512,256]{1,0:T(8,128)(2,1)S(1)} %collective-permute-done.6.a1_ref, bf16[512,256]{1,0:T(8,128)(2,1)S(1)} %collective-permute-done.7.a2_ref, ...), custom_call_target="tpu_custom_call" | custom-call | flops 1879048192 | bytes 6553600 | tf_op jit(solution)/shard_map/merged/pallas_call | solution.py:284
  111.6 1.2 copy-done.2
  112.8 7.4 %all-to-all-start.2 = ((bf16[32,16,1792]{2,1,0:T(8,128)(2,1)}), bf16[32,16,1792]{2,1,0:T(8,128)(2,1)S(1)}, u32[]{:S(2)}, u32[]{:S(2)}) async-start(bf16[32,16,1792]{2,1,0:T(8,128)(2,1)} %bitcast.33), calls=%async_computation.2 | async-start | bytes 3670016 | tf_op jit(solution)/shard_map/all_to_all | solution.py:425
  120.2 0.0 copy-start
  120.2 2.0 copy-done
  122.2 1.5 copy-done.3
  123.7 3.6 %partials.3 = (f32[512,256]{1,0:T(8,128)}, f32[512,256]{1,0:T(8,128)}, bf16[512,256]{1,0:T(8,128)(2,1)}, bf16[512,256]{1,0:T(8,128)(2,1)}, bf16[512,1792]{1,0:T(8,128)(2,1)}) custom-call(s32[4]{0:T(128)S(1)} %pad_add_fusion.side_ref, bf16[512,1792]{1,0:T(8,128)(2,1)S(1)} %bitcast.28, bf16[1024,1792]{1,0:T(8,128)(2,1)S(1)} %bitcast.25), custom_call_target="tpu_custom_call" | custom-call | flops 1879048192 | bytes 6815744 | tf_op jit(solution)/shard_map/partials/pallas_call | solution.py:233
  127.3 0.5 collective-permute-start.10
  127.7 1.1 collective-permute-start.9
  128.8 6.2 %collective-permute-done.10 = bf16[512,256]{1,0:T(8,128)(2,1)S(1)} collective-permute-done((bf16[512,256]{1,0:T(8,128)(2,1)}, bf16[512,256]{1,0:T(8,128)(2,1)S(1)}, u32[]{:S(2)}, u32[]{:S(2)}) %collective-permute-start.10) | collective-permute-done | bytes 262176 | tf_op jit(solution)/shard_map/ppermute | solution.py:410
  135.1 1.1 add_convert_fusion
  136.2 1.6 collective-permute-start.11
  137.8 7.0 %weight_parts.1 = (bf16[512,1792]{1,0:T(8,128)(2,1)}, bf16[192,1792]{1,0:T(8,128)(2,1)}, bf16[192,1792]{1,0:T(8,128)(2,1)}, bf16[128,1792]{1,0:T(8,128)(2,1)}) custom-call(s32[4]{0:T(128)S(1)} %pad_add_fusion.side_ref, bf16[1024,512]{1,0:T(8,128)(2,1)} %get-tuple-element.66.act_ref, bf16[512,1792]{1,0:T(8,128)(2,1)} %get-tuple-element.67.d_ref), custom_call_target="tpu_custom_call" | custom-call | flops 1879048192 | bytes 6553600 | tf_op jit(solution)/shard_map/weight_parts/pallas_call | solution.py:319
  144.8 1.2 collective-permute-done.11
  146.0 0.4 multiply_convert_fusion.a0_ref
  146.4 1.5 collective-permute-start.13
  147.8 0.0 collective-permute-start.12
  147.9 4.1 %collective-permute-done.13.a2_ref = bf16[512,256]{1,0:T(8,128)(2,1)S(1)} collective-permute-done((bf16[512,256]{1,0:T(8,128)(2,1)S(1)}, bf16[512,256]{1,0:T(8,128)(2,1)S(1)}, u32[]{:S(2)}, u32[]{:S(2)}) %collective-permute-start.13) | collective-permute-done | bytes 262176 | tf_op jit(solution)/shard_map/ppermute | solution.py:410
  152.0 2.3 collective-permute-start.15
  154.3 6.8 %collective-permute-done.12.a1_ref = bf16[512,256]{1,0:T(8,128)(2,1)S(1)} collective-permute-done((bf16[512,256]{1,0:T(8,128)(2,1)S(1)}, bf16[512,256]{1,0:T(8,128)(2,1)S(1)}, u32[]{:S(2)}, u32[]{:S(2)}) %collective-permute-start.12) | collective-permute-done | bytes 262176 | tf_op jit(solution)/shard_map/ppermute | solution.py:410
  161.1 2.0 hold.3.w_ref
  163.1 3.5 %collective-permute-done.14.a3_ref = bf16[512,256]{1,0:T(8,128)(2,1)S(1)} collective-permute-done((bf16[512,256]{1,0:T(8,128)(2,1)S(1)}, bf16[512,256]{1,0:T(8,128)(2,1)S(1)}, u32[]{:S(2)}, u32[]{:S(2)}) %collective-permute-start.14) | collective-permute-done | bytes 262176 | tf_op jit(solution)/shard_map/ppermute | solution.py:410
  166.6 3.6 %merged.3 = bf16[512,1792]{1,0:T(8,128)(2,1)} custom-call(s32[4]{0:T(128)S(1)} %pad_add_fusion.side_ref, bf16[512,256]{1,0:T(8,128)(2,1)S(1)} %multiply_convert_fusion.a0_ref, bf16[512,256]{1,0:T(8,128)(2,1)S(1)} %collective-permute-done.12.a1_ref, bf16[512,256]{1,0:T(8,128)(2,1)S(1)} %collective-permute-done.13.a2_ref, ...), custom_call_target="tpu_custom_call" | custom-call | flops 1879048192 | bytes 6553600 | tf_op jit(solution)/shard_map/merged/pallas_call | solution.py:284
  170.2 7.3 %collective-permute-done.15.part_ref = bf16[192,1792]{1,0:T(8,128)(2,1)S(1)} collective-permute-done((bf16[192,1792]{1,0:T(8,128)(2,1)S(1)}, bf16[192,1792]{1,0:T(8,128)(2,1)S(1)}, u32[]{:S(2)}, u32[]{:S(2)}) %collective-permute-start.15) | collective-permute-done | bytes 688160 | tf_op jit(solution)/shard_map/ppermute | solution.py:419
  177.6 9.3 %all-to-all-start.3 = ((bf16[32,16,1792]{2,1,0:T(8,128)(2,1)}), bf16[32,16,1792]{2,1,0:T(8,128)(2,1)}, u32[]{:S(2)}, u32[]{:S(2)}) async-start(bf16[32,16,1792]{2,1,0:T(8,128)(2,1)} %bitcast.34), calls=%async_computation.3 | async-start | bytes 3670016 | tf_op jit(solution)/shard_map/all_to_all | solution.py:425
  186.9 2.4 %collective-permute-start.17 = (bf16[192,1792]{1,0:T(8,128)(2,1)}, bf16[192,1792]{1,0:T(8,128)(2,1)S(1)}, u32[]{:S(2)}, u32[]{:S(2)}) collective-permute-start(bf16[192,1792]{1,0:T(8,128)(2,1)} %get-tuple-element.83), channel_id=1, source_target_pairs={{0,224},{32,192},{64,160},{96,128},{128,96},{160,64},{192,32},{224... | collective-permute-start | bytes 2064392 | tf_op jit(solution)/shard_map/ppermute | solution.py:419
  189.3 2.8 %collective-permute-start.16 = (bf16[128,1792]{1,0:T(8,128)(2,1)}, bf16[128,1792]{1,0:T(8,128)(2,1)S(1)}, u32[]{:S(2)}, u32[]{:S(2)}) collective-permute-start(bf16[128,1792]{1,0:T(8,128)(2,1)} %get-tuple-element.82), channel_id=1, source_target_pairs={{0,224},{32,192},{64,160},{96,128},{128,96},{160,64},{192,32},{224... | collective-permute-start | bytes 1376264 | tf_op jit(solution)/shard_map/ppermute | solution.py:419
  192.1 2.0 add_rows.3.own_ref
  194.0 25.6 %collective-permute-done.17.part_ref = bf16[192,1792]{1,0:T(8,128)(2,1)S(1)} collective-permute-done((bf16[192,1792]{1,0:T(8,128)(2,1)}, bf16[192,1792]{1,0:T(8,128)(2,1)S(1)}, u32[]{:S(2)}, u32[]{:S(2)}) %collective-permute-start.17) | collective-permute-done | bytes 688160 | tf_op jit(solution)/shard_map/ppermute | solution.py:419
  219.6 1.9 add_rows.4.own_ref
  221.6 1.4 combine.2
  223.0 8.6 %all-to-all-done.3 = bf16[32,16,1792]{2,1,0:T(8,128)(2,1)} async-done(((bf16[32,16,1792]{2,1,0:T(8,128)(2,1)}), bf16[32,16,1792]{2,1,0:T(8,128)(2,1)}, u32[]{:S(2)}, u32[]{:S(2)}) %all-to-all-start.3) | async-done | bytes 1835040 | tf_op jit(solution)/shard_map/all_to_all | solution.py:425
  231.6 2.9 %combine.3 = bf16[256,1792]{1,0:T(8,128)(2,1)} custom-call(bf16[256,512]{1,0:T(8,128)(2,1)S(1)} %get-tuple-element.80.refs_0_, bf16[512,1792]{1,0:T(8,128)(2,1)} %bitcast.21.refs_1_), custom_call_target="tpu_custom_call" | custom-call | flops 469762048 | bytes 2752512 | tf_op jit(solution)/shard_map/combine/pallas_call | solution.py:396
  234.5 1.8 add_rows.5
  (24 shorter events, 0.1 us)
Async XLA Ops:
  4.3 55.7 %all-to-all-start = ((bf16[32,16,1792]{2,1,0:T(8,128)(2,1)}), bf16[32,16,1792]{2,1,0:T(8,128)(2,1)S(1)}, u32[]{:S(2)}, u32[]{:S(2)}) async-start(bf16[32,16,1792]{2,1,0:T(8,128)(2,1)} %bitcast.32), calls=%async_computation | async-start | bytes 3670016 | tf_op jit(solution)/shard_map/all_to_all | solution.py:425
  19.1 2.2 collective-permute-start
  19.4 20.4 %collective-permute-start.1 = (bf16[128,1792]{1,0:T(8,128)(2,1)}, bf16[128,1792]{1,0:T(8,128)(2,1)S(1)}, u32[]{:S(2)}, u32[]{:S(2)}) collective-permute-start(bf16[128,1792]{1,0:T(8,128)(2,1)} %get-tuple-element.49), channel_id=1, source_target_pairs={{0,16},{1,17},{2,18},{3,19},{4,20},{5,21},{6,22},{7,23},{8,24},{9,... | collective-permute-start | bytes 1376264 | tf_op jit(solution)/shard_map/ppermute | solution.py:448
  20.9 38.2 %collective-permute-start.2 = (bf16[128,1792]{1,0:T(8,128)(2,1)}, bf16[128,1792]{1,0:T(8,128)(2,1)S(1)}, u32[]{:S(2)}, u32[]{:S(2)}) collective-permute-start(bf16[128,1792]{1,0:T(8,128)(2,1)} %get-tuple-element.50), channel_id=1, source_target_pairs={{0,17},{1,16},{2,19},{3,18},{4,21},{5,20},{6,23},{7,22},{8,25},{9,... | collective-permute-start | bytes 1376264 | tf_op jit(solution)/shard_map/ppermute | solution.py:448
  21.3 18.5 %copy-start.9 = (bf16[128,1792]{1,0:T(8,128)(2,1)}, bf16[128,1792]{1,0:T(8,128)(2,1)S(1)}, u32[]{:S(2)}) copy-start(bf16[128,1792]{1,0:T(8,128)(2,1)S(1)} %collective-permute-done) | copy-start | bytes 1376260
  39.7 0.8 copy-start.10
  59.1 0.9 copy-start.8
  60.0 2.5 %copy-start.4 = (bf16[32,16,1792]{2,1,0:T(8,128)(2,1)}, bf16[32,16,1792]{2,1,0:T(8,128)(2,1)S(1)}, u32[]{:S(2)}) copy-start(bf16[32,16,1792]{2,1,0:T(8,128)(2,1)S(1)} %all-to-all-done) | copy-start | bytes 5505028
  62.4 49.1 %all-to-all-start.1 = ((bf16[8,64,1792]{2,1,0:T(8,128)(2,1)}), bf16[8,64,1792]{2,1,0:T(8,128)(2,1)S(1)}, u32[]{:S(2)}, u32[]{:S(2)}) async-start(bf16[8,64,1792]{2,1,0:T(8,128)(2,1)} %bitcast.30), calls=%async_computation.1 | async-start | bytes 3670016 | tf_op jit(solution)/shard_map/all_to_all | solution.py:425
  67.4 2.0 copy-start.1
  69.4 1.5 copy-start.5
  74.5 9.0 %collective-permute-start.3 = (bf16[512,256]{1,0:T(8,128)(2,1)}, bf16[512,256]{1,0:T(8,128)(2,1)S(1)}, u32[]{:S(2)}, u32[]{:S(2)}) collective-permute-start(bf16[512,256]{1,0:T(8,128)(2,1)} %get-tuple-element.53), channel_id=1, source_target_pairs={{0,32},{32,0},{64,96},{96,64},{128,160},{160,128},{192,224},{224,1... | collective-permute-start | bytes 786440 | tf_op jit(solution)/shard_map/ppermute | solution.py:410
  77.1 7.1 %collective-permute-start.4 = (bf16[512,256]{1,0:T(8,128)(2,1)}, bf16[512,256]{1,0:T(8,128)(2,1)S(1)}, u32[]{:S(2)}, u32[]{:S(2)}) collective-permute-start(bf16[512,256]{1,0:T(8,128)(2,1)} %get-tuple-element.54), channel_id=1, source_target_pairs={{0,64},{32,96},{64,0},{96,32},{128,192},{160,224},{192,128},{224,1... | collective-permute-start | bytes 786440 | tf_op jit(solution)/shard_map/ppermute | solution.py:410
  78.4 11.8 %collective-permute-start.5 = (bf16[512,256]{1,0:T(8,128)(2,1)}, bf16[512,256]{1,0:T(8,128)(2,1)S(1)}, u32[]{:S(2)}, u32[]{:S(2)}) collective-permute-start(bf16[512,256]{1,0:T(8,128)(2,1)} %get-tuple-element.55), channel_id=1, source_target_pairs={{0,96},{32,64},{64,32},{96,0},{128,224},{160,192},{192,160},{224,1... | collective-permute-start | bytes 786440 | tf_op jit(solution)/shard_map/ppermute | solution.py:410
  91.5 8.8 %collective-permute-start.8 = (bf16[512,256]{1,0:T(8,128)(2,1)S(1)}, bf16[512,256]{1,0:T(8,128)(2,1)S(1)}, u32[]{:S(2)}, u32[]{:S(2)}) collective-permute-start(bf16[512,256]{1,0:T(8,128)(2,1)S(1)} %multiply_convert_fusion.1.a0_ref), channel_id=1, source_target_pairs={{0,96},{32,64},{64,32},{96,0},{128,224},{160,192},{192,160},{224,1... | collective-permute-start | bytes 786440 | tf_op jit(solution)/shard_map/ppermute | solution.py:410
  93.9 13.8 %collective-permute-start.7 = (bf16[512,256]{1,0:T(8,128)(2,1)S(1)}, bf16[512,256]{1,0:T(8,128)(2,1)S(1)}, u32[]{:S(2)}, u32[]{:S(2)}) collective-permute-start(bf16[512,256]{1,0:T(8,128)(2,1)S(1)} %multiply_convert_fusion.1.a0_ref), channel_id=1, source_target_pairs={{0,64},{32,96},{64,0},{96,32},{128,192},{160,224},{192,128},{224,1... | collective-permute-start | bytes 786440 | tf_op jit(solution)/shard_map/ppermute | solution.py:410
  95.2 12.5 %collective-permute-start.6 = (bf16[512,256]{1,0:T(8,128)(2,1)S(1)}, bf16[512,256]{1,0:T(8,128)(2,1)S(1)}, u32[]{:S(2)}, u32[]{:S(2)}) collective-permute-start(bf16[512,256]{1,0:T(8,128)(2,1)S(1)} %multiply_convert_fusion.1.a0_ref), channel_id=1, source_target_pairs={{0,32},{32,0},{64,96},{96,64},{128,160},{160,128},{192,224},{224,1... | collective-permute-start | bytes 786440 | tf_op jit(solution)/shard_map/ppermute | solution.py:410
  111.6 1.2 copy-start.2
  112.8 64.8 %all-to-all-start.2 = ((bf16[32,16,1792]{2,1,0:T(8,128)(2,1)}), bf16[32,16,1792]{2,1,0:T(8,128)(2,1)S(1)}, u32[]{:S(2)}, u32[]{:S(2)}) async-start(bf16[32,16,1792]{2,1,0:T(8,128)(2,1)} %bitcast.33), calls=%async_computation.2 | async-start | bytes 3670016 | tf_op jit(solution)/shard_map/all_to_all | solution.py:425
  120.2 2.0 copy-start
  122.2 1.5 copy-start.3
  127.3 7.8 %collective-permute-start.10 = (bf16[512,256]{1,0:T(8,128)(2,1)}, bf16[512,256]{1,0:T(8,128)(2,1)S(1)}, u32[]{:S(2)}, u32[]{:S(2)}) collective-permute-start(bf16[512,256]{1,0:T(8,128)(2,1)} %get-tuple-element.65), channel_id=1, source_target_pairs={{0,64},{32,96},{64,0},{96,32},{128,192},{160,224},{192,128},{224,1... | collective-permute-start | bytes 786440 | tf_op jit(solution)/shard_map/ppermute | solution.py:410
  127.7 17.1 %collective-permute-start.9 = (bf16[512,256]{1,0:T(8,128)(2,1)}, bf16[512,256]{1,0:T(8,128)(2,1)S(1)}, u32[]{:S(2)}, u32[]{:S(2)}) collective-permute-start(bf16[512,256]{1,0:T(8,128)(2,1)} %get-tuple-element.63), channel_id=1, source_target_pairs={{0,64},{32,96},{64,0},{96,32},{128,192},{160,224},{192,128},{224,1... | collective-permute-start | bytes 786440 | tf_op jit(solution)/shard_map/ppermute | solution.py:410
  136.2 9.8 %collective-permute-start.11 = (bf16[512,256]{1,0:T(8,128)(2,1)S(1)}, bf16[512,256]{1,0:T(8,128)(2,1)S(1)}, u32[]{:S(2)}, u32[]{:S(2)}) collective-permute-start(bf16[512,256]{1,0:T(8,128)(2,1)S(1)} %add_convert_fusion), channel_id=1, source_target_pairs={{0,32},{32,0},{64,96},{96,64},{128,160},{160,128},{192,224},{224,1... | collective-permute-start | bytes 786440 | tf_op jit(solution)/shard_map/ppermute | solution.py:410
  137.8 8.2 %copy-start.6 = (f32[512,256]{1,0:T(8,128)S(1)}, f32[512,256]{1,0:T(8,128)}, u32[]{:S(2)}) copy-start(f32[512,256]{1,0:T(8,128)} %get-tuple-element.52) | copy-start | bytes 1572868
  137.8 8.2 %copy-start.7 = (f32[512,256]{1,0:T(8,128)S(1)}, f32[512,256]{1,0:T(8,128)}, u32[]{:S(2)}) copy-start(f32[512,256]{1,0:T(8,128)} %get-tuple-element.62) | copy-start | bytes 1572868
  144.8 7.2 %copy-start.11 = (bf16[192,1792]{1,0:T(8,128)(2,1)S(1)}, bf16[192,1792]{1,0:T(8,128)(2,1)}, u32[]{:S(2)}) copy-start(bf16[192,1792]{1,0:T(8,128)(2,1)} %get-tuple-element.76) | copy-start | bytes 2064388
  146.4 5.6 %collective-permute-start.13 = (bf16[512,256]{1,0:T(8,128)(2,1)S(1)}, bf16[512,256]{1,0:T(8,128)(2,1)S(1)}, u32[]{:S(2)}, u32[]{:S(2)}) collective-permute-start(bf16[512,256]{1,0:T(8,128)(2,1)S(1)} %multiply_convert_fusion.a0_ref), channel_id=1, source_target_pairs={{0,64},{32,96},{64,0},{96,32},{128,192},{160,224},{192,128},{224,1... | collective-permute-start | bytes 786440 | tf_op jit(solution)/shard_map/ppermute | solution.py:410
  147.8 13.2 %collective-permute-start.12 = (bf16[512,256]{1,0:T(8,128)(2,1)S(1)}, bf16[512,256]{1,0:T(8,128)(2,1)S(1)}, u32[]{:S(2)}, u32[]{:S(2)}) collective-permute-start(bf16[512,256]{1,0:T(8,128)(2,1)S(1)} %multiply_convert_fusion.a0_ref), channel_id=1, source_target_pairs={{0,32},{32,0},{64,96},{96,64},{128,160},{160,128},{192,224},{224,1... | collective-permute-start | bytes 786440 | tf_op jit(solution)/shard_map/ppermute | solution.py:410
  152.0 25.6 %collective-permute-start.15 = (bf16[192,1792]{1,0:T(8,128)(2,1)S(1)}, bf16[192,1792]{1,0:T(8,128)(2,1)S(1)}, u32[]{:S(2)}, u32[]{:S(2)}) collective-permute-start(bf16[192,1792]{1,0:T(8,128)(2,1)S(1)} %copy-done.11), channel_id=1, source_target_pairs={{0,224},{32,192},{64,160},{96,128},{128,96},{160,64},{192,32},{224... | collective-permute-start | bytes 2064392 | tf_op jit(solution)/shard_map/ppermute | solution.py:419
  161.1 5.5 %collective-permute-start.14 = (bf16[512,256]{1,0:T(8,128)(2,1)S(1)}, bf16[512,256]{1,0:T(8,128)(2,1)S(1)}, u32[]{:S(2)}, u32[]{:S(2)}) collective-permute-start(bf16[512,256]{1,0:T(8,128)(2,1)S(1)} %collective-permute-done.12.a1_ref), channel_id=1, source_target_pairs={{0,64},{32,96},{64,0},{96,32},{128,192},{160,224},{192,128},{224,1... | collective-permute-start | bytes 786440 | tf_op jit(solution)/shard_map/ppermute | solution.py:410
  177.6 54.0 %all-to-all-start.3 = ((bf16[32,16,1792]{2,1,0:T(8,128)(2,1)}), bf16[32,16,1792]{2,1,0:T(8,128)(2,1)}, u32[]{:S(2)}, u32[]{:S(2)}) async-start(bf16[32,16,1792]{2,1,0:T(8,128)(2,1)} %bitcast.34), calls=%async_computation.3 | async-start | bytes 3670016 | tf_op jit(solution)/shard_map/all_to_all | solution.py:425
  186.9 32.7 %collective-permute-start.17 = (bf16[192,1792]{1,0:T(8,128)(2,1)}, bf16[192,1792]{1,0:T(8,128)(2,1)S(1)}, u32[]{:S(2)}, u32[]{:S(2)}) collective-permute-start(bf16[192,1792]{1,0:T(8,128)(2,1)} %get-tuple-element.83), channel_id=1, source_target_pairs={{0,224},{32,192},{64,160},{96,128},{128,96},{160,64},{192,32},{224... | collective-permute-start | bytes 2064392 | tf_op jit(solution)/shard_map/ppermute | solution.py:419
  189.3 45.2 %collective-permute-start.16 = (bf16[128,1792]{1,0:T(8,128)(2,1)}, bf16[128,1792]{1,0:T(8,128)(2,1)S(1)}, u32[]{:S(2)}, u32[]{:S(2)}) collective-permute-start(bf16[128,1792]{1,0:T(8,128)(2,1)} %get-tuple-element.82), channel_id=1, source_target_pairs={{0,224},{32,192},{64,160},{96,128},{128,96},{160,64},{192,32},{224... | collective-permute-start | bytes 1376264 | tf_op jit(solution)/shard_map/ppermute | solution.py:419

commit v5 on v4

--- a/solution.py
+++ b/solution.py
@@ -151,14 +151,20 @@
 
 def regroup_kernel(side_ref, *refs, members):
     pieces, (out_ref, held, sems) = refs[: len(members)], refs[-3:]
-    arriving = [pltpu.make_async_copy(ref, held.at[i], sems.at[i]) for i, ref in enumerate(pieces)]
-    leaving = []
-    for copy in arriving:
-        copy.start()
-    for i, (j, copy) in enumerate(zip(members, arriving)):
-        place = (side_ref[2] ^ (j // 2)) * 2 + (side_ref[3] ^ (j % 2))
-        copy.wait()
-        leaving.append(pltpu.make_async_copy(held.at[i], out_ref.at[:, place], sems.at[len(members) + i]))
+    depth = held.shape[1]
+    cuts = [slice(z, z + depth // 4) for z in range(0, depth, depth // 4)]
+    arriving, leaving = [], []
+    for i, ref in enumerate(pieces):
+        for cut in cuts:
+            copy = pltpu.make_async_copy(ref.at[cut], held.at[i, cut], sems.at[0, len(arriving)])
+            copy.start()
+            arriving.append((i, cut, copy))
+    for i, cut, copy in arriving:
+        place = (side_ref[2] ^ (members[i] // 2)) * 2 + (side_ref[3] ^ (members[i] % 2))
+        copy.wait()
+        leaving.append(
+            pltpu.make_async_copy(held.at[i, cut], out_ref.at[cut, place], sems.at[1, len(leaving)])
+        )
         leaving[-1].start()
     for copy in leaving:
         copy.wait()
@@ -175,7 +181,7 @@
         out_shape=pltpu.HBM((depth, 4, CAP, width), BF),
         scratch_shapes=[
             pltpu.VMEM((len(members), depth, CAP, width), BF),
-            pltpu.SemaphoreType.DMA((2 * len(members),)),
+            pltpu.SemaphoreType.DMA((2, 4 * len(members))),
         ],
         input_output_aliases={1 + len(pieces): 0} if more else {},
         compiler_params=params(),
@@ -351,7 +357,7 @@
 
 def add_rows(own, part, start):
     rows, width = part.shape
-    step = 64
+    step = 32
     return pl.pallas_call(
         functools.partial(add_kernel, start=start, step=step),
         in_specs=[RESIDENT, FAR],

time: 238 us -> 238 us (level)
  no operation moved by 1% of the time
where the time goes in v5:
time: 238 us; the launch traced here: 236 us
  waiting for transfers between devices  120 us (50%)
  starting transfers between devices  55.4 us (23%)
  Pallas kernels  48.3 us (20%)
  local copies, waits for them, and re-layouts  9.1 us (4%)
  other arithmetic  2.79 us (1%)
    ppermute x12, waiting for transfers between devices, to_member(): return lax.ppermute(block, 'pipe', [(p, p ^ flip) for p in range(count)])  43.5 us
    ppermute x3, waiting for transfers between devices, shards(): lax.ppermute(pieces[j], 'expert', [(e, e ^ flip) for e in range(experts)])  34.2 us
    ppermute x3, waiting for transfers between devices, to_mirror(): lax.ppermute(block, 'pipe', [(p, count - 1 - p) for p in range(count)])  32.6 us
    all_to_all x4, starting transfers between devices, exchange(): lax.all_to_all(blocks, 'expert', split_axis=0, concat_axis=0, tiled=True,...  32.3 us
    ppermute x12, starting transfers between devices, to_member(): return lax.ppermute(block, 'pipe', [(p, p ^ flip) for p in range(count)])  13.4 us
    all_to_all x4, waiting for transfers between devices, exchange(): lax.all_to_all(blocks, 'expert', split_axis=0, concat_axis=0, tiled=True,...  9.48 us
    unnamed x24, local copies, waits for them, and re-layouts  9.1 us
    pallas_call x2, Pallas kernels, merged(): pl.pallas_call(functools.partial(merge_kernel, transposed=transposed), in...  7.54 us
  transfers between devices with their start and end apart: 22, of which 16 were waited for; matrix products, arithmetic and copies ran while one was open for 1% of the time, Pallas kernels for 17%

profile of v5, /device:TPU:1, one launch (start us, length us, event | category | flops | bytes accessed | tf_op | source)
XLA Modules:
  0.0 236.4 jit_solution(9955913800018395316)
XLA Ops:
  0.7 0.1 pad_add_fusion.side_ref
  0.7 3.5 %dispatch.3 = bf16[512,1792]{1,0:T(8,128)(2,1)} custom-call(s32[4]{0:T(128)S(1)} %pad_add_fusion.side_ref, s32[8,256]{1,0:T(8,128)} %bitcast.39, s32[8,256]{1,0:T(8,128)} %bitcast.41, bf16[8,256]{1,0:T(8,128)(2,1)} %bitcast.43, bf16[8,256]{1,0:T(8,128)(2,1)} %bitcast.45, bf16[256,1792]{1,0:T(8,128)(2,1)} %x_ref.3), custom_call_target="tpu_custom_call" | custom-call | flops 469762048 | bytes 2752512 | tf_op jit(solution)/shard_map/dispatch/pallas_call | solution.py:133
  4.3 11.1 %all-to-all-start = ((bf16[32,16,1792]{2,1,0:T(8,128)(2,1)}), bf16[32,16,1792]{2,1,0:T(8,128)(2,1)S(1)}, u32[]{:S(2)}, u32[]{:S(2)}) async-start(bf16[32,16,1792]{2,1,0:T(8,128)(2,1)} %bitcast.32), calls=%async_computation | async-start | bytes 3670016 | tf_op jit(solution)/shard_map/all_to_all | solution.py:431
  15.3 3.7 %dispatch.2 = (bf16[128,1792]{1,0:T(8,128)(2,1)}, bf16[128,1792]{1,0:T(8,128)(2,1)}, bf16[128,1792]{1,0:T(8,128)(2,1)}, bf16[128,1792]{1,0:T(8,128)(2,1)}, bf16[...) custom-call(s32[4]{0:T(128)S(1)} %pad_add_fusion.side_ref, s32[8,256]{1,0:T(8,128)} %bitcast.40, s32[8,256]{1,0:T(8,128)} %bitcast.42, ...), custom_call_target="tpu_custom_call" | custom-call | flops 469762048 | bytes 2752512 | tf_op jit(solution)/shard_map/dispatch/pallas_call | solution.py:133
  19.1 0.3 collective-permute-start
  19.4 1.5 collective-permute-start.1
  20.9 0.4 collective-permute-start.2
  21.3 18.4 %collective-permute-done.1 = bf16[128,1792]{1,0:T(8,128)(2,1)S(1)} collective-permute-done((bf16[128,1792]{1,0:T(8,128)(2,1)}, bf16[128,1792]{1,0:T(8,128)(2,1)S(1)}, u32[]{:S(2)}, u32[]{:S(2)}) %collective-permute-start.1) | collective-permute-done | bytes 458784 | tf_op jit(solution)/shard_map/ppermute | solution.py:454
  39.7 0.8 copy-done.10
  40.5 2.8 %regroup.2.refs_1_ = bf16[8,4,16,1792]{3,2,1,0:T(8,128)(2,1)} custom-call(s32[4]{0:T(128)S(1)} %pad_add_fusion.side_ref, bf16[8,16,1792]{2,1,0:T(8,128)(2,1)} %bitcast.36, bf16[8,16,1792]{2,1,0:T(8,128)(2,1)} %bitcast.37, bf16[8,16,1792]{2,1,0:T(8,128)(2,1)} %bitcast.38), custom_call_target="tpu_custom_call" | custom-call | bytes 2752512 | tf_op jit(solution)/shard_map/regroup/pallas_call | solution.py:177
  43.4 15.7 %collective-permute-done.2 = bf16[128,1792]{1,0:T(8,128)(2,1)S(1)} collective-permute-done((bf16[128,1792]{1,0:T(8,128)(2,1)}, bf16[128,1792]{1,0:T(8,128)(2,1)S(1)}, u32[]{:S(2)}, u32[]{:S(2)}) %collective-permute-start.2) | collective-permute-done | bytes 458784 | tf_op jit(solution)/shard_map/ppermute | solution.py:454
  59.1 0.9 all-to-all-done
  60.0 2.4 %regroup.3 = bf16[8,4,16,1792]{3,2,1,0:T(8,128)(2,1)} custom-call(s32[4]{0:T(128)S(1)} %pad_add_fusion.side_ref, bf16[8,16,1792]{2,1,0:T(8,128)(2,1)} %bitcast.35, bf16[8,4,16,1792]{3,2,1,0:T(8,128)(2,1)} %regroup.2.refs_1_), custom_call_target="tpu_custom_call", output_to_operand_aliasing={{}: (2, {})} | custom-call | bytes 917504 | tf_op jit(solution)/shard_map/regroup/pallas_call | solution.py:177
  62.4 4.9 %all-to-all-start.1 = ((bf16[8,64,1792]{2,1,0:T(8,128)(2,1)}), bf16[8,64,1792]{2,1,0:T(8,128)(2,1)S(1)}, u32[]{:S(2)}, u32[]{:S(2)}) async-start(bf16[8,64,1792]{2,1,0:T(8,128)(2,1)} %bitcast.30), calls=%async_computation.1 | async-start | bytes 3670016 | tf_op jit(solution)/shard_map/all_to_all | solution.py:431
  67.3 2.0 copy-done.1
  69.4 1.5 copy-done.5
  70.9 3.6 %partials.2 = (f32[512,256]{1,0:T(8,128)}, bf16[512,256]{1,0:T(8,128)(2,1)}, bf16[512,256]{1,0:T(8,128)(2,1)}, bf16[512,256]{1,0:T(8,128)(2,1)}) custom-call(s32[4]{0:T(128)S(1)} %pad_add_fusion.side_ref, bf16[512,1792]{1,0:T(8,128)(2,1)S(1)} %bitcast.29, bf16[1792,1024]{1,0:T(8,128)(2,1)S(1)} %bitcast.27), custom_call_target="tpu_custom_call" | custom-call | flops 1879048192 | bytes 6815744 | tf_op jit(solution)/shard_map/partials/pallas_call | solution.py:239
  74.5 2.5 %collective-permute-start.3 = (bf16[512,256]{1,0:T(8,128)(2,1)}, bf16[512,256]{1,0:T(8,128)(2,1)S(1)}, u32[]{:S(2)}, u32[]{:S(2)}) collective-permute-start(bf16[512,256]{1,0:T(8,128)(2,1)} %get-tuple-element.53), channel_id=1, source_target_pairs={{0,32},{32,0},{64,96},{96,64},{128,160},{160,128},{192,224},{224,1... | collective-permute-start | bytes 786440 | tf_op jit(solution)/shard_map/ppermute | solution.py:416
  77.0 1.3 collective-permute-start.4
  78.3 0.4 collective-permute-start.5
  78.7 4.7 %collective-permute-done.3 = bf16[512,256]{1,0:T(8,128)(2,1)S(1)} collective-permute-done((bf16[512,256]{1,0:T(8,128)(2,1)}, bf16[512,256]{1,0:T(8,128)(2,1)S(1)}, u32[]{:S(2)}, u32[]{:S(2)}) %collective-permute-start.3) | collective-permute-done | bytes 262176 | tf_op jit(solution)/shard_map/ppermute | solution.py:416
  83.5 0.6 collective-permute-done.4
  84.1 6.0 %collective-permute-done.5 = bf16[512,256]{1,0:T(8,128)(2,1)S(1)} collective-permute-done((bf16[512,256]{1,0:T(8,128)(2,1)}, bf16[512,256]{1,0:T(8,128)(2,1)S(1)}, u32[]{:S(2)}, u32[]{:S(2)}) %collective-permute-start.5) | collective-permute-done | bytes 262176 | tf_op jit(solution)/shard_map/ppermute | solution.py:416
  90.1 1.3 multiply_convert_fusion.1.a0_ref
  91.4 2.4 %collective-permute-start.8 = (bf16[512,256]{1,0:T(8,128)(2,1)S(1)}, bf16[512,256]{1,0:T(8,128)(2,1)S(1)}, u32[]{:S(2)}, u32[]{:S(2)}) collective-permute-start(bf16[512,256]{1,0:T(8,128)(2,1)S(1)} %multiply_convert_fusion.1.a0_ref), channel_id=1, source_target_pairs={{0,96},{32,64},{64,32},{96,0},{128,224},{160,192},{192,160},{224,1... | collective-permute-start | bytes 786440 | tf_op jit(solution)/shard_map/ppermute | solution.py:416
  93.8 1.3 collective-permute-start.7
  95.1 0.5 collective-permute-start.6
  95.6 2.0 hold.2.w_ref
  97.7 2.5 %collective-permute-done.8.a3_ref = bf16[512,256]{1,0:T(8,128)(2,1)S(1)} collective-permute-done((bf16[512,256]{1,0:T(8,128)(2,1)S(1)}, bf16[512,256]{1,0:T(8,128)(2,1)S(1)}, u32[]{:S(2)}, u32[]{:S(2)}) %collective-permute-start.8) | collective-permute-done | bytes 262176 | tf_op jit(solution)/shard_map/ppermute | solution.py:416
  100.2 7.4 %collective-permute-done.7.a2_ref = bf16[512,256]{1,0:T(8,128)(2,1)S(1)} collective-permute-done((bf16[512,256]{1,0:T(8,128)(2,1)S(1)}, bf16[512,256]{1,0:T(8,128)(2,1)S(1)}, u32[]{:S(2)}, u32[]{:S(2)}) %collective-permute-start.7) | collective-permute-done | bytes 262176 | tf_op jit(solution)/shard_map/ppermute | solution.py:416
  107.6 3.9 %merged.2 = (bf16[512,1792]{1,0:T(8,128)(2,1)}, bf16[1024,512]{1,0:T(8,128)(2,1)}) custom-call(s32[4]{0:T(128)S(1)} %pad_add_fusion.side_ref, bf16[512,256]{1,0:T(8,128)(2,1)S(1)} %multiply_convert_fusion.1.a0_ref, bf16[512,256]{1,0:T(8,128)(2,1)S(1)} %collective-permute-done.6.a1_ref, bf16[512,256]{1,0:T(8,128)(2,1)S(1)} %collective-permute-done.7.a2_ref, ...), custom_call_target="tpu_custom_call" | custom-call | flops 1879048192 | bytes 6553600 | tf_op jit(solution)/shard_map/merged/pallas_call | solution.py:290
  111.5 0.0 copy-start.2
  111.5 1.2 copy-done.2
  112.7 7.3 %all-to-all-start.2 = ((bf16[32,16,1792]{2,1,0:T(8,128)(2,1)}), bf16[32,16,1792]{2,1,0:T(8,128)(2,1)S(1)}, u32[]{:S(2)}, u32[]{:S(2)}) async-start(bf16[32,16,1792]{2,1,0:T(8,128)(2,1)} %bitcast.33), calls=%async_computation.2 | async-start | bytes 3670016 | tf_op jit(solution)/shard_map/all_to_all | solution.py:431
  120.1 2.0 copy-done
  122.1 1.5 copy-done.3
  123.6 3.6 %partials.3 = (f32[512,256]{1,0:T(8,128)}, f32[512,256]{1,0:T(8,128)}, bf16[512,256]{1,0:T(8,128)(2,1)}, bf16[512,256]{1,0:T(8,128)(2,1)}, bf16[512,1792]{1,0:T(8,128)(2,1)}) custom-call(s32[4]{0:T(128)S(1)} %pad_add_fusion.side_ref, bf16[512,1792]{1,0:T(8,128)(2,1)S(1)} %bitcast.28, bf16[1024,1792]{1,0:T(8,128)(2,1)S(1)} %bitcast.25), custom_call_target="tpu_custom_call" | custom-call | flops 1879048192 | bytes 6815744 | tf_op jit(solution)/shard_map/partials/pallas_call | solution.py:239
  127.2 0.5 collective-permute-start.10
  127.7 1.1 collective-permute-start.9
  128.8 6.4 %collective-permute-done.10 = bf16[512,256]{1,0:T(8,128)(2,1)S(1)} collective-permute-done((bf16[512,256]{1,0:T(8,128)(2,1)}, bf16[512,256]{1,0:T(8,128)(2,1)S(1)}, u32[]{:S(2)}, u32[]{:S(2)}) %collective-permute-start.10) | collective-permute-done | bytes 262176 | tf_op jit(solution)/shard_map/ppermute | solution.py:416
  135.2 1.1 add_convert_fusion
  136.3 1.6 collective-permute-start.11
  137.9 7.0 %weight_parts.1 = (bf16[512,1792]{1,0:T(8,128)(2,1)}, bf16[192,1792]{1,0:T(8,128)(2,1)}, bf16[192,1792]{1,0:T(8,128)(2,1)}, bf16[128,1792]{1,0:T(8,128)(2,1)}) custom-call(s32[4]{0:T(128)S(1)} %pad_add_fusion.side_ref, bf16[1024,512]{1,0:T(8,128)(2,1)} %get-tuple-element.66.act_ref, bf16[512,1792]{1,0:T(8,128)(2,1)} %get-tuple-element.67.d_ref), custom_call_target="tpu_custom_call" | custom-call | flops 1879048192 | bytes 6553600 | tf_op jit(solution)/shard_map/weight_parts/pallas_call | solution.py:325
  145.0 1.2 collective-permute-done.11
  146.2 0.4 multiply_convert_fusion.a0_ref
  146.5 1.7 collective-permute-start.13
  148.2 4.2 %collective-permute-done.13.a2_ref = bf16[512,256]{1,0:T(8,128)(2,1)S(1)} collective-permute-done((bf16[512,256]{1,0:T(8,128)(2,1)S(1)}, bf16[512,256]{1,0:T(8,128)(2,1)S(1)}, u32[]{:S(2)}, u32[]{:S(2)}) %collective-permute-start.13) | collective-permute-done | bytes 262176 | tf_op jit(solution)/shard_map/ppermute | solution.py:416
  152.4 2.3 collective-permute-start.15
  154.7 7.0 %collective-permute-done.12.a1_ref = bf16[512,256]{1,0:T(8,128)(2,1)S(1)} collective-permute-done((bf16[512,256]{1,0:T(8,128)(2,1)S(1)}, bf16[512,256]{1,0:T(8,128)(2,1)S(1)}, u32[]{:S(2)}, u32[]{:S(2)}) %collective-permute-start.12) | collective-permute-done | bytes 262176 | tf_op jit(solution)/shard_map/ppermute | solution.py:416
  161.7 0.1 collective-permute-start.14
  161.7 2.0 hold.3.w_ref
  163.8 3.4 %collective-permute-done.14.a3_ref = bf16[512,256]{1,0:T(8,128)(2,1)S(1)} collective-permute-done((bf16[512,256]{1,0:T(8,128)(2,1)S(1)}, bf16[512,256]{1,0:T(8,128)(2,1)S(1)}, u32[]{:S(2)}, u32[]{:S(2)}) %collective-permute-start.14) | collective-permute-done | bytes 262176 | tf_op jit(solution)/shard_map/ppermute | solution.py:416
  167.2 3.6 %merged.3 = bf16[512,1792]{1,0:T(8,128)(2,1)} custom-call(s32[4]{0:T(128)S(1)} %pad_add_fusion.side_ref, bf16[512,256]{1,0:T(8,128)(2,1)S(1)} %multiply_convert_fusion.a0_ref, bf16[512,256]{1,0:T(8,128)(2,1)S(1)} %collective-permute-done.12.a1_ref, bf16[512,256]{1,0:T(8,128)(2,1)S(1)} %collective-permute-done.13.a2_ref, ...), custom_call_target="tpu_custom_call" | custom-call | flops 1879048192 | bytes 6553600 | tf_op jit(solution)/shard_map/merged/pallas_call | solution.py:290
  170.8 7.0 %collective-permute-done.15.part_ref = bf16[192,1792]{1,0:T(8,128)(2,1)S(1)} collective-permute-done((bf16[192,1792]{1,0:T(8,128)(2,1)S(1)}, bf16[192,1792]{1,0:T(8,128)(2,1)S(1)}, u32[]{:S(2)}, u32[]{:S(2)}) %collective-permute-start.15) | collective-permute-done | bytes 688160 | tf_op jit(solution)/shard_map/ppermute | solution.py:425
  177.8 9.0 %all-to-all-start.3 = ((bf16[32,16,1792]{2,1,0:T(8,128)(2,1)}), bf16[32,16,1792]{2,1,0:T(8,128)(2,1)}, u32[]{:S(2)}, u32[]{:S(2)}) async-start(bf16[32,16,1792]{2,1,0:T(8,128)(2,1)} %bitcast.34), calls=%async_computation.3 | async-start | bytes 3670016 | tf_op jit(solution)/shard_map/all_to_all | solution.py:431
  186.8 2.4 %collective-permute-start.17 = (bf16[192,1792]{1,0:T(8,128)(2,1)}, bf16[192,1792]{1,0:T(8,128)(2,1)S(1)}, u32[]{:S(2)}, u32[]{:S(2)}) collective-permute-start(bf16[192,1792]{1,0:T(8,128)(2,1)} %get-tuple-element.83), channel_id=1, source_target_pairs={{0,224},{32,192},{64,160},{96,128},{128,96},{160,64},{192,32},{224... | collective-permute-start | bytes 2064392 | tf_op jit(solution)/shard_map/ppermute | solution.py:425
  189.2 2.8 %collective-permute-start.16 = (bf16[128,1792]{1,0:T(8,128)(2,1)}, bf16[128,1792]{1,0:T(8,128)(2,1)S(1)}, u32[]{:S(2)}, u32[]{:S(2)}) collective-permute-start(bf16[128,1792]{1,0:T(8,128)(2,1)} %get-tuple-element.82), channel_id=1, source_target_pairs={{0,224},{32,192},{64,160},{96,128},{128,96},{160,64},{192,32},{224... | collective-permute-start | bytes 1376264 | tf_op jit(solution)/shard_map/ppermute | solution.py:425
  192.0 2.0 add_rows.3.own_ref
  194.0 25.6 %collective-permute-done.17.part_ref = bf16[192,1792]{1,0:T(8,128)(2,1)S(1)} collective-permute-done((bf16[192,1792]{1,0:T(8,128)(2,1)}, bf16[192,1792]{1,0:T(8,128)(2,1)S(1)}, u32[]{:S(2)}, u32[]{:S(2)}) %collective-permute-start.17) | collective-permute-done | bytes 688160 | tf_op jit(solution)/shard_map/ppermute | solution.py:425
  219.5 2.0 add_rows.4.own_ref
  221.5 1.4 combine.2
  222.9 8.6 %all-to-all-done.3 = bf16[32,16,1792]{2,1,0:T(8,128)(2,1)} async-done(((bf16[32,16,1792]{2,1,0:T(8,128)(2,1)}), bf16[32,16,1792]{2,1,0:T(8,128)(2,1)}, u32[]{:S(2)}, u32[]{:S(2)}) %all-to-all-start.3) | async-done | bytes 1835040 | tf_op jit(solution)/shard_map/all_to_all | solution.py:431
  231.5 2.9 %combine.3 = bf16[256,1792]{1,0:T(8,128)(2,1)} custom-call(bf16[256,512]{1,0:T(8,128)(2,1)S(1)} %get-tuple-element.80.refs_0_, bf16[512,1792]{1,0:T(8,128)(2,1)} %bitcast.21.refs_1_), custom_call_target="tpu_custom_call" | custom-call | flops 469762048 | bytes 2752512 | tf_op jit(solution)/shard_map/combine/pallas_call | solution.py:402
  234.5 1.8 add_rows.5
  (24 shorter events, 0.1 us)
Async XLA Ops:
  4.3 55.7 %all-to-all-start = ((bf16[32,16,1792]{2,1,0:T(8,128)(2,1)}), bf16[32,16,1792]{2,1,0:T(8,128)(2,1)S(1)}, u32[]{:S(2)}, u32[]{:S(2)}) async-start(bf16[32,16,1792]{2,1,0:T(8,128)(2,1)} %bitcast.32), calls=%async_computation | async-start | bytes 3670016 | tf_op jit(solution)/shard_map/all_to_all | solution.py:431
  19.1 2.2 collective-permute-start
  19.4 20.4 %collective-permute-start.1 = (bf16[128,1792]{1,0:T(8,128)(2,1)}, bf16[128,1792]{1,0:T(8,128)(2,1)S(1)}, u32[]{:S(2)}, u32[]{:S(2)}) collective-permute-start(bf16[128,1792]{1,0:T(8,128)(2,1)} %get-tuple-element.49), channel_id=1, source_target_pairs={{0,16},{1,17},{2,18},{3,19},{4,20},{5,21},{6,22},{7,23},{8,24},{9,... | collective-permute-start | bytes 1376264 | tf_op jit(solution)/shard_map/ppermute | solution.py:454
  20.9 38.2 %collective-permute-start.2 = (bf16[128,1792]{1,0:T(8,128)(2,1)}, bf16[128,1792]{1,0:T(8,128)(2,1)S(1)}, u32[]{:S(2)}, u32[]{:S(2)}) collective-permute-start(bf16[128,1792]{1,0:T(8,128)(2,1)} %get-tuple-element.50), channel_id=1, source_target_pairs={{0,17},{1,16},{2,19},{3,18},{4,21},{5,20},{6,23},{7,22},{8,25},{9,... | collective-permute-start | bytes 1376264 | tf_op jit(solution)/shard_map/ppermute | solution.py:454
  21.3 18.5 %copy-start.9 = (bf16[128,1792]{1,0:T(8,128)(2,1)}, bf16[128,1792]{1,0:T(8,128)(2,1)S(1)}, u32[]{:S(2)}) copy-start(bf16[128,1792]{1,0:T(8,128)(2,1)S(1)} %collective-permute-done) | copy-start | bytes 1376260
  39.7 0.8 copy-start.10
  59.1 0.9 copy-start.8
  60.0 2.4 %copy-start.4 = (bf16[32,16,1792]{2,1,0:T(8,128)(2,1)}, bf16[32,16,1792]{2,1,0:T(8,128)(2,1)S(1)}, u32[]{:S(2)}) copy-start(bf16[32,16,1792]{2,1,0:T(8,128)(2,1)S(1)} %all-to-all-done) | copy-start | bytes 5505028
  62.4 49.1 %all-to-all-start.1 = ((bf16[8,64,1792]{2,1,0:T(8,128)(2,1)}), bf16[8,64,1792]{2,1,0:T(8,128)(2,1)S(1)}, u32[]{:S(2)}, u32[]{:S(2)}) async-start(bf16[8,64,1792]{2,1,0:T(8,128)(2,1)} %bitcast.30), calls=%async_computation.1 | async-start | bytes 3670016 | tf_op jit(solution)/shard_map/all_to_all | solution.py:431
  67.3 2.0 copy-start.1
  69.4 1.5 copy-start.5
  74.5 9.0 %collective-permute-start.3 = (bf16[512,256]{1,0:T(8,128)(2,1)}, bf16[512,256]{1,0:T(8,128)(2,1)S(1)}, u32[]{:S(2)}, u32[]{:S(2)}) collective-permute-start(bf16[512,256]{1,0:T(8,128)(2,1)} %get-tuple-element.53), channel_id=1, source_target_pairs={{0,32},{32,0},{64,96},{96,64},{128,160},{160,128},{192,224},{224,1... | collective-permute-start | bytes 786440 | tf_op jit(solution)/shard_map/ppermute | solution.py:416
  77.0 7.1 %collective-permute-start.4 = (bf16[512,256]{1,0:T(8,128)(2,1)}, bf16[512,256]{1,0:T(8,128)(2,1)S(1)}, u32[]{:S(2)}, u32[]{:S(2)}) collective-permute-start(bf16[512,256]{1,0:T(8,128)(2,1)} %get-tuple-element.54), channel_id=1, source_target_pairs={{0,64},{32,96},{64,0},{96,32},{128,192},{160,224},{192,128},{224,1... | collective-permute-start | bytes 786440 | tf_op jit(solution)/shard_map/ppermute | solution.py:416
  78.3 11.8 %collective-permute-start.5 = (bf16[512,256]{1,0:T(8,128)(2,1)}, bf16[512,256]{1,0:T(8,128)(2,1)S(1)}, u32[]{:S(2)}, u32[]{:S(2)}) collective-permute-start(bf16[512,256]{1,0:T(8,128)(2,1)} %get-tuple-element.55), channel_id=1, source_target_pairs={{0,96},{32,64},{64,32},{96,0},{128,224},{160,192},{192,160},{224,1... | collective-permute-start | bytes 786440 | tf_op jit(solution)/shard_map/ppermute | solution.py:416
  91.4 8.8 %collective-permute-start.8 = (bf16[512,256]{1,0:T(8,128)(2,1)S(1)}, bf16[512,256]{1,0:T(8,128)(2,1)S(1)}, u32[]{:S(2)}, u32[]{:S(2)}) collective-permute-start(bf16[512,256]{1,0:T(8,128)(2,1)S(1)} %multiply_convert_fusion.1.a0_ref), channel_id=1, source_target_pairs={{0,96},{32,64},{64,32},{96,0},{128,224},{160,192},{192,160},{224,1... | collective-permute-start | bytes 786440 | tf_op jit(solution)/shard_map/ppermute | solution.py:416
  93.8 13.8 %collective-permute-start.7 = (bf16[512,256]{1,0:T(8,128)(2,1)S(1)}, bf16[512,256]{1,0:T(8,128)(2,1)S(1)}, u32[]{:S(2)}, u32[]{:S(2)}) collective-permute-start(bf16[512,256]{1,0:T(8,128)(2,1)S(1)} %multiply_convert_fusion.1.a0_ref), channel_id=1, source_target_pairs={{0,64},{32,96},{64,0},{96,32},{128,192},{160,224},{192,128},{224,1... | collective-permute-start | bytes 786440 | tf_op jit(solution)/shard_map/ppermute | solution.py:416
  95.1 12.5 %collective-permute-start.6 = (bf16[512,256]{1,0:T(8,128)(2,1)S(1)}, bf16[512,256]{1,0:T(8,128)(2,1)S(1)}, u32[]{:S(2)}, u32[]{:S(2)}) collective-permute-start(bf16[512,256]{1,0:T(8,128)(2,1)S(1)} %multiply_convert_fusion.1.a0_ref), channel_id=1, source_target_pairs={{0,32},{32,0},{64,96},{96,64},{128,160},{160,128},{192,224},{224,1... | collective-permute-start | bytes 786440 | tf_op jit(solution)/shard_map/ppermute | solution.py:416
  111.5 1.2 copy-start.2
  112.7 65.1 %all-to-all-start.2 = ((bf16[32,16,1792]{2,1,0:T(8,128)(2,1)}), bf16[32,16,1792]{2,1,0:T(8,128)(2,1)S(1)}, u32[]{:S(2)}, u32[]{:S(2)}) async-start(bf16[32,16,1792]{2,1,0:T(8,128)(2,1)} %bitcast.33), calls=%async_computation.2 | async-start | bytes 3670016 | tf_op jit(solution)/shard_map/all_to_all | solution.py:431
  120.1 2.0 copy-start
  122.1 1.5 copy-start.3
  127.2 8.0 %collective-permute-start.10 = (bf16[512,256]{1,0:T(8,128)(2,1)}, bf16[512,256]{1,0:T(8,128)(2,1)S(1)}, u32[]{:S(2)}, u32[]{:S(2)}) collective-permute-start(bf16[512,256]{1,0:T(8,128)(2,1)} %get-tuple-element.65), channel_id=1, source_target_pairs={{0,64},{32,96},{64,0},{96,32},{128,192},{160,224},{192,128},{224,1... | collective-permute-start | bytes 786440 | tf_op jit(solution)/shard_map/ppermute | solution.py:416
  127.7 17.3 %collective-permute-start.9 = (bf16[512,256]{1,0:T(8,128)(2,1)}, bf16[512,256]{1,0:T(8,128)(2,1)S(1)}, u32[]{:S(2)}, u32[]{:S(2)}) collective-permute-start(bf16[512,256]{1,0:T(8,128)(2,1)} %get-tuple-element.63), channel_id=1, source_target_pairs={{0,64},{32,96},{64,0},{96,32},{128,192},{160,224},{192,128},{224,1... | collective-permute-start | bytes 786440 | tf_op jit(solution)/shard_map/ppermute | solution.py:416
  136.3 9.9 %collective-permute-start.11 = (bf16[512,256]{1,0:T(8,128)(2,1)S(1)}, bf16[512,256]{1,0:T(8,128)(2,1)S(1)}, u32[]{:S(2)}, u32[]{:S(2)}) collective-permute-start(bf16[512,256]{1,0:T(8,128)(2,1)S(1)} %add_convert_fusion), channel_id=1, source_target_pairs={{0,32},{32,0},{64,96},{96,64},{128,160},{160,128},{192,224},{224,1... | collective-permute-start | bytes 786440 | tf_op jit(solution)/shard_map/ppermute | solution.py:416
  137.9 8.3 %copy-start.6 = (f32[512,256]{1,0:T(8,128)S(1)}, f32[512,256]{1,0:T(8,128)}, u32[]{:S(2)}) copy-start(f32[512,256]{1,0:T(8,128)} %get-tuple-element.52) | copy-start | bytes 1572868
  137.9 8.3 %copy-start.7 = (f32[512,256]{1,0:T(8,128)S(1)}, f32[512,256]{1,0:T(8,128)}, u32[]{:S(2)}) copy-start(f32[512,256]{1,0:T(8,128)} %get-tuple-element.62) | copy-start | bytes 1572868
  144.9 7.5 %copy-start.11 = (bf16[192,1792]{1,0:T(8,128)(2,1)S(1)}, bf16[192,1792]{1,0:T(8,128)(2,1)}, u32[]{:S(2)}) copy-start(bf16[192,1792]{1,0:T(8,128)(2,1)} %get-tuple-element.76) | copy-start | bytes 2064388
  146.5 5.9 %collective-permute-start.13 = (bf16[512,256]{1,0:T(8,128)(2,1)S(1)}, bf16[512,256]{1,0:T(8,128)(2,1)S(1)}, u32[]{:S(2)}, u32[]{:S(2)}) collective-permute-start(bf16[512,256]{1,0:T(8,128)(2,1)S(1)} %multiply_convert_fusion.a0_ref), channel_id=1, source_target_pairs={{0,64},{32,96},{64,0},{96,32},{128,192},{160,224},{192,128},{224,1... | collective-permute-start | bytes 786440 | tf_op jit(solution)/shard_map/ppermute | solution.py:416
  148.2 13.4 %collective-permute-start.12 = (bf16[512,256]{1,0:T(8,128)(2,1)S(1)}, bf16[512,256]{1,0:T(8,128)(2,1)S(1)}, u32[]{:S(2)}, u32[]{:S(2)}) collective-permute-start(bf16[512,256]{1,0:T(8,128)(2,1)S(1)} %multiply_convert_fusion.a0_ref), channel_id=1, source_target_pairs={{0,32},{32,0},{64,96},{96,64},{128,160},{160,128},{192,224},{224,1... | collective-permute-start | bytes 786440 | tf_op jit(solution)/shard_map/ppermute | solution.py:416
  152.4 25.4 %collective-permute-start.15 = (bf16[192,1792]{1,0:T(8,128)(2,1)S(1)}, bf16[192,1792]{1,0:T(8,128)(2,1)S(1)}, u32[]{:S(2)}, u32[]{:S(2)}) collective-permute-start(bf16[192,1792]{1,0:T(8,128)(2,1)S(1)} %copy-done.11), channel_id=1, source_target_pairs={{0,224},{32,192},{64,160},{96,128},{128,96},{160,64},{192,32},{224... | collective-permute-start | bytes 2064392 | tf_op jit(solution)/shard_map/ppermute | solution.py:425
  161.7 5.5 %collective-permute-start.14 = (bf16[512,256]{1,0:T(8,128)(2,1)S(1)}, bf16[512,256]{1,0:T(8,128)(2,1)S(1)}, u32[]{:S(2)}, u32[]{:S(2)}) collective-permute-start(bf16[512,256]{1,0:T(8,128)(2,1)S(1)} %collective-permute-done.12.a1_ref), channel_id=1, source_target_pairs={{0,64},{32,96},{64,0},{96,32},{128,192},{160,224},{192,128},{224,1... | collective-permute-start | bytes 786440 | tf_op jit(solution)/shard_map/ppermute | solution.py:416
  177.8 53.7 %all-to-all-start.3 = ((bf16[32,16,1792]{2,1,0:T(8,128)(2,1)}), bf16[32,16,1792]{2,1,0:T(8,128)(2,1)}, u32[]{:S(2)}, u32[]{:S(2)}) async-start(bf16[32,16,1792]{2,1,0:T(8,128)(2,1)} %bitcast.34), calls=%async_computation.3 | async-start | bytes 3670016 | tf_op jit(solution)/shard_map/all_to_all | solution.py:431
  186.8 32.7 %collective-permute-start.17 = (bf16[192,1792]{1,0:T(8,128)(2,1)}, bf16[192,1792]{1,0:T(8,128)(2,1)S(1)}, u32[]{:S(2)}, u32[]{:S(2)}) collective-permute-start(bf16[192,1792]{1,0:T(8,128)(2,1)} %get-tuple-element.83), channel_id=1, source_target_pairs={{0,224},{32,192},{64,160},{96,128},{128,96},{160,64},{192,32},{224... | collective-permute-start | bytes 2064392 | tf_op jit(solution)/shard_map/ppermute | solution.py:425
  189.2 45.2 %collective-permute-start.16 = (bf16[128,1792]{1,0:T(8,128)(2,1)}, bf16[128,1792]{1,0:T(8,128)(2,1)S(1)}, u32[]{:S(2)}, u32[]{:S(2)}) collective-permute-start(bf16[128,1792]{1,0:T(8,128)(2,1)} %get-tuple-element.82), channel_id=1, source_target_pairs={{0,224},{32,192},{64,160},{96,128},{128,96},{160,64},{192,32},{224... | collective-permute-start | bytes 1376264 | tf_op jit(solution)/shard_map/ppermute | solution.py:425
